TPU v7x, 32 devices: a whole 2x2x4 slice. The times are simulated.
32 devices in a mesh: ctx: 16 (over z, x, core), batch: 2 (over y).
Axes of the slice: x: 2, y: 2, z: 4, core: 2. Of those that a mesh axis runs over, the one named last changes fastest.
Arguments:
- queries: bfloat16 [2, 8192, 256], P('batch', 'ctx')
- keys: bfloat16 [2, 8192, 256], P('batch', 'ctx'), may hold values from -6 to 6
- values: bfloat16 [2, 8192, 256], P('batch', 'ctx'), may hold values from -6 to 6
- output_weight: bfloat16 [256, 512], replicated, may hold values from -0.375 to 0.375
- output_grad: bfloat16 [2, 8192, 512], P('batch', 'ctx'), may hold values from -6 to 6
- rand_blocks: int32 [2, 128, 3], P('batch', 'ctx'), may hold values from 0 to 127, as said below
- glob_pos: int32 [2, 256], P('batch'), may hold values from 0 to 8191, as said below
Outputs:
- attended: bfloat16 [2, 8192, 512], P('batch', 'ctx')
- grad_queries: bfloat16 [2, 8192, 256], P('batch', 'ctx')
- grad_keys: bfloat16 [2, 8192, 256], P('batch', 'ctx')
- grad_values: bfloat16 [2, 8192, 256], P('batch', 'ctx')
- grad_weight: float32 [256, 512], replicated
Inputs may be any that keep to these rules, and one draw needn't show every extreme that they name: `rand_blocks`: blocks b and c lie in the same range when b // 8 == c // 8. The 24 numbers of one range of query blocks name at most 2 blocks of any one range; in every sequence there is a range of which every range of query blocks names exactly 2 blocks. `glob_pos`: the positions of one sequence are distinct.
All inputs are finite; a program needn't handle non-finite values.
Results may differ from a plain program's by a relative error of at most 0.0096.
Values may be sent and summed in bfloat16 or wider, within the bound.
No kernel may reach another device: no remote copies, remote signals or barrier semaphores. Data moves between devices by JAX's collectives and lax.ppermute only.
A program may use at most 128 MiB of HBM per device.

v0:
```python
import jax
import jax.numpy as jnp
from jax import lax
from jax.sharding import PartitionSpec as P

BLK = 64
HEADS = 4
RAND = 3


def padded_2(block, sides, width):
    for axis, dim in sides:
        count = lax.axis_size(axis)
        forward = [(i, i + 1) for i in range(count - 1)]
        forward.append((count - 1, 0))
        backward = [(target, source) for source, target in forward]
        low = lax.ppermute(
            lax.slice_in_dim(block, block.shape[dim] - width, None, axis=dim), axis, forward
        )
        high = lax.ppermute(lax.slice_in_dim(block, 0, width, axis=dim), axis, backward)
        block = jnp.concatenate([low, block, high], axis=dim)
    return block


def product(form, left, right):
    return jnp.einsum(form, left, right, preferred_element_type=jnp.float32)


def attend(query_group, local_keys, local_values, glob_keys, glob_values, grad_group, score_scale):
    scores_local = product("nqhd,nkhd->nhqk", query_group, local_keys) * score_scale
    scores_glob = product("nqhd,khd->nhqk", query_group, glob_keys) * score_scale
    row_max = jnp.maximum(
        jnp.max(scores_local, axis=-1, keepdims=True), jnp.max(scores_glob, axis=-1, keepdims=True)
    )
    expo_local = jnp.exp(scores_local - row_max)
    expo_glob = jnp.exp(scores_glob - row_max)
    denominator = jnp.sum(expo_local, axis=-1, keepdims=True) + jnp.sum(
        expo_glob, axis=-1, keepdims=True
    )
    probs_local = expo_local / denominator
    probs_glob = expo_glob / denominator
    probs_local16 = probs_local.astype(jnp.bfloat16)
    probs_glob16 = probs_glob.astype(jnp.bfloat16)
    attention = product("nhqk,nkhd->nqhd", probs_local16, local_values) + product(
        "nhqk,khd->nqhd", probs_glob16, glob_values
    )
    vgrad_local = product("nhqk,nqhd->nkhd", probs_local16, grad_group)
    vgrad_glob = product("nhqk,nqhd->khd", probs_glob16, grad_group)
    dprob_local = product("nqhd,nkhd->nhqk", grad_group, local_values)
    dprob_glob = product("nqhd,khd->nhqk", grad_group, glob_values)
    delta = jnp.swapaxes(jnp.sum(grad_group.astype(jnp.float32) * attention, axis=-1), 1, 2)[
        ..., None
    ]
    dscore_local = (probs_local * (dprob_local - delta) * score_scale).astype(jnp.bfloat16)
    dscore_glob = (probs_glob * (dprob_glob - delta) * score_scale).astype(jnp.bfloat16)
    grad_query = product("nhqk,nkhd->nqhd", dscore_local, local_keys) + product(
        "nhqk,khd->nqhd", dscore_glob, glob_keys
    )
    kgrad_local = product("nhqk,nqhd->nkhd", dscore_local, query_group)
    kgrad_glob = product("nhqk,nqhd->khd", dscore_glob, query_group)
    return (attention, grad_query, kgrad_local, vgrad_local, kgrad_glob, vgrad_glob)


def shards(queries, keys, values, output_weight, output_grad, rand_blocks, glob_pos):
    tokens_here = queries.shape[1]
    width = queries.shape[2]
    head_size = width // HEADS
    block = BLK
    query_blocks = tokens_here // block
    span_devices = lax.axis_size("ctx")
    capacity = query_blocks * RAND // span_devices + 1
    requests = query_blocks * RAND
    score_scale = head_size ** (-0.5)
    query_rows = queries[0]
    grad_rows = output_grad[0]
    key_value = jnp.concatenate([keys[0], values[0]], axis=1)
    grad_attn = lax.dot_general(
        grad_rows, output_weight, (((1,), (1,)), ((), ())), preferred_element_type=jnp.float32
    ).astype(jnp.bfloat16)
    padded = padded_2(key_value, (("ctx", 0),), block)
    padded_blocks = padded.reshape(query_blocks + 2, block, 2 * width)
    window = jnp.concatenate([padded_blocks[:-2], padded_blocks[1:-1], padded_blocks[2:]], axis=1)
    first_token = lax.axis_index("ctx") * tokens_here
    positions = glob_pos[0]
    owned_rows = (
        positions[:, None] == first_token + jnp.arange(tokens_here, dtype=jnp.int32)[None, :]
    )
    glob_sum = lax.psum(
        jnp.dot(owned_rows.astype(jnp.bfloat16), key_value, preferred_element_type=jnp.float32),
        "ctx",
    )
    glob_pair = glob_sum.astype(jnp.bfloat16)
    glob_count = glob_pair.shape[0]
    wanted = rand_blocks[0].reshape(requests)
    owner_dev = wanted // query_blocks
    local_block = wanted % query_blocks
    request_order = jnp.arange(requests, dtype=jnp.int32)
    slot_rank = jnp.sum(
        (
            (owner_dev[:, None] == owner_dev[None, :])
            & (request_order[None, :] < request_order[:, None])
        ).astype(jnp.int32),
        axis=1,
    )
    slot_index = owner_dev * capacity + slot_rank
    all_slots = jnp.arange(span_devices * capacity, dtype=jnp.int32)
    listed = (
        jnp.sum(
            jnp.where(slot_index[:, None] == all_slots[None, :], local_block[:, None] + 1, 0),
            axis=0,
        )
        - 1
    )
    asked_for = lax.all_to_all(
        listed.reshape(span_devices, capacity), "ctx", split_axis=0, concat_axis=0, tiled=True
    )
    asked_flat = asked_for.reshape(span_devices * capacity)
    own_blocks = key_value.reshape(query_blocks, block, 2 * width)
    reply_blocks = jnp.where(
        (asked_flat >= 0)[:, None, None],
        jnp.take(own_blocks, jnp.maximum(asked_flat, 0), axis=0),
        jnp.zeros((), jnp.bfloat16),
    )
    arrived = lax.all_to_all(
        reply_blocks.reshape(span_devices, capacity, block, 2 * width),
        "ctx",
        split_axis=0,
        concat_axis=0,
        tiled=True,
    )
    fetched = jnp.take(
        arrived.reshape(span_devices * capacity, block, 2 * width), slot_index, axis=0
    )
    fetched = fetched.reshape(query_blocks, RAND * block, 2 * width)
    local_pair = jnp.concatenate([window, fetched], axis=1)
    span = local_pair.shape[1]
    groups = query_blocks // 8
    local_keys = local_pair[..., :width].reshape(groups, 8, span, HEADS, head_size)
    local_values = local_pair[..., width:].reshape(groups, 8, span, HEADS, head_size)
    glob_keys = glob_pair[:, :width].reshape(glob_count, HEADS, head_size)
    glob_values = glob_pair[:, width:].reshape(glob_count, HEADS, head_size)
    query_groups = query_rows.reshape(groups, 8, block, HEADS, head_size)
    grad_groups = grad_attn.reshape(groups, 8, block, HEADS, head_size)

    def one_group(members):
        return attend(
            members[0], members[1], members[2], glob_keys, glob_values, members[3], score_scale
        )

    attention, grad_query, kgrad_local, vgrad_local, kgrad_glob, vgrad_glob = lax.map(
        one_group, (query_groups, local_keys, local_values, grad_groups)
    )
    attention_rows = attention.reshape(tokens_here, width).astype(jnp.bfloat16)
    attended = jnp.dot(attention_rows, output_weight, preferred_element_type=jnp.float32).astype(
        jnp.bfloat16
    )
    weight_term = lax.dot_general(
        attention_rows, grad_rows, (((0,), (0,)), ((), ())), preferred_element_type=jnp.float32
    )
    grad_weight = lax.psum(weight_term, ("ctx", "batch"))
    local_grads = jnp.concatenate(
        [
            kgrad_local.reshape(query_blocks, span, width),
            vgrad_local.reshape(query_blocks, span, width),
        ],
        axis=2,
    )
    win_grads = local_grads[:, : 3 * block].reshape(query_blocks, 3, block, 2 * width)
    window_sum = (
        jnp.pad(win_grads[:, 0], ((0, 2), (0, 0), (0, 0)))
        + jnp.pad(win_grads[:, 1], ((1, 1), (0, 0), (0, 0)))
        + jnp.pad(win_grads[:, 2], ((2, 0), (0, 0), (0, 0)))
    )
    rim_parts = padded_2(
        jnp.stack([window_sum[0], window_sum[-1]]).astype(jnp.bfloat16), (("ctx", 0),), 1
    ).astype(jnp.float32)
    inner_sum = window_sum[1:-1]
    inner_sum = inner_sum.at[0].add(rim_parts[0]).at[query_blocks - 1].add(rim_parts[3])
    rand_grads = (
        local_grads[:, 3 * block :].reshape(requests, block, 2 * width).astype(jnp.bfloat16)
    )
    outgoing = (
        jnp.zeros((span_devices * capacity, block, 2 * width), jnp.bfloat16)
        .at[slot_index]
        .set(rand_grads)
    )
    returned = lax.all_to_all(
        outgoing.reshape(span_devices, capacity, block, 2 * width),
        "ctx",
        split_axis=0,
        concat_axis=0,
        tiled=True,
    )
    chooser = (asked_flat[None, :] == jnp.arange(query_blocks, dtype=jnp.int32)[:, None]).astype(
        jnp.bfloat16
    )
    gathered_in = jnp.dot(
        chooser,
        returned.reshape(span_devices * capacity, block * 2 * width),
        preferred_element_type=jnp.float32,
    ).reshape(query_blocks, block, 2 * width)
    glob_grads = jnp.concatenate(
        [
            jnp.sum(kgrad_glob, axis=0).reshape(glob_count, width),
            jnp.sum(vgrad_glob, axis=0).reshape(glob_count, width),
        ],
        axis=1,
    )
    glob_total = lax.psum(glob_grads, "ctx")
    inside = (positions >= first_token) & (positions < first_token + tokens_here)
    target = jnp.where(inside, positions - first_token, tokens_here)
    glob_part = (
        jnp.zeros((tokens_here, 2 * width), jnp.float32).at[target].add(glob_total, mode="drop")
    )
    grand_total = (inner_sum + gathered_in).reshape(tokens_here, 2 * width) + glob_part
    grad_queries = grad_query.reshape(tokens_here, width).astype(jnp.bfloat16)
    return (
        attended[None],
        grad_queries[None],
        grand_total[:, :width].astype(jnp.bfloat16)[None],
        grand_total[:, width:].astype(jnp.bfloat16)[None],
        grad_weight,
    )


def solution(mesh):
    in_specs = (
        P("batch", "ctx", None),
        P("batch", "ctx", None),
        P("batch", "ctx", None),
        P(),
        P("batch", "ctx", None),
        P("batch", "ctx", None),
        P("batch", None),
    )
    out_specs = (
        P("batch", "ctx", None),
        P("batch", "ctx", None),
        P("batch", "ctx", None),
        P("batch", "ctx", None),
        P(),
    )
    return jax.shard_map(shards, mesh=mesh, in_specs=in_specs, out_specs=out_specs, check_vma=False)
```

profile of v0, /device:TPU:0, one launch (start us, length us, event | category | flops | bytes accessed | tf_op | source)
XLA Modules:
  0.0 450.1 jit_solution(18099345991687602854)
XLA Ops:
  9.1 7.4 %all-to-all-start = ((s32[16,1,2]{2,1,0:T(1,128)}), s32[16,1,2]{2,1,0:T(1,128)S(1)}, u32[]{:S(2)}, u32[]{:S(2)}) async-start(s32[16,1,2]{2,1,0:T(1,128)} %bitcast.6), calls=%async_computation | async-start | bytes 16384 | tf_op jit(solution)/shard_map/all_to_all | solution.py:114
  17.5 5.3 %all-to-all-done = s32[16,1,2]{2,1,0:T(1,128)S(1)} async-done(((s32[16,1,2]{2,1,0:T(1,128)}), s32[16,1,2]{2,1,0:T(1,128)S(1)}, u32[]{:S(2)}, u32[]{:S(2)}) %all-to-all-start) | async-done | bytes 160 | tf_op jit(solution)/shard_map/all_to_all | solution.py:114
  25.6 4.6 %all-to-all-start.1 = ((bf16[16,2,64,512]{3,2,1,0:T(8,128)(2,1)}), bf16[16,2,64,512]{3,2,1,0:T(8,128)(2,1)}, u32[]{:S(2)}, u32[]{:S(2)}) async-start(bf16[16,2,64,512]{3,2,1,0:T(8,128)(2,1)} %select_select_fusion), calls=%async_computation.1 | async-start | bytes 4194304 | tf_op jit(solution)/shard_map/all_to_all | solution.py:124
  31.1 4.2 collective-permute-start.1
  39.0 87.4 %all-reduce.10 = bf16[256,512]{1,0:T(8,128)(2,1)S(1)} all-reduce(f32[256,512]{1,0:T(8,128)S(1)} %fusion.23), channel_id=1, replica_groups=mesh['ctx'=16,'batch'=2] {'ctx'}, use_global_device_ids=true, to_apply=%region_3.4 | all-reduce | flops 131072 | bytes 786432 | tf_op jit(solution)/shard_map/psum | solution.py:88
  135.5 3.4 gather_fusion.1
  143.2 2.6 copy.209
  149.9 2.7 copy.208
  152.5 4.8 %fusion.20 = f32[8,4,64,384]{3,2,1,0:T(8,128)} fusion(bf16[8,64,4,64]{1,0,3,2:T(8,128)(2,1)} %copy-done.16, f32[8,4,384,64]{2,3,1,0:T(8,128)} %copy-done.2, f32[8,4,64]{2,1,0:T(4,128)S(1)} %copy.216, f32[8,4,64]{2,1,0:T(4,128)S(1)} %copy.214), kind=kOutput, calls=%fused_computation.45 | convolution fusion | flops 103809024 | bytes 6569984 | tf_op jit(solution)/shard_map/while/body/eval_jaxpr/nhqk,nqhd->nkhd/dot_general | solution.py:26
  159.2 3.5 copy.230
  162.8 3.1 multiply_reduce_fusion
  169.8 3.6 copy.229
  173.4 3.2 fusion.1
  178.3 5.9 %scatter_fusion = bf16[32,64,512]{2,1,0:T(8,128)(2,1)} fusion(bf16[32,64,512]{2,1,0:T(8,128)(2,1)} %broadcast_in_dim.116, s32[24]{0:T(128)S(1)} %copy-done.31, bf16[24,64,512]{2,1,0:T(8,128)(2,1)} %bitcast.215), kind=kCustom, calls=%fused_computation.2 | custom fusion | bytes 4718688 | tf_op jit(solution)/shard_map/scatter | solution.py:185
  184.2 4.6 %all-to-all-start.2 = ((bf16[16,2,64,512]{3,2,1,0:T(8,128)(2,1)}), bf16[16,2,64,512]{3,2,1,0:T(8,128)(2,1)}, u32[]{:S(2)}, u32[]{:S(2)}) async-start(bf16[16,2,64,512]{3,2,1,0:T(8,128)(2,1)} %bitcast.207), calls=%async_computation.2 | async-start | bytes 4194304 | tf_op jit(solution)/shard_map/all_to_all | solution.py:187
  190.4 2.7 fusion.58
  206.9 4.2 collective-permute-start.3
  221.5 10.7 %collective-permute-done.2 = bf16[1,64,512]{2,0,1:T(2,128)(2,1)} collective-permute-done((bf16[1,64,512]{2,0,1:T(2,128)(2,1)S(1)}, bf16[1,64,512]{2,0,1:T(2,128)(2,1)}, u32[]{:S(2)}, u32[]{:S(2)}) %collective-permute-start.2) | collective-permute-done | bytes 65568 | tf_op jit(solution)/shard_map/ppermute | solution.py:17
  233.8 3.8 scatter-add.14
  239.6 3.8 scatter-add.18
  243.4 3.1 fusion.11
  247.1 60.7 %all-reduce.7.cloned.1.call-done = f32[256,512]{1,0:T(8,128)} async-done(((f32[256,512]{1,0:T(8,128)}), f32[256,512]{1,0:T(8,128)}) %all-reduce.7.cloned.1.call-update) | async-done | bytes 524304 | tf_op jit(solution)/shard_map/psum | solution.py:209
  307.8 3.0 scatter_fusion.1
  311.7 129.7 %all-reduce.9.cloned.1.call-done = f32[256,512]{1,0:T(8,128)} async-done(((f32[256,512]{1,0:T(8,128)}), f32[256,512]{1,0:T(8,128)}) %all-reduce.9.cloned.1.call-update) | async-done | bytes 524304 | tf_op jit(solution)/shard_map/psum | solution.py:160
  (170 shorter events, 67.7 us)
Async XLA Ops:
  7.2 119.4 %copy-start = (bf16[1,512,512]{2,1,0:T(8,128)(2,1)S(1)}, bf16[1,512,512]{2,1,0:T(8,128)(2,1)}, u32[]{:S(2)}) copy-start(bf16[1,512,512]{2,1,0:T(8,128)(2,1)} %param.15) | copy-start | bytes 1572868
  9.1 13.7 %all-to-all-start = ((s32[16,1,2]{2,1,0:T(1,128)}), s32[16,1,2]{2,1,0:T(1,128)S(1)}, u32[]{:S(2)}, u32[]{:S(2)}) async-start(s32[16,1,2]{2,1,0:T(1,128)} %bitcast.6), calls=%async_computation | async-start | bytes 16384 | tf_op jit(solution)/shard_map/all_to_all | solution.py:114
  25.6 4.6 %copy-start.10 = (bf16[1,512,256]{2,1,0:T(8,128)(2,1)S(1)}, bf16[1,512,256]{2,1,0:T(8,128)(2,1)}, u32[]{:S(2)}) copy-start(bf16[1,512,256]{2,1,0:T(8,128)(2,1)} %param.13) | copy-start | bytes 786436
  25.6 4.6 %copy-start.11 = (bf16[1,512,256]{2,1,0:T(8,128)(2,1)S(1)}, bf16[1,512,256]{2,1,0:T(8,128)(2,1)}, u32[]{:S(2)}) copy-start(bf16[1,512,256]{2,1,0:T(8,128)(2,1)} %param.12) | copy-start | bytes 786436
  25.6 10.5 %copy-start.27 = (bf16[1,512,256]{2,1,0:T(8,128)(2,1)S(1)}, bf16[1,512,256]{2,1,0:T(8,128)(2,1)}, u32[]{:S(2)}) copy-start(bf16[1,512,256]{2,1,0:T(8,128)(2,1)} %param.11) | copy-start | bytes 786436
  25.6 109.9 %all-to-all-start.1 = ((bf16[16,2,64,512]{3,2,1,0:T(8,128)(2,1)}), bf16[16,2,64,512]{3,2,1,0:T(8,128)(2,1)}, u32[]{:S(2)}, u32[]{:S(2)}) async-start(bf16[16,2,64,512]{3,2,1,0:T(8,128)(2,1)} %select_select_fusion), calls=%async_computation.1 | async-start | bytes 4194304 | tf_op jit(solution)/shard_map/all_to_all | solution.py:124
  30.2 8.2 %copy-start.29 = (s32[1,8,3]{1,0,2:T(1,128)S(1)}, s32[1,8,3]{1,0,2:T(1,128)}, u32[]{:S(2)}) copy-start(s32[1,8,3]{1,0,2:T(1,128)} %param.16) | copy-start | bytes 292
  30.2 8.5 %copy-start.32 = (s32[1,256]{1,0:T(1,128)S(1)}, s32[1,256]{1,0:T(1,128)}, u32[]{:S(2)}) copy-start(s32[1,256]{1,0:T(1,128)} %param.17) | copy-start | bytes 3076
  30.9 102.7 %collective-permute-start = (bf16[64,512]{1,0:T(8,128)(2,1)}, bf16[64,512]{1,0:T(8,128)(2,1)}, u32[]{:S(2)}, u32[]{:S(2)}) collective-permute-start(bf16[64,512]{1,0:T(8,128)(2,1)} %get-tuple-element.108), channel_id=1, source_target_pairs={{0,2},{2,4},{4,6},{6,8},{8,10},{10,12},{12,14},{14,16},{16,18},{18... | collective-permute-start | bytes 196616 | tf_op jit(solution)/shard_map/ppermute | solution.py:17
  31.1 102.5 %collective-permute-start.1 = (bf16[64,512]{1,0:T(8,128)(2,1)}, bf16[64,512]{1,0:T(8,128)(2,1)}, u32[]{:S(2)}, u32[]{:S(2)}) collective-permute-start(bf16[64,512]{1,0:T(8,128)(2,1)} %get-tuple-element.109), channel_id=1, source_target_pairs={{2,0},{4,2},{6,4},{8,6},{10,8},{12,10},{14,12},{16,14},{18,16},{20... | collective-permute-start | bytes 196616 | tf_op jit(solution)/shard_map/ppermute | solution.py:20
  37.4 89.2 %copy-start.22 = (bf16[256,512]{1,0:T(8,128)(2,1)S(1)}, bf16[256,512]{1,0:T(8,128)(2,1)}, u32[]{:S(2)}) copy-start(bf16[256,512]{1,0:T(8,128)(2,1)} %param.14) | copy-start | bytes 786436
  152.5 4.8 %copy-start.3 = (f32[8,4,384,64]{2,3,1,0:T(8,128)S(1)}, f32[8,4,384,64]{2,3,1,0:T(8,128)}, u32[]{:S(2)}) copy-start(f32[8,4,384,64]{2,3,1,0:T(8,128)} %copy-done.2) | copy-start | bytes 9437188
  152.5 4.8 %copy-start.19 = (bf16[8,384,256]{1,2,0:T(8,128)(2,1)S(1)}, bf16[8,384,256]{1,2,0:T(8,128)(2,1)}, u32[]{:S(2)}) copy-start(bf16[8,384,256]{1,2,0:T(8,128)(2,1)} %copy.208) | copy-start | bytes 4718596
  159.2 3.6 copy-start.26
  162.8 3.1 copy-start.20
  184.2 4.9 %copy-start.33 = (s32[1,256]{1,0:T(1,128)S(1)}, s32[1,256]{1,0:T(1,128)}, u32[]{:S(2)}) copy-start(s32[1,256]{1,0:T(1,128)} %param.17) | copy-start | bytes 3076
  184.2 59.2 %all-to-all-start.2 = ((bf16[16,2,64,512]{3,2,1,0:T(8,128)(2,1)}), bf16[16,2,64,512]{3,2,1,0:T(8,128)(2,1)}, u32[]{:S(2)}, u32[]{:S(2)}) async-start(bf16[16,2,64,512]{3,2,1,0:T(8,128)(2,1)} %bitcast.207), calls=%async_computation.2 | async-start | bytes 4194304 | tf_op jit(solution)/shard_map/all_to_all | solution.py:187
  188.8 119.0 %all-reduce.7.cloned.1.call-start = ((), (), s32[]{:S(2)}) async-start(), calls=%async_computation.3 | async-start | bytes 1048576 | tf_op jit(solution)/shard_map/psum | solution.py:209
  200.0 241.4 %all-reduce.9.cloned.1.call-start = ((), (), s32[]{:S(2)}) async-start(), calls=%async_computation.4 | async-start | bytes 1048576 | tf_op jit(solution)/shard_map/psum | solution.py:160
  204.5 6.7 %copy-start.24 = (bf16[8,64,4,64]{1,3,2,0:T(8,128)(2,1)S(1)}, bf16[8,64,4,64]{1,3,2,0:T(8,128)(2,1)}, u32[]{:S(2)}) copy-start(bf16[8,64,4,64]{1,3,2,0:T(8,128)(2,1)} %get-tuple-element.103) | copy-start | bytes 786436
  206.5 5.4 %copy-start.1 = (bf16[8,384,256]{1,2,0:T(8,128)(2,1)S(1)}, bf16[8,384,256]{1,2,0:T(8,128)(2,1)}, u32[]{:S(2)}) copy-start(bf16[8,384,256]{1,2,0:T(8,128)(2,1)} %copy.209) | copy-start | bytes 4718596
  206.7 25.5 %collective-permute-start.2 = (bf16[1,64,512]{2,0,1:T(2,128)(2,1)S(1)}, bf16[1,64,512]{2,0,1:T(2,128)(2,1)}, u32[]{:S(2)}, u32[]{:S(2)}) collective-permute-start(bf16[1,64,512]{2,0,1:T(2,128)(2,1)S(1)} %get-tuple-element.100), channel_id=1, source_target_pairs={{0,2},{2,4},{4,6},{6,8},{8,10},{10,12},{12,14},{14,16},{16,18},{18... | collective-permute-start | bytes 196616 | tf_op jit(solution)/shard_map/ppermute | solution.py:17
  206.9 25.2 %collective-permute-start.3 = (bf16[1,64,512]{2,0,1:T(2,128)(2,1)S(1)}, bf16[1,64,512]{2,0,1:T(2,128)(2,1)}, u32[]{:S(2)}, u32[]{:S(2)}) collective-permute-start(bf16[1,64,512]{2,0,1:T(2,128)(2,1)S(1)} %get-tuple-element.101), channel_id=1, source_target_pairs={{2,0},{4,2},{6,4},{8,6},{10,8},{12,10},{14,12},{16,14},{18,16},{20... | collective-permute-start | bytes 196616 | tf_op jit(solution)/shard_map/ppermute | solution.py:20
  214.1 3.7 copy-start.8
  (20 other events, 42.0 us)
Sparse Core Ops, SparseCore 0:
  200.1 107.6 all-reduce.6
  313.1 128.3 all-reduce.8
where the time goes:
time: 451 us; the launch traced here: 450 us
  waiting for transfers between devices  206 us (46%)
  blocking collectives  87.4 us (19%)
  local copies, waits for them, and re-layouts  55.6 us (12%)
  matrix products  31.8 us (7%)
  other arithmetic  28.4 us (6%)
  starting transfers between devices  25.7 us (6%)
  between operations  14.7 us (3%)
    psum x1, waiting for transfers between devices, shards(): grad_weight = lax.psum(weight_term, ('ctx', 'batch'))  130 us
    psum x1, blocking collectives, shards(): lax.psum(jnp.dot(owned_rows.astype(jnp.bfloat16), key_value, preferred_el...  87.4 us
    psum x1, waiting for transfers between devices, shards(): glob_total = lax.psum(glob_grads, 'ctx')  60.7 us
    dot_general x10, matrix products, product(): return jnp.einsum(form, left, right, preferred_element_type=jnp.float32)  22.6 us
    ppermute x2, waiting for transfers between devices, padded_2(): lax.ppermute(lax.slice_in_dim(block, block.shape[dim] - width, None, axis...  10.7 us
  transfers between devices with their start and end apart: 9, of which 4 were waited for; matrix products, arithmetic and copies ran while one was open for 13% of the time, Pallas kernels for 0%

commit v1 on v0

v1 whole, which is shorter than its diff:
```python
import functools

import jax
import jax.numpy as jnp
from jax import lax
from jax.experimental import pallas as pl
from jax.experimental.pallas import tpu as pltpu
from jax.sharding import PartitionSpec as P

BLK = 64
HEADS = 4
RAND = 3
LANES = 128
MIB = 1024 * 1024
LOG2E = 1.4426950408889634

F32 = jnp.float32
BF16 = jnp.bfloat16
VMEM = pl.BlockSpec(memory_space=pltpu.VMEM)
SMEM = pl.BlockSpec(memory_space=pltpu.SMEM)


def params(mib):
    return pltpu.CompilerParams(vmem_limit_bytes=mib * MIB)


def dot(left, right, over_left, over_right):
    return lax.dot_general(
        left, right, (((over_left,), (over_right,)), ((), ())), preferred_element_type=F32
    )


def ask_kernel(span_devices, capacity, first_ref, want_ref, pos_ref, k_ref, v_ref,
               send_ref, slot_ref, count_ref, list_ref):
    tokens, width = k_ref.shape
    glob = pos_ref.shape[1]
    query_blocks = tokens // BLK
    rows = glob // span_devices
    for dev in range(span_devices):
        count_ref[dev] = 0
        for slot in range(capacity):
            list_ref[dev * capacity + slot] = -1

    def request(at, carry):
        wanted = want_ref[at]
        owner = lax.div(wanted, query_blocks)
        slot = owner * capacity + jnp.minimum(count_ref[owner], capacity - 1)
        count_ref[owner] = count_ref[owner] + 1
        list_ref[slot] = wanted - owner * query_blocks
        slot_ref[at] = slot
        return carry

    lax.fori_loop(0, query_blocks * RAND, request, 0)
    here = first_ref[0] + lax.broadcasted_iota(jnp.int32, (tokens, glob), 0)
    owned = jnp.where(here == pos_ref[...], 1.0, 0.0).astype(BF16)
    send_ref[:, :width] = dot(owned, k_ref[...], 0, 0).astype(BF16)
    send_ref[:, width : 2 * width] = dot(owned, v_ref[...], 0, 0).astype(BF16)
    row = lax.broadcasted_iota(jnp.int32, (glob, LANES), 0)
    lane = lax.broadcasted_iota(jnp.int32, (glob, LANES), 1)
    listed = jnp.full((glob, LANES), -1, jnp.int32)
    for dev in range(span_devices):
        mine = (row >= dev * rows) & (row < (dev + 1) * rows)
        for slot in range(capacity):
            listed = jnp.where(mine & (lane == slot), list_ref[dev * capacity + slot], listed)
    send_ref[:, 2 * width :] = listed.astype(F32).astype(BF16)


def reply_kernel(span_devices, capacity, got_ref, k_ref, v_ref, out_ref, glob_ref, asked_ref,
                 asked_smem, sem):
    tokens, width = k_ref.shape
    glob = got_ref.shape[0]
    rows = glob // span_devices
    source = lax.broadcasted_iota(jnp.int32, (span_devices, glob), 1)
    target = lax.broadcasted_iota(jnp.int32, (span_devices, glob), 0)
    pick = jnp.where(source == target * rows, 1.0, 0.0).astype(BF16)
    asked_ref[...] = dot(pick, got_ref[:, 2 * width :], 1, 0).astype(jnp.int32)
    copy = pltpu.make_async_copy(asked_ref, asked_smem, sem)
    copy.start()
    source = lax.broadcasted_iota(jnp.int32, (rows, glob), 1)
    target = lax.broadcasted_iota(jnp.int32, (rows, glob), 0)
    total = jnp.where(lax.rem(source, rows) == target, 1.0, 0.0).astype(BF16)
    glob_ref[...] = dot(total, got_ref[:, : 2 * width], 1, 0).astype(BF16)
    copy.wait()
    for dev in range(span_devices):
        for slot in range(capacity):
            block = jnp.maximum(asked_smem[dev, slot], 0)
            source = pl.ds(pl.multiple_of(block * BLK, BLK), BLK)
            target = pl.ds((dev * capacity + slot) * BLK, BLK)
            out_ref[target, :width] = k_ref[source, :]
            out_ref[target, width:] = v_ref[source, :]


def attend_kernel(slot_ref, q_ref, ga_ref, og_ref, k_ref, v_ref, low_ref, high_ref, glob_ref, arr_ref,
                  out_ref, red_ref, inner_ref, elow_ref, ehigh_ref, att_ref, dq_ref,
                  pad_ref, kc_ref, vc_ref, acc_ref, gacc_ref):
    tokens, width = q_ref.shape
    query_blocks = tokens // BLK
    head_size = width // HEADS
    scale = head_size ** (-0.5)
    win, local = 3 * BLK, (3 + RAND) * BLK
    pad_ref[:BLK] = low_ref[...]
    pad_ref[BLK : BLK + tokens, :width] = k_ref[...]
    pad_ref[BLK : BLK + tokens, width:] = v_ref[...]
    pad_ref[BLK + tokens :] = high_ref[...]
    kc_ref[local:] = glob_ref[:, :width]
    vc_ref[local:] = glob_ref[:, width:]
    acc_ref[...] = jnp.zeros_like(acc_ref)
    gacc_ref[...] = jnp.zeros_like(gacc_ref)
    row_head = lax.broadcasted_iota(jnp.int32, (HEADS * BLK, width), 0) // BLK
    lane_head = lax.broadcasted_iota(jnp.int32, (HEADS * BLK, width), 1) // head_size
    mask = jnp.where(row_head == lane_head, 1.0, 0.0).astype(BF16)
    keep = jnp.where(row_head == lane_head, 1.0, 0.0)

    def by_head(rows):
        return jnp.concatenate([rows] * HEADS, axis=0) * mask

    def own_head(full):
        kept = full * keep
        return sum(kept[h * BLK : (h + 1) * BLK] for h in range(HEADS))

    def one_block(i, carry):
        base = pl.multiple_of(i * BLK, BLK)
        slots = []
        kc_ref[:win] = pad_ref[pl.ds(base, win), :width]
        vc_ref[:win] = pad_ref[pl.ds(base, win), width:]
        for j in range(RAND):
            slot = pl.ds(pl.multiple_of(slot_ref[i * RAND + j] * BLK, BLK), BLK)
            slots.append(slot)
            kc_ref[win + j * BLK : win + (j + 1) * BLK] = arr_ref[slot, :width]
            vc_ref[win + j * BLK : win + (j + 1) * BLK] = arr_ref[slot, width:]
        q_by_head = by_head(q_ref[pl.ds(base, BLK), :])
        ga_by_head = by_head(ga_ref[pl.ds(base, BLK), :])
        scores = dot(kc_ref[...], q_by_head, 1, 1) * (scale * LOG2E)
        expo = jnp.exp2(scores - jnp.max(scores, axis=0, keepdims=True))
        probs = expo * (1.0 / jnp.sum(expo, axis=0, keepdims=True))
        probs16 = probs.astype(BF16)
        dprobs = dot(vc_ref[...], ga_by_head, 1, 1)
        delta = jnp.sum(probs16.astype(F32) * dprobs, axis=0, keepdims=True)
        dscores = (probs * (dprobs - delta) * scale).astype(BF16)
        att_ref[pl.ds(base, BLK), :] = own_head(dot(probs16, vc_ref[...], 0, 0)).astype(BF16)
        dq_ref[pl.ds(base, BLK), :] = own_head(dot(dscores, kc_ref[...], 0, 0)).astype(BF16)
        for part, terms in (
            (slice(0, width), dot(dscores, q_by_head, 1, 0)),
            (slice(width, 2 * width), dot(probs16, ga_by_head, 1, 0)),
        ):
            acc_ref[pl.ds(base, win), part] += terms[:win]
            gacc_ref[:, part] += terms[local:]
            for j in range(RAND):
                out_ref[slots[j], part] = terms[win + j * BLK : win + (j + 1) * BLK].astype(BF16)
        return carry

    lax.fori_loop(0, query_blocks, one_block, 0)
    inner_ref[...] = acc_ref[BLK : BLK + tokens]
    elow_ref[...] = acc_ref[:BLK].astype(BF16)
    ehigh_ref[...] = acc_ref[BLK + tokens :].astype(BF16)
    red_ref[:, : 2 * width] = gacc_ref[...].astype(BF16)
    red_ref[:, 2 * width :] = dot(att_ref[...], og_ref[...], 0, 0).astype(BF16)


def share_kernel(span_devices, got_ref, glob_ref, weight_ref):
    count, width = got_ref.shape
    rows = count // span_devices
    source = lax.broadcasted_iota(jnp.int32, (rows, count), 1)
    target = lax.broadcasted_iota(jnp.int32, (rows, count), 0)
    total = jnp.where(lax.rem(source, rows) == target, 1.0, 0.0).astype(BF16)
    part = glob_ref.shape[1]
    glob_ref[...] = dot(total, got_ref[:, :part], 1, 0).astype(BF16)
    weight_ref[...] = dot(total, got_ref[:, part:], 1, 0)


def finish_kernel(span_devices, capacity, first_ref, asked_ref, pos_ref, back_ref, inner_ref,
                  from_low_ref, from_high_ref, glob_ref, dk_ref, dv_ref, acc_ref):
    tokens, width = dk_ref.shape
    glob = glob_ref.shape[0]
    here = first_ref[0] + lax.broadcasted_iota(jnp.int32, (tokens, glob), 0)
    owned = jnp.where(here == pos_ref[...], 1.0, 0.0).astype(BF16)
    acc_ref[...] = inner_ref[...] + dot(owned, glob_ref[...], 1, 0)
    acc_ref[:BLK] += from_low_ref[...].astype(F32)
    acc_ref[tokens - BLK :] += from_high_ref[...].astype(F32)
    for dev in range(span_devices):
        for slot in range(capacity):
            block = asked_ref[dev, slot]

            @pl.when(block >= 0)
            def _():
                rows = pl.ds(pl.multiple_of(block * BLK, BLK), BLK)
                at = (dev * capacity + slot) * BLK
                acc_ref[rows, :] += back_ref[at : at + BLK, :].astype(F32)

    dk_ref[...] = acc_ref[:, :width].astype(BF16)
    dv_ref[...] = acc_ref[:, width:].astype(BF16)


def shards(queries, keys, values, output_weight, output_grad, rand_blocks, glob_pos):
    q, k, v, og = queries[0], keys[0], values[0], output_grad[0]
    tokens, width = q.shape
    model = og.shape[1]
    glob = glob_pos.shape[1]
    query_blocks = tokens // BLK
    span = lax.axis_size("ctx")
    batch = lax.axis_size("batch")
    requests = query_blocks * RAND
    capacity = requests // span + 1
    slots = span * capacity
    rows = glob // span
    first = (lax.axis_index("ctx") * tokens).astype(jnp.int32).reshape(1)
    shape = jax.ShapeDtypeStruct
    forward = [(i, (i + 1) % span) for i in range(span)]
    backward = [(target, source) for source, target in forward]

    def swap(x):
        return lax.all_to_all(x, "ctx", split_axis=0, concat_axis=0, tiled=True)

    send, slot_index = pl.pallas_call(
        functools.partial(ask_kernel, span, capacity),
        name="ask",
        out_shape=(shape((glob, 2 * width + LANES), BF16), shape((requests,), jnp.int32)),
        in_specs=[SMEM, SMEM, VMEM, VMEM, VMEM],
        out_specs=(VMEM, SMEM),
        scratch_shapes=[pltpu.SMEM((span,), jnp.int32), pltpu.SMEM((slots,), jnp.int32)],
        compiler_params=params(16),
    )(first, rand_blocks.reshape(requests), glob_pos, k, v)
    got = swap(send)
    key_value_edges = [
        jnp.concatenate([k[edge], v[edge]], axis=1)
        for edge in (slice(tokens - BLK, tokens), slice(0, BLK))
    ]
    low = lax.ppermute(key_value_edges[0], "ctx", forward)
    high = lax.ppermute(key_value_edges[1], "ctx", backward)
    grad_attn = dot(og, output_weight, 1, 1).astype(BF16)

    reply, glob_mine, asked = pl.pallas_call(
        functools.partial(reply_kernel, span, capacity),
        name="reply",
        out_shape=(
            shape((slots * BLK, 2 * width), BF16),
            shape((rows, 2 * width), BF16),
            shape((span, LANES), jnp.int32),
        ),
        in_specs=[VMEM] * 3,
        out_specs=(VMEM,) * 3,
        scratch_shapes=[pltpu.SMEM((span, LANES), jnp.int32), pltpu.SemaphoreType.DMA],
        compiler_params=params(16),
    )(got, k, v)
    arrived = swap(reply)
    glob_rows = lax.all_gather(glob_mine, "ctx", axis=0, tiled=True)

    block = (3 + RAND) * BLK + glob
    outgoing, reduce_terms, inner, edge_low, edge_high, attention_rows, grad_queries = pl.pallas_call(
        attend_kernel,
        name="attend",
        out_shape=(
            shape((slots * BLK, 2 * width), BF16),
            shape((glob, 2 * width + model), BF16),
            shape((tokens, 2 * width), F32),
            shape((BLK, 2 * width), BF16),
            shape((BLK, 2 * width), BF16),
            shape((tokens, width), BF16),
            shape((tokens, width), BF16),
        ),
        in_specs=[SMEM] + [VMEM] * 9,
        out_specs=(VMEM,) * 7,
        scratch_shapes=[
            pltpu.VMEM((tokens + 2 * BLK, 2 * width), BF16),
            pltpu.VMEM((block, width), BF16),
            pltpu.VMEM((block, width), BF16),
            pltpu.VMEM((tokens + 2 * BLK, 2 * width), F32),
            pltpu.VMEM((glob, 2 * width), F32),
        ],
        compiler_params=params(32),
    )(slot_index, q, grad_attn, og, k, v, low, high, glob_rows, arrived)

    reduced = swap(reduce_terms)
    back = swap(outgoing)
    from_high = lax.ppermute(edge_low, "ctx", backward)
    from_low = lax.ppermute(edge_high, "ctx", forward)
    glob_share, weight_share = pl.pallas_call(
        functools.partial(share_kernel, span),
        name="share",
        out_shape=(shape((rows, 2 * width), BF16), shape((rows, model), F32)),
        in_specs=[VMEM],
        out_specs=(VMEM,) * 2,
        compiler_params=params(16),
    )(reduced)
    weight_sum = weight_share
    for step in range(1, batch):
        weight_sum = weight_sum + lax.ppermute(
            weight_share, "batch", [(i, (i + step) % batch) for i in range(batch)]
        )
    glob_total = lax.all_gather(glob_share, "ctx", axis=0, tiled=True)
    grad_weight = lax.all_gather(weight_sum, "ctx", axis=0, tiled=True)
    attended = dot(attention_rows, output_weight, 1, 0).astype(BF16)

    grad_keys, grad_values = pl.pallas_call(
        functools.partial(finish_kernel, span, capacity),
        name="finish",
        out_shape=(shape((tokens, width), BF16), shape((tokens, width), BF16)),
        in_specs=[SMEM, SMEM] + [VMEM] * 6,
        out_specs=(VMEM,) * 2,
        scratch_shapes=[pltpu.VMEM((tokens, 2 * width), F32)],
        compiler_params=params(24),
    )(first, asked, glob_pos, back, inner, from_low, from_high, glob_total)
    return (
        attended[None],
        grad_queries[None],
        grad_keys[None],
        grad_values[None],
        grad_weight,
    )


def solution(mesh):
    in_specs = (
        P("batch", "ctx", None),
        P("batch", "ctx", None),
        P("batch", "ctx", None),
        P(),
        P("batch", "ctx", None),
        P("batch", "ctx", None),
        P("batch", None),
    )
    out_specs = (
        P("batch", "ctx", None),
        P("batch", "ctx", None),
        P("batch", "ctx", None),
        P("batch", "ctx", None),
        P(),
    )
    return jax.shard_map(shards, mesh=mesh, in_specs=in_specs, out_specs=out_specs, check_vma=False)
```

time: 451 us -> 218 us (0.48)
  waiting for transfers between devices: 206 us -> 0.02 us
  blocking collectives: 87.4 us -> 165 us
  local copies, waits for them, and re-layouts: 55.6 us -> 15.2 us
  matrix products: 31.8 us -> 2.13 us
  other arithmetic: 28.4 us -> 0.02 us
  Pallas kernels: 0 us -> 16.3 us
  between operations: 14.7 us -> 0.85 us
  starting transfers between devices: 25.7 us -> 18.6 us
    psum x2 -> x0, waiting for transfers between devices: 190 us -> none  [the longest x1 130 us: shards(): grad_weight = lax.psum(weight_term, ('ctx', 'batch'))]
    all_gather x0 -> x3, blocking collectives: none -> 124 us  [the longest x1 51 us: shards(): glob_rows = lax.all_gather(glob_mine, 'ctx', axis=0, tiled=True)]
    psum x1 -> x0, blocking collectives: 87.4 us -> none  [shards(): lax.psum(jnp.dot(owned_rows.astype(jnp.bfloat16), key_value, preferred_el...]
    all_to_all x0 -> x2, blocking collectives: none -> 40.6 us  [swap(): return lax.all_to_all(x, 'ctx', split_axis=0, concat_axis=0, tiled=True)]
    dot_general x15 -> x2, matrix products: 28.6 us -> 2.13 us  [dot(): lax.dot_general(left, right, (((over_left,), (over_right,)), ((), ())), p...]
    pallas_call x0 -> x5, Pallas kernels: none -> 16.3 us  [the longest x1 11.4 us: shards(): pl.pallas_call(attend_kernel, name='attend', out_shape=(shape((slots * BL...]
    slice x9 -> x1, local copies, waits for them, and re-layouts: 11.6 us -> 0.01 us  [shards(): v[edge]]
    ppermute x4 -> x5, waiting for transfers between devices: 10.7 us -> 0.01 us  [the longest x1 0.01 us: shards(): low = lax.ppermute(key_value_edges[0], 'ctx', forward)]
  transfers between devices with their start and end apart: 9 -> 7, of which waited for: 4 -> 0; matrix products, arithmetic and copies ran while one was open for 13% -> 1% of each run, Pallas kernels for 0% -> 0%
where the time goes in v1:
time: 218 us
  blocking collectives  165 us (76%)
  starting transfers between devices  18.6 us (9%)
  Pallas kernels  16.3 us (7%)
  local copies, waits for them, and re-layouts  15.2 us (7%)
    all_gather x1, blocking collectives, shards(): glob_rows = lax.all_gather(glob_mine, 'ctx', axis=0, tiled=True)  51 us
    all_gather x1, blocking collectives, shards(): glob_total = lax.all_gather(glob_share, 'ctx', axis=0, tiled=True)  48.6 us
    all_to_all x2, blocking collectives, swap(): return lax.all_to_all(x, 'ctx', split_axis=0, concat_axis=0, tiled=True)  40.6 us
    all_gather x1, blocking collectives, shards(): grad_weight = lax.all_gather(weight_sum, 'ctx', axis=0, tiled=True)  24.3 us
    unnamed x56, local copies, waits for them, and re-layouts  15.1 us
    pallas_call x1, Pallas kernels, shards(): pl.pallas_call(attend_kernel, name='attend', out_shape=(shape((slots * BL...  11.4 us
    all_to_all x2, starting transfers between devices, swap(): return lax.all_to_all(x, 'ctx', split_axis=0, concat_axis=0, tiled=True)  8.09 us
  transfers between devices with their start and end apart: 7, of which 0 were waited for; matrix products, arithmetic and copies ran while one was open for 1% of the time, Pallas kernels for 0%

profile of v1, /device:TPU:0, one launch (start us, length us, event | category | flops | bytes accessed | tf_op | source)
XLA Modules:
  0.0 217.7 jit_solution(11794950510910865303)
XLA Ops:
  1.5 1.0 copy-done.1
  2.5 0.9 copy-done.4
  4.1 1.5 ask.1
  5.6 18.3 %all_to_all.44 = bf16[16,16,640]{2,1,0:T(8,128)(2,1)S(1)} all-to-all(bf16[16,16,640]{2,1,0:T(8,128)(2,1)S(1)} %bitcast.45), channel_id=1, replica_groups=mesh['ctx'=16,'batch'=2] {'ctx'}, dimensions={0} | all-to-all | bytes 655360 | tf_op jit(solution)/shard_map/all_to_all | solution.py:212
  23.9 0.9 copy-done.2
  24.8 0.9 copy-done.5
  25.8 1.0 reply.1
  26.7 1.3 copy-done.9
  28.7 3.8 %all-to-all-start.1 = ((bf16[16,128,512]{2,1,0:T(8,128)(2,1)}), bf16[16,128,512]{2,1,0:T(8,128)(2,1)S(1)}, u32[]{:S(2)}, u32[]{:S(2)}) async-start(bf16[16,128,512]{2,1,0:T(8,128)(2,1)} %bitcast.41), calls=%async_computation.1 | async-start | bytes 4194304 | tf_op jit(solution)/shard_map/all_to_all | solution.py:212
  32.9 4.2 %collective-permute-start.1 = (bf16[64,512]{1,0:T(8,128)(2,1)S(1)}, bf16[64,512]{1,0:T(8,128)(2,1)S(1)}, u32[]{:S(2)}, u32[]{:S(2)}) collective-permute-start(bf16[64,512]{1,0:T(8,128)(2,1)S(1)} %pad_maximum_fusion.1), channel_id=1, source_target_pairs={{2,0},{4,2},{6,4},{8,6},{10,8},{12,10},{14,12},{16,14},{18,16},{20... | collective-permute-start | bytes 196616 | tf_op jit(solution)/shard_map/ppermute | solution.py:229
  37.1 1.0 convolution_convert_fusion.1.ga_ref
  38.1 51.0 %all_gather.9.glob_ref = bf16[256,512]{1,0:T(8,128)(2,1)} all-gather(bf16[16,512]{1,0:T(8,128)(2,1)S(1)} %get-tuple-element.23), channel_id=1, replica_groups=mesh['ctx'=16,'batch'=2] {'ctx'}, dimensions={0}, use_global_device_ids=true | all-gather | bytes 278528 | tf_op jit(solution)/shard_map/all_gather | solution.py:246
  92.7 11.4 %attend.1 = (bf16[2048,512]{1,0:T(8,128)(2,1)S(1)}, bf16[256,1024]{1,0:T(8,128)(2,1)S(1)}, f32[512,512]{1,0:T(8,128)S(1)}, bf16[64,512]{1,0:T(8,128)(2,1)S(1)}, ...) custom-call(s32[24]{0:T(128)S(1)} %copy-done.22, ...), custom_call_target="tpu_custom_call" | custom-call | tf_op jit(solution)/shard_map/attend/pallas_call | solution.py:249
  104.1 1.4 copy-done.8
  105.4 1.0 copy-done.12
  106.4 22.3 %all_to_all.45 = bf16[16,16,1024]{2,1,0:T(8,128)(2,1)S(1)} all-to-all(bf16[16,16,1024]{2,1,0:T(8,128)(2,1)S(1)} %bitcast.44), channel_id=1, replica_groups=mesh['ctx'=16,'batch'=2] {'ctx'}, dimensions={0} | all-to-all | bytes 1048576 | tf_op jit(solution)/shard_map/all_to_all | solution.py:212
  128.8 4.2 %all-to-all-start.2 = ((bf16[16,128,512]{2,1,0:T(8,128)(2,1)}), bf16[16,128,512]{2,1,0:T(8,128)(2,1)S(1)}, u32[]{:S(2)}, u32[]{:S(2)}) async-start(bf16[16,128,512]{2,1,0:T(8,128)(2,1)} %bitcast.40), calls=%async_computation.2 | async-start | bytes 4194304 | tf_op jit(solution)/shard_map/all_to_all | solution.py:212
  133.5 4.0 %collective-permute-start.3 = (bf16[64,512]{1,0:T(8,128)(2,1)S(1)}, bf16[64,512]{1,0:T(8,128)(2,1)S(1)}, u32[]{:S(2)}, u32[]{:S(2)}) collective-permute-start(bf16[64,512]{1,0:T(8,128)(2,1)S(1)} %copy-done.24), channel_id=1, source_target_pairs={{2,0},{4,2},{6,4},{8,6},{10,8},{12,10},{14,12},{16,14},{18,16},{20... | collective-permute-start | bytes 196616 | tf_op jit(solution)/shard_map/ppermute | solution.py:275
  137.6 1.1 fusion
  138.8 1.5 collective-permute-start.4
  140.4 48.6 %all_gather.10.glob_ref = bf16[256,512]{1,0:T(8,128)(2,1)S(1)} all-gather(bf16[16,512]{1,0:T(8,128)(2,1)S(1)} %get-tuple-element.33), channel_id=1, replica_groups=mesh['ctx'=16,'batch'=2] {'ctx'}, dimensions={0}, use_global_device_ids=true | all-gather | bytes 278528 | tf_op jit(solution)/shard_map/all_gather | solution.py:290
  189.0 24.3 %all_gather.11 = f32[256,512]{1,0:T(8,128)S(1)} all-gather(f32[16,512]{1,0:T(8,128)S(1)} %add.3), channel_id=1, replica_groups=mesh['ctx'=16,'batch'=2] {'ctx'}, dimensions={0}, use_global_device_ids=true | all-gather | bytes 557056 | tf_op jit(solution)/shard_map/all_gather | solution.py:291
  213.4 1.2 copy-done.13
  214.6 2.3 %finish.1 = (bf16[512,256]{1,0:T(8,128)(2,1)}, bf16[512,256]{1,0:T(8,128)(2,1)}) custom-call(s32[1]{0:T(128)} %bitcast.first_ref, s32[16,128]{1,0:T(8,128)S(1)} %copy-done.18, s32[1,256]{1,0:T(1,128)S(1)} %copy-done.20, bf16[2048,512]{1,0:T(8,128)(2,1)S(1)} %bitcast.31, f32[512,512]{1,0:T(8,128)S(1)} %copy-done.13, ...), custom_call_target="tpu_custom_call" | custom-call | tf_op jit(solution)/shard_map/finish/pallas_call | solution.py:294
  (63 shorter events, 7.5 us)
Async XLA Ops:
  0.6 36.5 %copy-start = (bf16[256,512]{1,0:T(8,128)(2,1)S(1)}, bf16[256,512]{1,0:T(8,128)(2,1)}, u32[]{:S(2)}) copy-start(bf16[256,512]{1,0:T(8,128)(2,1)} %param.10) | copy-start | bytes 786436
  5.6 18.3 %copy-start.21 = (s32[24]{0:T(128)}, s32[24]{0:T(128)S(1)}, u32[]{:S(2)}) copy-start(s32[24]{0:T(128)S(1)} %get-tuple-element.21.slot_ref) | copy-start | bytes 292
  26.7 1.4 copy-start.9
  28.7 3.9 %copy-start.3 = (bf16[1,512,256]{2,1,0:T(8,128)(2,1)S(1)}, bf16[1,512,256]{2,1,0:T(8,128)(2,1)}, u32[]{:S(2)}) copy-start(bf16[1,512,256]{2,1,0:T(8,128)(2,1)} %param.8) | copy-start | bytes 786436
  28.7 3.9 %copy-start.6 = (bf16[1,512,256]{2,1,0:T(8,128)(2,1)S(1)}, bf16[1,512,256]{2,1,0:T(8,128)(2,1)}, u32[]{:S(2)}) copy-start(bf16[1,512,256]{2,1,0:T(8,128)(2,1)} %param.9) | copy-start | bytes 786436
  28.7 8.4 %copy-start.7 = (bf16[1,512,512]{2,1,0:T(8,128)(2,1)S(1)}, bf16[1,512,512]{2,1,0:T(8,128)(2,1)}, u32[]{:S(2)}) copy-start(bf16[1,512,512]{2,1,0:T(8,128)(2,1)} %param.11) | copy-start | bytes 1572868
  28.7 60.5 %all-to-all-start.1 = ((bf16[16,128,512]{2,1,0:T(8,128)(2,1)}), bf16[16,128,512]{2,1,0:T(8,128)(2,1)S(1)}, u32[]{:S(2)}, u32[]{:S(2)}) async-start(bf16[16,128,512]{2,1,0:T(8,128)(2,1)} %bitcast.41), calls=%async_computation.1 | async-start | bytes 4194304 | tf_op jit(solution)/shard_map/all_to_all | solution.py:212
  32.6 56.6 %collective-permute-start = (bf16[64,512]{1,0:T(8,128)(2,1)S(1)}, bf16[64,512]{1,0:T(8,128)(2,1)S(1)}, u32[]{:S(2)}, u32[]{:S(2)}) collective-permute-start(bf16[64,512]{1,0:T(8,128)(2,1)S(1)} %pad_maximum_fusion), channel_id=1, source_target_pairs={{0,2},{2,4},{4,6},{6,8},{8,10},{10,12},{12,14},{14,16},{16,18},{18... | collective-permute-start | bytes 196616 | tf_op jit(solution)/shard_map/ppermute | solution.py:228
  32.9 56.2 %collective-permute-start.1 = (bf16[64,512]{1,0:T(8,128)(2,1)S(1)}, bf16[64,512]{1,0:T(8,128)(2,1)S(1)}, u32[]{:S(2)}, u32[]{:S(2)}) collective-permute-start(bf16[64,512]{1,0:T(8,128)(2,1)S(1)} %pad_maximum_fusion.1), channel_id=1, source_target_pairs={{2,0},{4,2},{6,4},{8,6},{10,8},{12,10},{14,12},{16,14},{18,16},{20... | collective-permute-start | bytes 196616 | tf_op jit(solution)/shard_map/ppermute | solution.py:229
  104.1 1.4 copy-start.8
  105.4 1.0 copy-start.12
  106.4 22.3 %copy-start.15 = (bf16[512,256]{1,0:T(8,128)(2,1)}, bf16[512,256]{1,0:T(8,128)(2,1)S(1)}, u32[]{:S(2)}) copy-start(bf16[512,256]{1,0:T(8,128)(2,1)S(1)} %get-tuple-element.25) | copy-start | bytes 786436
  106.4 22.3 %copy-start.23 = (bf16[64,512]{1,0:T(8,128)(2,1)}, bf16[64,512]{1,0:T(8,128)(2,1)S(1)}, u32[]{:S(2)}) copy-start(bf16[64,512]{1,0:T(8,128)(2,1)S(1)} %get-tuple-element.31) | copy-start | bytes 196612
  106.4 22.3 %copy-start.25 = (bf16[64,512]{1,0:T(8,128)(2,1)}, bf16[64,512]{1,0:T(8,128)(2,1)S(1)}, u32[]{:S(2)}) copy-start(bf16[64,512]{1,0:T(8,128)(2,1)S(1)} %get-tuple-element.30) | copy-start | bytes 196612
  128.7 4.3 %copy-start.26 = (bf16[64,512]{1,0:T(8,128)(2,1)S(1)}, bf16[64,512]{1,0:T(8,128)(2,1)}, u32[]{:S(2)}) copy-start(bf16[64,512]{1,0:T(8,128)(2,1)} %copy-done.25) | copy-start | bytes 196612
  128.8 4.8 %copy-start.24 = (bf16[64,512]{1,0:T(8,128)(2,1)S(1)}, bf16[64,512]{1,0:T(8,128)(2,1)}, u32[]{:S(2)}) copy-start(bf16[64,512]{1,0:T(8,128)(2,1)} %copy-done.23) | copy-start | bytes 196612
  128.8 8.8 %copy-start.16 = (bf16[512,256]{1,0:T(8,128)(2,1)S(1)}, bf16[512,256]{1,0:T(8,128)(2,1)}, u32[]{:S(2)}) copy-start(bf16[512,256]{1,0:T(8,128)(2,1)} %copy-done.15) | copy-start | bytes 786436
  128.8 84.6 %all-to-all-start.2 = ((bf16[16,128,512]{2,1,0:T(8,128)(2,1)}), bf16[16,128,512]{2,1,0:T(8,128)(2,1)S(1)}, u32[]{:S(2)}, u32[]{:S(2)}) async-start(bf16[16,128,512]{2,1,0:T(8,128)(2,1)} %bitcast.40), calls=%async_computation.2 | async-start | bytes 4194304 | tf_op jit(solution)/shard_map/all_to_all | solution.py:212
  133.0 80.3 %copy-start.18 = (s32[16,128]{1,0:T(8,128)S(1)}, s32[16,128]{1,0:T(8,128)}, u32[]{:S(2)}) copy-start(s32[16,128]{1,0:T(8,128)} %copy-done.17) | copy-start | bytes 24580
  133.0 80.3 %copy-start.20 = (s32[1,256]{1,0:T(1,128)S(1)}, s32[1,256]{1,0:T(1,128)}, u32[]{:S(2)}) copy-start(s32[1,256]{1,0:T(1,128)} %pos_ref.3) | copy-start | bytes 3076
  133.1 80.3 %collective-permute-start.2 = (bf16[64,512]{1,0:T(8,128)(2,1)S(1)}, bf16[64,512]{1,0:T(8,128)(2,1)S(1)}, u32[]{:S(2)}, u32[]{:S(2)}) collective-permute-start(bf16[64,512]{1,0:T(8,128)(2,1)S(1)} %copy-done.26), channel_id=1, source_target_pairs={{0,2},{2,4},{4,6},{6,8},{8,10},{10,12},{12,14},{14,16},{16,18},{18... | collective-permute-start | bytes 196616 | tf_op jit(solution)/shard_map/ppermute | solution.py:276
  133.5 79.8 %collective-permute-start.3 = (bf16[64,512]{1,0:T(8,128)(2,1)S(1)}, bf16[64,512]{1,0:T(8,128)(2,1)S(1)}, u32[]{:S(2)}, u32[]{:S(2)}) collective-permute-start(bf16[64,512]{1,0:T(8,128)(2,1)S(1)} %copy-done.24), channel_id=1, source_target_pairs={{2,0},{4,2},{6,4},{8,6},{10,8},{12,10},{14,12},{16,14},{18,16},{20... | collective-permute-start | bytes 196616 | tf_op jit(solution)/shard_map/ppermute | solution.py:275
  138.8 50.1 %collective-permute-start.4 = (f32[16,512]{1,0:T(8,128)S(1)}, f32[16,512]{1,0:T(8,128)S(1)}, u32[]{:S(2)}, u32[]{:S(2)}) collective-permute-start(f32[16,512]{1,0:T(8,128)S(1)} %get-tuple-element.36), channel_id=1, source_target_pairs={{0,1},{1,0},{2,3},{3,2},{4,5},{5,4},{6,7},{7,6},{8,9},{9,8},{10,11... | collective-permute-start | bytes 98312 | tf_op jit(solution)/shard_map/ppermute | solution.py:287
  213.4 1.2 copy-start.13
  (10 other events, 8.6 us)

commit v2 on v1

v2 whole, which is shorter than its diff:
```python
import functools

import jax
import jax.numpy as jnp
from jax import lax
from jax.experimental import pallas as pl
from jax.experimental.pallas import tpu as pltpu
from jax.sharding import PartitionSpec as P

BLK = 64
HEADS = 4
RAND = 3
LANES = 128
MIB = 1024 * 1024
LOG2E = 1.4426950408889634

F32 = jnp.float32
BF16 = jnp.bfloat16
VMEM = pl.BlockSpec(memory_space=pltpu.VMEM)
SMEM = pl.BlockSpec(memory_space=pltpu.SMEM)


def params(mib):
    return pltpu.CompilerParams(vmem_limit_bytes=mib * MIB)


def dot(left, right, over_left, over_right):
    return lax.dot_general(
        left, right, (((over_left,), (over_right,)), ((), ())), preferred_element_type=F32
    )


def ask_kernel(half, capacity, strides, here_ref, want_ref, pos_ref, k_ref, v_ref,
               send_ref, place_ref, count_ref, list_ref):
    tokens, width = k_ref.shape
    glob = pos_ref.shape[1]
    query_blocks = tokens // BLK
    requests = query_blocks * RAND
    rows = glob // half
    lists = 2 * capacity
    me = here_ref[0]
    my_half = lax.div(me, half)
    for entry in range(2 * half):
        count_ref[entry] = 0
    for entry in range(half * lists):
        list_ref[entry] = -1

    def request(at, carry):
        wanted = want_ref[at]
        owner = lax.div(wanted, query_blocks)
        rank = jnp.minimum(count_ref[owner], capacity - 1)
        count_ref[owner] = count_ref[owner] + 1
        owner_half = lax.div(owner, half)
        member = owner - owner_half * half
        slot = jnp.where(owner_half == my_half, 0, capacity) + rank
        list_ref[member * lists + slot] = wanted - owner * query_blocks
        for use in range(3):
            place_ref[use * requests + at] = member * strides[use] + slot * BLK
        return carry

    lax.fori_loop(0, requests, request, 0)
    here = me * tokens + lax.broadcasted_iota(jnp.int32, (tokens, glob), 0)
    owned = jnp.where(here == pos_ref[...], 1.0, 0.0).astype(BF16)
    send_ref[:, :width] = dot(owned, k_ref[...], 0, 0).astype(BF16)
    send_ref[:, width : 2 * width] = dot(owned, v_ref[...], 0, 0).astype(BF16)
    lane = lax.broadcasted_iota(jnp.int32, (rows, LANES), 1)
    for member in range(half):
        listed = jnp.full((rows, LANES), -1, jnp.int32)
        for slot in range(lists):
            listed = jnp.where(lane == slot, list_ref[member * lists + slot], listed)
        send_ref[member * rows : (member + 1) * rows, 2 * width :] = listed.astype(F32).astype(BF16)


def heard_kernel(half, got_ref, glob_ref, asked_ref):
    glob = got_ref.shape[0]
    rows = glob // half
    wide = glob_ref.shape[1]
    source = lax.broadcasted_iota(jnp.int32, (half, glob), 1)
    target = lax.broadcasted_iota(jnp.int32, (half, glob), 0)
    pick = jnp.where(source == target * rows, 1.0, 0.0).astype(BF16)
    asked_ref[...] = dot(pick, got_ref[:, wide:], 1, 0).astype(jnp.int32)
    source = lax.broadcasted_iota(jnp.int32, (rows, glob), 1)
    target = lax.broadcasted_iota(jnp.int32, (rows, glob), 0)
    total = jnp.where(lax.rem(source, rows) == target, 1.0, 0.0).astype(BF16)
    glob_ref[...] = dot(total, got_ref[:, :wide], 1, 0).astype(BF16)


def reply_kernel(half, capacity, asked_ref, k_ref, v_ref, mk_ref, mv_ref, glob_ref, mglob_ref, out_ref):
    tokens, width = k_ref.shape
    stride = out_ref.shape[0] // half
    share = (glob_ref[...].astype(F32) + mglob_ref[...].astype(F32)).astype(BF16)
    for member in range(half):
        for slot in range(2 * capacity):
            block = jnp.maximum(asked_ref[member, slot], 0)
            source = pl.ds(pl.multiple_of(block * BLK, BLK), BLK)
            target = pl.ds(member * stride + slot * BLK, BLK)
            own = slot < capacity
            out_ref[target, :width] = (k_ref if own else mk_ref)[source, :]
            out_ref[target, width:] = (v_ref if own else mv_ref)[source, :]
        out_ref[member * stride + 2 * capacity * BLK : (member + 1) * stride, :] = share


def attend_kernel(half, capacity, place_ref, q_ref, ga_ref, og_ref, k_ref, v_ref, low_ref, high_ref, arr_ref,
                  dk_out_ref, dv_out_ref, inner_k_ref, inner_v_ref, elow_ref, ehigh_ref, att_ref, dq_ref,
                  pad_ref, kc_ref, vc_ref, acc_ref, gacc_ref):
    tokens, width = q_ref.shape
    query_blocks = tokens // BLK
    head_size = width // HEADS
    scale = head_size ** (-0.5)
    win, local = 3 * BLK, (3 + RAND) * BLK
    requests = query_blocks * RAND
    pad_ref[:BLK] = low_ref[...]
    pad_ref[BLK : BLK + tokens, :width] = k_ref[...]
    pad_ref[BLK : BLK + tokens, width:] = v_ref[...]
    pad_ref[BLK + tokens :] = high_ref[...]
    skip = 2 * capacity * BLK
    rows = gacc_ref.shape[0] // half
    for member in range(half):
        at = member * (arr_ref.shape[0] // half) + skip
        kc_ref[local + member * rows : local + (member + 1) * rows] = arr_ref[at : at + rows, :width]
        vc_ref[local + member * rows : local + (member + 1) * rows] = arr_ref[at : at + rows, width:]
    acc_ref[...] = jnp.zeros_like(acc_ref)
    gacc_ref[...] = jnp.zeros_like(gacc_ref)
    row_head = lax.broadcasted_iota(jnp.int32, (HEADS * BLK, width), 0) // BLK
    lane_head = lax.broadcasted_iota(jnp.int32, (HEADS * BLK, width), 1) // head_size
    mask = jnp.where(row_head == lane_head, 1.0, 0.0).astype(BF16)
    keep = jnp.where(row_head == lane_head, 1.0, 0.0)

    def by_head(rows):
        return jnp.concatenate([rows] * HEADS, axis=0) * mask

    def own_head(full):
        kept = full * keep
        return sum(kept[h * BLK : (h + 1) * BLK] for h in range(HEADS))

    def one_block(i, carry):
        base = pl.multiple_of(i * BLK, BLK)
        kc_ref[:win] = pad_ref[pl.ds(base, win), :width]
        vc_ref[:win] = pad_ref[pl.ds(base, win), width:]
        for j in range(RAND):
            slot = pl.ds(pl.multiple_of(place_ref[i * RAND + j], BLK), BLK)
            kc_ref[win + j * BLK : win + (j + 1) * BLK] = arr_ref[slot, :width]
            vc_ref[win + j * BLK : win + (j + 1) * BLK] = arr_ref[slot, width:]
        q_by_head = by_head(q_ref[pl.ds(base, BLK), :])
        ga_by_head = by_head(ga_ref[pl.ds(base, BLK), :])
        scores = dot(kc_ref[...], q_by_head, 1, 1) * (scale * LOG2E)
        expo = jnp.exp2(scores - jnp.max(scores, axis=0, keepdims=True))
        probs = expo * (1.0 / jnp.sum(expo, axis=0, keepdims=True))
        probs16 = probs.astype(BF16)
        dprobs = dot(vc_ref[...], ga_by_head, 1, 1)
        delta = jnp.sum(probs16.astype(F32) * dprobs, axis=0, keepdims=True)
        dscores = (probs * (dprobs - delta) * scale).astype(BF16)
        att_ref[pl.ds(base, BLK), :] = own_head(dot(probs16, vc_ref[...], 0, 0)).astype(BF16)
        dq_ref[pl.ds(base, BLK), :] = own_head(dot(dscores, kc_ref[...], 0, 0)).astype(BF16)
        for out_ref, at, part, terms in (
            (dv_out_ref, 1, slice(width, 2 * width), dot(probs16, ga_by_head, 1, 0)),
            (dk_out_ref, 2, slice(0, width), dot(dscores, q_by_head, 1, 0)),
        ):
            acc_ref[pl.ds(base, win), part] += terms[:win]
            gacc_ref[:, part] += terms[local:]
            for j in range(RAND):
                slot = place_ref[at * requests + i * RAND + j]
                out_ref[pl.ds(pl.multiple_of(slot, 16), BLK), :] = terms[
                    win + j * BLK : win + (j + 1) * BLK
                ].astype(BF16)
        return carry

    lax.fori_loop(0, query_blocks, one_block, 0)
    inner_k_ref[...] = acc_ref[BLK : BLK + tokens, :width]
    inner_v_ref[...] = acc_ref[BLK : BLK + tokens, width:]
    elow_ref[...] = acc_ref[:BLK].astype(BF16)
    ehigh_ref[...] = acc_ref[BLK + tokens :].astype(BF16)
    gacc_ref[:, 2 * width :] = dot(att_ref[...], og_ref[...], 0, 0)
    stride = dv_out_ref.shape[0] // half
    for member in range(half):
        for part in range(gacc_ref.shape[1] // width):
            at = member * stride + skip + part * rows
            dv_out_ref[at : at + rows, :] = gacc_ref[
                member * rows : (member + 1) * rows, part * width : (part + 1) * width
            ].astype(BF16)


def fold_kernel(half, capacity, asked_ref, back_ref, inner_ref, own_ref, mirror_ref, *rest):
    stride = back_ref.shape[0] // half
    skip = 2 * capacity * BLK
    mirror_acc = rest[-1]
    own_ref[...] = inner_ref[...]
    mirror_acc[...] = jnp.zeros_like(mirror_acc)
    for member in range(half):
        for slot in range(2 * capacity):
            block = asked_ref[member, slot]
            acc_ref = own_ref if slot < capacity else mirror_acc
            at = member * stride + slot * BLK

            @pl.when(block >= 0)
            def _():
                rows = pl.ds(pl.multiple_of(block * BLK, BLK), BLK)
                acc_ref[rows, :] += back_ref[at : at + BLK, :].astype(F32)

    mirror_ref[...] = mirror_acc[...].astype(BF16)
    if len(rest) > 1:
        share_ref = rest[0]
        rows, wide = share_ref.shape
        width = back_ref.shape[1]
        total = back_ref[skip:stride, :].astype(F32)
        for member in range(1, half):
            total += back_ref[member * stride + skip : (member + 1) * stride, :].astype(F32)
        for part in range(wide // width):
            share_ref[:, part * width : (part + 1) * width] = total[
                part * rows : (part + 1) * rows
            ].astype(BF16)


def finish_kernel(here_ref, pos_ref, own_k_ref, own_v_ref, far_k_ref, far_v_ref, from_low_ref,
                  from_high_ref, glob_ref, dk_ref, dv_ref, acc_ref):
    tokens, width = dk_ref.shape
    glob = glob_ref.shape[0]
    here = here_ref[0] * tokens + lax.broadcasted_iota(jnp.int32, (tokens, glob), 0)
    owned = jnp.where(here == pos_ref[...], 1.0, 0.0).astype(BF16)
    for part, own_ref, far_ref, out_ref in (
        (slice(0, width), own_k_ref, far_k_ref, dk_ref),
        (slice(width, 2 * width), own_v_ref, far_v_ref, dv_ref),
    ):
        acc_ref[...] = own_ref[...] + far_ref[...].astype(F32) + dot(owned, glob_ref[:, part], 1, 0)
        acc_ref[:BLK] += from_low_ref[:, part].astype(F32)
        acc_ref[tokens - BLK :] += from_high_ref[:, part].astype(F32)
        out_ref[...] = acc_ref[...].astype(BF16)


def shards(queries, keys, values, output_weight, output_grad, rand_blocks, glob_pos):
    q, k, v, og = queries[0], keys[0], values[0], output_grad[0]
    tokens, width = q.shape
    model = og.shape[1]
    glob = glob_pos.shape[1]
    query_blocks = tokens // BLK
    span = lax.axis_size("ctx")
    batch = lax.axis_size("batch")
    requests = query_blocks * RAND
    capacity = requests // span + 1
    half = span // 2
    rows = glob // half
    wide = 2 * width + model
    skip = 2 * capacity * BLK
    strides = (skip + rows, skip + rows * wide // width, skip)
    here = lax.axis_index("ctx").astype(jnp.int32).reshape(1)
    shape = jax.ShapeDtypeStruct
    forward = [(i, (i + 1) % span) for i in range(span)]
    backward = [(target, source) for source, target in forward]
    mirror = [(i, (i + half) % span) for i in range(span)]
    halves = [list(range(half)), list(range(half, span))]

    def swap(x):
        return lax.all_to_all(
            x, "ctx", split_axis=0, concat_axis=0, axis_index_groups=halves, tiled=True
        )

    mirror_k = lax.ppermute(k, "ctx", mirror)
    mirror_v = lax.ppermute(v, "ctx", mirror)
    send, places = pl.pallas_call(
        functools.partial(ask_kernel, half, capacity, strides),
        name="ask",
        out_shape=(shape((glob, 2 * width + LANES), BF16), shape((3 * requests,), jnp.int32)),
        in_specs=[SMEM, SMEM, VMEM, VMEM, VMEM],
        out_specs=(VMEM, SMEM),
        scratch_shapes=[pltpu.SMEM((span,), jnp.int32), pltpu.SMEM((span * capacity,), jnp.int32)],
        compiler_params=params(16),
    )(here, rand_blocks.reshape(requests), glob_pos, k, v)
    got = swap(send)
    key_value_edges = [
        jnp.concatenate([k[edge], v[edge]], axis=1)
        for edge in (slice(tokens - BLK, tokens), slice(0, BLK))
    ]
    low = lax.ppermute(key_value_edges[0], "ctx", forward)
    high = lax.ppermute(key_value_edges[1], "ctx", backward)
    grad_attn = dot(og, output_weight, 1, 1).astype(BF16)

    glob_here, asked = pl.pallas_call(
        functools.partial(heard_kernel, half),
        name="heard",
        out_shape=(shape((rows, 2 * width), BF16), shape((half, LANES), jnp.int32)),
        in_specs=[VMEM],
        out_specs=(VMEM,) * 2,
        compiler_params=params(16),
    )(got)
    glob_there = lax.ppermute(glob_here, "ctx", mirror)
    reply = pl.pallas_call(
        functools.partial(reply_kernel, half, capacity),
        name="reply",
        out_shape=shape((half * strides[0], 2 * width), BF16),
        in_specs=[SMEM] + [VMEM] * 6,
        out_specs=VMEM,
        compiler_params=params(16),
    )(asked, k, v, mirror_k, mirror_v, glob_here, glob_there)
    reply, low, high = lax.optimization_barrier((reply, low, high))
    arrived = swap(reply)

    block = (3 + RAND) * BLK + glob
    dk_out, dv_out, inner_k, inner_v, edge_low, edge_high, attention_rows, grad_queries = pl.pallas_call(
        functools.partial(attend_kernel, half, capacity),
        name="attend",
        out_shape=(
            shape((half * strides[2], width), BF16),
            shape((half * strides[1], width), BF16),
            shape((tokens, width), F32),
            shape((tokens, width), F32),
            shape((BLK, 2 * width), BF16),
            shape((BLK, 2 * width), BF16),
            shape((tokens, width), BF16),
            shape((tokens, width), BF16),
        ),
        in_specs=[SMEM] + [VMEM] * 8,
        out_specs=(VMEM,) * 8,
        scratch_shapes=[
            pltpu.VMEM((tokens + 2 * BLK, 2 * width), BF16),
            pltpu.VMEM((block, width), BF16),
            pltpu.VMEM((block, width), BF16),
            pltpu.VMEM((tokens + 2 * BLK, 2 * width), F32),
            pltpu.VMEM((glob, wide), F32),
        ],
        compiler_params=params(32),
    )(places, q, grad_attn, og, k, v, low, high, arrived)

    from_high = lax.ppermute(edge_low, "ctx", backward)
    from_low = lax.ppermute(edge_high, "ctx", forward)
    dv_back = swap(dv_out)
    dk_out, dv_back = lax.optimization_barrier((dk_out, dv_back))
    dk_back = swap(dk_out)

    def fold(name, back, inner, more):
        return pl.pallas_call(
            functools.partial(fold_kernel, half, capacity),
            name=name,
            out_shape=(shape((tokens, width), F32), shape((tokens, width), BF16)) + more,
            in_specs=[SMEM, VMEM, VMEM],
            out_specs=(VMEM,) * (2 + len(more)),
            scratch_shapes=[pltpu.VMEM((tokens, width), F32)],
            compiler_params=params(16),
        )(asked, back, inner)

    own_v, give_v, share = fold("fold_values", dv_back, inner_v, (shape((rows, wide), BF16),))
    weight_share = share[:, 2 * width :]
    glob_sum = share[:, : 2 * width].astype(F32) + lax.ppermute(
        share[:, : 2 * width], "ctx", mirror
    ).astype(F32)
    weight_sum = weight_share.astype(F32) + lax.ppermute(weight_share, "ctx", mirror).astype(F32)
    for step in range(1, batch):
        same, crossed = (
            lax.ppermute(
                weight_share,
                ("ctx", "batch"),
                [
                    (i * batch + b, (i + shift) % span * batch + (b + step) % batch)
                    for i in range(span)
                    for b in range(batch)
                ],
            ).astype(F32)
            for shift in (0, half)
        )
        weight_sum += same + crossed
    far_v = lax.ppermute(give_v, "ctx", mirror)
    dk_back, far_v = lax.optimization_barrier((dk_back, far_v))
    own_k, give_k = fold("fold_keys", dk_back, inner_k, ())
    far_k = lax.ppermute(give_k, "ctx", mirror)
    share = jnp.concatenate([glob_sum, weight_sum], axis=1).astype(BF16)
    share, own_k = lax.optimization_barrier((share, own_k))
    totals = swap(jnp.tile(share, (half, 1)))
    grad_weight = totals[:, 2 * width :].astype(F32)
    attended = dot(attention_rows, output_weight, 1, 0).astype(BF16)

    grad_keys, grad_values = pl.pallas_call(
        finish_kernel,
        name="finish",
        out_shape=(shape((tokens, width), BF16), shape((tokens, width), BF16)),
        in_specs=[SMEM] + [VMEM] * 8,
        out_specs=(VMEM,) * 2,
        scratch_shapes=[pltpu.VMEM((tokens, width), F32)],
        compiler_params=params(24),
    )(here, glob_pos, own_k, own_v, far_k, far_v, from_low, from_high, totals)
    return (
        attended[None],
        grad_queries[None],
        grad_keys[None],
        grad_values[None],
        grad_weight,
    )


def solution(mesh):
    in_specs = (
        P("batch", "ctx", None),
        P("batch", "ctx", None),
        P("batch", "ctx", None),
        P(),
        P("batch", "ctx", None),
        P("batch", "ctx", None),
        P("batch", None),
    )
    out_specs = (
        P("batch", "ctx", None),
        P("batch", "ctx", None),
        P("batch", "ctx", None),
        P("batch", "ctx", None),
        P(),
    )
    return jax.shard_map(shards, mesh=mesh, in_specs=in_specs, out_specs=out_specs, check_vma=False)
```

time: 218 us -> 164 us (0.75)
  blocking collectives: 165 us -> 22.8 us
  waiting for transfers between devices: 0.02 us -> 67.6 us
  starting transfers between devices: 18.6 us -> 37.8 us
    all_gather x3 -> x0, blocking collectives: 124 us -> none  [the longest x1 51 us: shards(): glob_rows = lax.all_gather(glob_mine, 'ctx', axis=0, tiled=True)]
    all_to_all x2 -> x4, waiting for transfers between devices: 0.01 us -> 45.1 us  [swap(): lax.all_to_all(x, 'ctx', split_axis=0, concat_axis=0, axis_index_groups=h...]
    ppermute x1 -> x9, waiting for transfers between devices: 0.01 us -> 22.5 us  [the longest x1 10.5 us: shards(): far_v = lax.ppermute(give_v, 'ctx', mirror)]
    all_to_all x2 -> x1, blocking collectives: 40.6 us -> 22.8 us  [swap(): lax.all_to_all(x, 'ctx', split_axis=0, concat_axis=0, axis_index_groups=h...]
    ppermute x1 -> x9, starting transfers between devices: 1.54 us -> 13.6 us  [the longest x1 4.1 us: shards(): mirror_k = lax.ppermute(k, 'ctx', mirror)]
    all_to_all x2 -> x4, starting transfers between devices: 8.09 us -> 14.9 us  [swap(): lax.all_to_all(x, 'ctx', split_axis=0, concat_axis=0, axis_index_groups=h...]
    unnamed x56 -> x47, local copies, waits for them, and re-layouts: 15.1 us -> 10.8 us
    pallas_call x5 -> x7, Pallas kernels: 16.3 us -> 17.6 us  [the longest x1 11.4 us: shards(): pl.pallas_call(functools.partial(attend_kernel, half, capacity), name='at...]
  transfers between devices with their start and end apart: 7 -> 17, of which waited for: 0 -> 9; matrix products, arithmetic and copies ran while one was open for 1% -> 4% of each run, Pallas kernels for 0% -> 2%
where the time goes in v2:
time: 164 us; the launch traced here: 163 us
  waiting for transfers between devices  67.6 us (41%)
  starting transfers between devices  37.8 us (23%)
  blocking collectives  22.8 us (14%)
  Pallas kernels  17.6 us (11%)
  local copies, waits for them, and re-layouts  13.3 us (8%)
  matrix products  2.47 us (2%)
    all_to_all x4, waiting for transfers between devices, swap(): lax.all_to_all(x, 'ctx', split_axis=0, concat_axis=0, axis_index_groups=h...  45.1 us
    all_to_all x1, blocking collectives, swap(): lax.all_to_all(x, 'ctx', split_axis=0, concat_axis=0, axis_index_groups=h...  22.8 us
    all_to_all x4, starting transfers between devices, swap(): lax.all_to_all(x, 'ctx', split_axis=0, concat_axis=0, axis_index_groups=h...  14.9 us
    pallas_call x1, Pallas kernels, shards(): pl.pallas_call(functools.partial(attend_kernel, half, capacity), name='at...  11.4 us
    unnamed x47, local copies, waits for them, and re-layouts  10.8 us
    ppermute x1, waiting for transfers between devices, shards(): far_v = lax.ppermute(give_v, 'ctx', mirror)  10.5 us
    ppermute x1, starting transfers between devices, shards(): high = lax.ppermute(key_value_edges[1], 'ctx', backward)  4.27 us
    ppermute x1, starting transfers between devices, shards(): mirror_k = lax.ppermute(k, 'ctx', mirror)  4.1 us
  transfers between devices with their start and end apart: 17, of which 9 were waited for; matrix products, arithmetic and copies ran while one was open for 4% of the time, Pallas kernels for 2%

profile of v2, /device:TPU:0, one launch (start us, length us, event | category | flops | bytes accessed | tf_op | source)
XLA Modules:
  0.0 163.3 jit_solution(15117167602227334913)
XLA Ops:
  0.6 4.1 %collective-permute-start = (bf16[512,256]{1,0:T(8,128)(2,1)}, bf16[512,256]{1,0:T(8,128)(2,1)S(1)}, u32[]{:S(2)}, u32[]{:S(2)}) collective-permute-start(bf16[512,256]{1,0:T(8,128)(2,1)} %bitcast.38), channel_id=1, source_target_pairs={{0,16},{2,18},{4,20},{6,22},{8,24},{10,26},{12,28},{14,30},{16,0},... | collective-permute-start | bytes 786440 | tf_op jit(solution)/shard_map/ppermute | solution.py:257
  8.2 2.0 %ask.1 = (bf16[256,640]{1,0:T(8,128)(2,1)}, s32[72]{0:T(128)S(1)}) custom-call(s32[1]{0:T(128)} %bitcast.here_ref, s32[24]{0:T(128)S(1)} %reshape.36.want_ref, s32[1,256]{1,0:T(1,128)S(1)} %copy-done.17, bf16[512,256]{1,0:T(8,128)(2,1)S(1)} %bitcast.39, bf16[512,256]{1,0:T(8,128)(2,1)S(1)} %bitcast.43), custom_call_target="tpu_custom_call" | custom-call | tf_op jit(solution)/shard_map/ask/pallas_call | solution.py:259
  10.3 4.0 %all-to-all-start = ((bf16[8,32,640]{2,1,0:T(8,128)(2,1)}), bf16[8,32,640]{2,1,0:T(8,128)(2,1)S(1)}, u32[]{:S(2)}, u32[]{:S(2)}) async-start(bf16[8,32,640]{2,1,0:T(8,128)(2,1)} %bitcast.5), calls=%async_computation | async-start | bytes 655360 | tf_op jit(solution)/shard_map/all_to_all | solution.py:253
  16.5 4.3 %collective-permute-start.4 = (bf16[64,512]{1,0:T(8,128)(2,1)S(1)}, bf16[64,512]{1,0:T(8,128)(2,1)S(1)}, u32[]{:S(2)}, u32[]{:S(2)}) collective-permute-start(bf16[64,512]{1,0:T(8,128)(2,1)S(1)} %pad_maximum_fusion.1), channel_id=1, source_target_pairs={{2,0},{4,2},{6,4},{8,6},{10,8},{12,10},{14,12},{16,14},{18,16},{20... | collective-permute-start | bytes 196616 | tf_op jit(solution)/shard_map/ppermute | solution.py:274
  20.7 10.8 %all-to-all-done = bf16[8,32,640]{2,1,0:T(8,128)(2,1)S(1)} async-done(((bf16[8,32,640]{2,1,0:T(8,128)(2,1)}), bf16[8,32,640]{2,1,0:T(8,128)(2,1)S(1)}, u32[]{:S(2)}, u32[]{:S(2)}) %all-to-all-start) | async-done | bytes 327712 | tf_op jit(solution)/shard_map/all_to_all | solution.py:253
  31.7 2.0 %collective-permute-start.2 = (bf16[32,512]{1,0:T(8,128)(2,1)S(1)}, bf16[32,512]{1,0:T(8,128)(2,1)S(1)}, u32[]{:S(2)}, u32[]{:S(2)}) collective-permute-start(bf16[32,512]{1,0:T(8,128)(2,1)S(1)} %get-tuple-element.36.glob_ref), channel_id=1, source_target_pairs={{0,16},{2,18},{4,20},{6,22},{8,24},{10,26},{12,28},{14,30},{16,0},... | collective-permute-start | bytes 98312 | tf_op jit(solution)/shard_map/ppermute | solution.py:285
  33.7 3.2 %collective-permute-done.2.mglob_ref = bf16[32,512]{1,0:T(8,128)(2,1)S(1)} collective-permute-done((bf16[32,512]{1,0:T(8,128)(2,1)S(1)}, bf16[32,512]{1,0:T(8,128)(2,1)S(1)}, u32[]{:S(2)}, u32[]{:S(2)}) %collective-permute-start.2) | collective-permute-done | bytes 32800 | tf_op jit(solution)/shard_map/ppermute | solution.py:285
  39.6 1.4 copy-done.1
  41.0 3.8 %all-to-all-start.1 = ((bf16[8,288,512]{2,1,0:T(8,128)(2,1)}), bf16[8,288,512]{2,1,0:T(8,128)(2,1)S(1)}, u32[]{:S(2)}, u32[]{:S(2)}) async-start(bf16[8,288,512]{2,1,0:T(8,128)(2,1)} %bitcast.33), calls=%async_computation.1 | async-start | bytes 4718592 | tf_op jit(solution)/shard_map/all_to_all | solution.py:253
  44.8 1.4 convolution_convert_fusion.1.ga_ref
  46.2 27.0 %all-to-all-done.1 = bf16[8,288,512]{2,1,0:T(8,128)(2,1)S(1)} async-done(((bf16[8,288,512]{2,1,0:T(8,128)(2,1)}), bf16[8,288,512]{2,1,0:T(8,128)(2,1)S(1)}, u32[]{:S(2)}, u32[]{:S(2)}) %all-to-all-start.1) | async-done | bytes 2359328 | tf_op jit(solution)/shard_map/all_to_all | solution.py:253
  75.2 11.4 %attend.1 = (bf16[2048,256]{1,0:T(8,128)(2,1)S(1)}, bf16[3072,256]{1,0:T(8,128)(2,1)S(1)}, f32[512,256]{1,0:T(8,128)S(1)}, f32[512,256]{1,0:T(8,128)S(1)}, bf16[...) custom-call(s32[72]{0:T(128)S(1)} %get-tuple-element.33.place_ref, ...), custom_call_target="tpu_custom_call" | custom-call | tf_op jit(solution)/shard_map/attend/pallas_call | solution.py:298
  86.6 22.8 %all_to_all.54 = bf16[8,384,256]{2,1,0:T(8,128)(2,1)S(1)} all-to-all(bf16[8,384,256]{2,1,0:T(8,128)(2,1)S(1)} %bitcast.47), channel_id=1, replica_groups={{0,2,4,6,8,10,12,14},{16,18,20,22,24,26,28,30},{1,3,5,7,9,11,13,15},{17..., dimensions={0} | all-to-all | bytes 3145728 | tf_op jit(solution)/shard_map/all_to_all | solution.py:253
  109.5 3.6 %all-to-all-start.3 = ((bf16[8,256,256]{2,1,0:T(8,128)(2,1)}), bf16[8,256,256]{2,1,0:T(8,128)(2,1)S(1)}, u32[]{:S(2)}, u32[]{:S(2)}) async-start(bf16[8,256,256]{2,1,0:T(8,128)(2,1)} %bitcast.49), calls=%async_computation.3 | async-start | bytes 2097152 | tf_op jit(solution)/shard_map/all_to_all | solution.py:253
  114.1 1.1 fold_values.1
  115.3 2.4 %collective-permute-start.5 = (bf16[32,512]{1,0:T(8,128)(2,1)S(1)}, bf16[32,512]{1,0:T(8,128)(2,1)S(1)}, u32[]{:S(2)}, u32[]{:S(2)}) collective-permute-start(bf16[32,512]{1,0:T(8,128)(2,1)S(1)} %get-tuple-element.67), channel_id=1, source_target_pairs={{0,16},{2,18},{4,20},{6,22},{8,24},{10,26},{12,28},{14,30},{16,0},... | collective-permute-start | bytes 98312 | tf_op jit(solution)/shard_map/ppermute | solution.py:342
  117.7 1.5 collective-permute-start.7
  119.8 2.3 %collective-permute-start.8 = (bf16[32,512]{1,0:T(8,128)(2,1)S(1)}, bf16[32,512]{1,0:T(8,128)(2,1)S(1)}, u32[]{:S(2)}, u32[]{:S(2)}) collective-permute-start(bf16[32,512]{1,0:T(8,128)(2,1)S(1)} %get-tuple-element.68), channel_id=1, source_target_pairs={{0,17},{1,16},{2,19},{3,18},{4,21},{5,20},{6,23},{7,22},{8,25},{9,... | collective-permute-start | bytes 98312 | tf_op jit(solution)/shard_map/ppermute | solution.py:348
  122.7 3.6 %collective-permute-done.5 = bf16[32,512]{1,0:T(8,128)(2,1)S(1)} collective-permute-done((bf16[32,512]{1,0:T(8,128)(2,1)S(1)}, bf16[32,512]{1,0:T(8,128)(2,1)S(1)}, u32[]{:S(2)}, u32[]{:S(2)}) %collective-permute-start.5) | collective-permute-done | bytes 32800 | tf_op jit(solution)/shard_map/ppermute | solution.py:342
  127.8 10.5 %collective-permute-done.9.far_v_ref = bf16[512,256]{1,0:T(8,128)(2,1)S(1)} collective-permute-done((bf16[512,256]{1,0:T(8,128)(2,1)S(1)}, bf16[512,256]{1,0:T(8,128)(2,1)S(1)}, u32[]{:S(2)}, u32[]{:S(2)}) %collective-permute-start.9) | collective-permute-done | bytes 262176 | tf_op jit(solution)/shard_map/ppermute | solution.py:360
  141.2 3.5 %all-to-all-start.4 = ((bf16[8,32,1024]{2,1,0:T(8,128)(2,1)}), bf16[8,32,1024]{2,1,0:T(8,128)(2,1)S(1)}, u32[]{:S(2)}, u32[]{:S(2)}) async-start(bf16[8,32,1024]{2,1,0:T(8,128)(2,1)} %tile.2), calls=%async_computation.4 | async-start | bytes 1048576 | tf_op jit(solution)/shard_map/all_to_all | solution.py:253
  145.1 4.1 %collective-permute-start.12 = (bf16[64,512]{1,0:T(8,128)(2,1)S(1)}, bf16[64,512]{1,0:T(8,128)(2,1)S(1)}, u32[]{:S(2)}, u32[]{:S(2)}) collective-permute-start(bf16[64,512]{1,0:T(8,128)(2,1)S(1)} %copy-done.20), channel_id=1, source_target_pairs={{2,0},{4,2},{6,4},{8,6},{10,8},{12,10},{14,12},{16,14},{18,16},{20... | collective-permute-start | bytes 196616 | tf_op jit(solution)/shard_map/ppermute | solution.py:323
  150.3 7.3 %all-to-all-done.4 = bf16[8,32,1024]{2,1,0:T(8,128)(2,1)S(1)} async-done(((bf16[8,32,1024]{2,1,0:T(8,128)(2,1)}), bf16[8,32,1024]{2,1,0:T(8,128)(2,1)S(1)}, u32[]{:S(2)}, u32[]{:S(2)}) %all-to-all-start.4) | async-done | bytes 524320 | tf_op jit(solution)/shard_map/all_to_all | solution.py:253
  158.5 3.7 %collective-permute-done.10.far_k_ref = bf16[512,256]{1,0:T(8,128)(2,1)S(1)} collective-permute-done((bf16[512,256]{1,0:T(8,128)(2,1)S(1)}, bf16[512,256]{1,0:T(8,128)(2,1)S(1)}, u32[]{:S(2)}, u32[]{:S(2)}) %collective-permute-start.10) | collective-permute-done | bytes 262176 | tf_op jit(solution)/shard_map/ppermute | solution.py:363
  (77 shorter events, 20.5 us)
Async XLA Ops:
  0.6 44.2 %copy-start = (bf16[256,512]{1,0:T(8,128)(2,1)S(1)}, bf16[256,512]{1,0:T(8,128)(2,1)}, u32[]{:S(2)}) copy-start(bf16[256,512]{1,0:T(8,128)(2,1)} %param.10) | copy-start | bytes 786436
  0.6 33.1 %collective-permute-start = (bf16[512,256]{1,0:T(8,128)(2,1)}, bf16[512,256]{1,0:T(8,128)(2,1)S(1)}, u32[]{:S(2)}, u32[]{:S(2)}) collective-permute-start(bf16[512,256]{1,0:T(8,128)(2,1)} %bitcast.38), channel_id=1, source_target_pairs={{0,16},{2,18},{4,20},{6,22},{8,24},{10,26},{12,28},{14,30},{16,0},... | collective-permute-start | bytes 786440 | tf_op jit(solution)/shard_map/ppermute | solution.py:257
  4.7 29.0 %collective-permute-start.1 = (bf16[512,256]{1,0:T(8,128)(2,1)}, bf16[512,256]{1,0:T(8,128)(2,1)S(1)}, u32[]{:S(2)}, u32[]{:S(2)}) collective-permute-start(bf16[512,256]{1,0:T(8,128)(2,1)} %bitcast.42), channel_id=1, source_target_pairs={{0,16},{2,18},{4,20},{6,22},{8,24},{10,26},{12,28},{14,30},{16,0},... | collective-permute-start | bytes 786440 | tf_op jit(solution)/shard_map/ppermute | solution.py:258
  10.3 21.2 %all-to-all-start = ((bf16[8,32,640]{2,1,0:T(8,128)(2,1)}), bf16[8,32,640]{2,1,0:T(8,128)(2,1)S(1)}, u32[]{:S(2)}, u32[]{:S(2)}) async-start(bf16[8,32,640]{2,1,0:T(8,128)(2,1)} %bitcast.5), calls=%async_computation | async-start | bytes 655360 | tf_op jit(solution)/shard_map/all_to_all | solution.py:253
  15.9 25.1 %collective-permute-start.3 = (bf16[64,512]{1,0:T(8,128)(2,1)S(1)}, bf16[64,512]{1,0:T(8,128)(2,1)S(1)}, u32[]{:S(2)}, u32[]{:S(2)}) collective-permute-start(bf16[64,512]{1,0:T(8,128)(2,1)S(1)} %pad_maximum_fusion), channel_id=1, source_target_pairs={{0,2},{2,4},{4,6},{6,8},{8,10},{10,12},{12,14},{14,16},{16,18},{18... | collective-permute-start | bytes 196616 | tf_op jit(solution)/shard_map/ppermute | solution.py:273
  16.5 24.5 %collective-permute-start.4 = (bf16[64,512]{1,0:T(8,128)(2,1)S(1)}, bf16[64,512]{1,0:T(8,128)(2,1)S(1)}, u32[]{:S(2)}, u32[]{:S(2)}) collective-permute-start(bf16[64,512]{1,0:T(8,128)(2,1)S(1)} %pad_maximum_fusion.1), channel_id=1, source_target_pairs={{2,0},{4,2},{6,4},{8,6},{10,8},{12,10},{14,12},{16,14},{18,16},{20... | collective-permute-start | bytes 196616 | tf_op jit(solution)/shard_map/ppermute | solution.py:274
  31.7 5.2 %collective-permute-start.2 = (bf16[32,512]{1,0:T(8,128)(2,1)S(1)}, bf16[32,512]{1,0:T(8,128)(2,1)S(1)}, u32[]{:S(2)}, u32[]{:S(2)}) collective-permute-start(bf16[32,512]{1,0:T(8,128)(2,1)S(1)} %get-tuple-element.36.glob_ref), channel_id=1, source_target_pairs={{0,16},{2,18},{4,20},{6,22},{8,24},{10,26},{12,28},{14,30},{16,0},... | collective-permute-start | bytes 98312 | tf_op jit(solution)/shard_map/ppermute | solution.py:285
  41.0 32.2 %copy-start.4 = (bf16[1,512,256]{2,1,0:T(8,128)(2,1)S(1)}, bf16[1,512,256]{2,1,0:T(8,128)(2,1)}, u32[]{:S(2)}) copy-start(bf16[1,512,256]{2,1,0:T(8,128)(2,1)} %param.8) | copy-start | bytes 786436
  41.0 32.2 %copy-start.7 = (bf16[1,512,256]{2,1,0:T(8,128)(2,1)S(1)}, bf16[1,512,256]{2,1,0:T(8,128)(2,1)}, u32[]{:S(2)}) copy-start(bf16[1,512,256]{2,1,0:T(8,128)(2,1)} %param.9) | copy-start | bytes 786436
  41.0 32.2 %all-to-all-start.1 = ((bf16[8,288,512]{2,1,0:T(8,128)(2,1)}), bf16[8,288,512]{2,1,0:T(8,128)(2,1)S(1)}, u32[]{:S(2)}, u32[]{:S(2)}) async-start(bf16[8,288,512]{2,1,0:T(8,128)(2,1)} %bitcast.33), calls=%async_computation.1 | async-start | bytes 4718592 | tf_op jit(solution)/shard_map/all_to_all | solution.py:253
  109.5 28.8 %all-to-all-start.3 = ((bf16[8,256,256]{2,1,0:T(8,128)(2,1)}), bf16[8,256,256]{2,1,0:T(8,128)(2,1)S(1)}, u32[]{:S(2)}, u32[]{:S(2)}) async-start(bf16[8,256,256]{2,1,0:T(8,128)(2,1)} %bitcast.49), calls=%async_computation.3 | async-start | bytes 2097152 | tf_op jit(solution)/shard_map/all_to_all | solution.py:253
  115.2 29.5 %copy-start.22 = (bf16[64,512]{1,0:T(8,128)(2,1)S(1)}, bf16[64,512]{1,0:T(8,128)(2,1)}, u32[]{:S(2)}) copy-start(bf16[64,512]{1,0:T(8,128)(2,1)} %copy-done.21) | copy-start | bytes 196612
  115.2 29.9 %copy-start.20 = (bf16[64,512]{1,0:T(8,128)(2,1)S(1)}, bf16[64,512]{1,0:T(8,128)(2,1)}, u32[]{:S(2)}) copy-start(bf16[64,512]{1,0:T(8,128)(2,1)} %copy-done.19) | copy-start | bytes 196612
  115.3 34.0 %copy-start.16 = (bf16[512,256]{1,0:T(8,128)(2,1)S(1)}, bf16[512,256]{1,0:T(8,128)(2,1)}, u32[]{:S(2)}) copy-start(bf16[512,256]{1,0:T(8,128)(2,1)} %copy-done.15) | copy-start | bytes 786436
  115.3 11.0 %collective-permute-start.5 = (bf16[32,512]{1,0:T(8,128)(2,1)S(1)}, bf16[32,512]{1,0:T(8,128)(2,1)S(1)}, u32[]{:S(2)}, u32[]{:S(2)}) collective-permute-start(bf16[32,512]{1,0:T(8,128)(2,1)S(1)} %get-tuple-element.67), channel_id=1, source_target_pairs={{0,16},{2,18},{4,20},{6,22},{8,24},{10,26},{12,28},{14,30},{16,0},... | collective-permute-start | bytes 98312 | tf_op jit(solution)/shard_map/ppermute | solution.py:342
  117.7 8.6 %collective-permute-start.7 = (bf16[32,512]{1,0:T(8,128)(2,1)S(1)}, bf16[32,512]{1,0:T(8,128)(2,1)S(1)}, u32[]{:S(2)}, u32[]{:S(2)}) collective-permute-start(bf16[32,512]{1,0:T(8,128)(2,1)S(1)} %get-tuple-element.68), channel_id=1, source_target_pairs={{0,1},{1,0},{2,3},{3,2},{4,5},{5,4},{6,7},{7,6},{8,9},{9,8},{10,11... | collective-permute-start | bytes 98312 | tf_op jit(solution)/shard_map/ppermute | solution.py:348
  119.3 7.8 %collective-permute-start.6 = (bf16[32,512]{1,0:T(8,128)(2,1)S(1)}, bf16[32,512]{1,0:T(8,128)(2,1)S(1)}, u32[]{:S(2)}, u32[]{:S(2)}) collective-permute-start(bf16[32,512]{1,0:T(8,128)(2,1)S(1)} %get-tuple-element.68), channel_id=1, source_target_pairs={{0,16},{2,18},{4,20},{6,22},{8,24},{10,26},{12,28},{14,30},{16,0},... | collective-permute-start | bytes 98312 | tf_op jit(solution)/shard_map/ppermute | solution.py:345
  119.8 7.9 %collective-permute-start.8 = (bf16[32,512]{1,0:T(8,128)(2,1)S(1)}, bf16[32,512]{1,0:T(8,128)(2,1)S(1)}, u32[]{:S(2)}, u32[]{:S(2)}) collective-permute-start(bf16[32,512]{1,0:T(8,128)(2,1)S(1)} %get-tuple-element.68), channel_id=1, source_target_pairs={{0,17},{1,16},{2,19},{3,18},{4,21},{5,20},{6,23},{7,22},{8,25},{9,... | collective-permute-start | bytes 98312 | tf_op jit(solution)/shard_map/ppermute | solution.py:348
  122.1 16.1 %collective-permute-start.9 = (bf16[512,256]{1,0:T(8,128)(2,1)S(1)}, bf16[512,256]{1,0:T(8,128)(2,1)S(1)}, u32[]{:S(2)}, u32[]{:S(2)}) collective-permute-start(bf16[512,256]{1,0:T(8,128)(2,1)S(1)} %get-tuple-element.48), channel_id=1, source_target_pairs={{0,16},{2,18},{4,20},{6,22},{8,24},{10,26},{12,28},{14,30},{16,0},... | collective-permute-start | bytes 786440 | tf_op jit(solution)/shard_map/ppermute | solution.py:360
  139.3 22.9 %copy-start.18 = (s32[1,256]{1,0:T(1,128)S(1)}, s32[1,256]{1,0:T(1,128)}, u32[]{:S(2)}) copy-start(s32[1,256]{1,0:T(1,128)} %pos_ref.3) | copy-start | bytes 3076
  141.2 16.4 %all-to-all-start.4 = ((bf16[8,32,1024]{2,1,0:T(8,128)(2,1)}), bf16[8,32,1024]{2,1,0:T(8,128)(2,1)S(1)}, u32[]{:S(2)}, u32[]{:S(2)}) async-start(bf16[8,32,1024]{2,1,0:T(8,128)(2,1)} %tile.2), calls=%async_computation.4 | async-start | bytes 1048576 | tf_op jit(solution)/shard_map/all_to_all | solution.py:253
  144.7 13.8 %collective-permute-start.11 = (bf16[64,512]{1,0:T(8,128)(2,1)S(1)}, bf16[64,512]{1,0:T(8,128)(2,1)S(1)}, u32[]{:S(2)}, u32[]{:S(2)}) collective-permute-start(bf16[64,512]{1,0:T(8,128)(2,1)S(1)} %copy-done.22), channel_id=1, source_target_pairs={{0,2},{2,4},{4,6},{6,8},{8,10},{10,12},{12,14},{14,16},{16,18},{18... | collective-permute-start | bytes 196616 | tf_op jit(solution)/shard_map/ppermute | solution.py:324
  145.1 13.4 %collective-permute-start.12 = (bf16[64,512]{1,0:T(8,128)(2,1)S(1)}, bf16[64,512]{1,0:T(8,128)(2,1)S(1)}, u32[]{:S(2)}, u32[]{:S(2)}) collective-permute-start(bf16[64,512]{1,0:T(8,128)(2,1)S(1)} %copy-done.20), channel_id=1, source_target_pairs={{2,0},{4,2},{6,4},{8,6},{10,8},{12,10},{14,12},{16,14},{18,16},{20... | collective-permute-start | bytes 196616 | tf_op jit(solution)/shard_map/ppermute | solution.py:323
  149.2 13.0 %collective-permute-start.10 = (bf16[512,256]{1,0:T(8,128)(2,1)S(1)}, bf16[512,256]{1,0:T(8,128)(2,1)S(1)}, u32[]{:S(2)}, u32[]{:S(2)}) collective-permute-start(bf16[512,256]{1,0:T(8,128)(2,1)S(1)} %get-tuple-element.54), channel_id=1, source_target_pairs={{0,16},{2,18},{4,20},{6,22},{8,24},{10,26},{12,28},{14,30},{16,0},... | collective-permute-start | bytes 786440 | tf_op jit(solution)/shard_map/ppermute | solution.py:363
  (16 other events, 147.3 us)

commit v3 on v2

--- a/solution.py
+++ b/solution.py
@@ -31,7 +31,7 @@
 
 
 def ask_kernel(half, capacity, strides, here_ref, want_ref, pos_ref, k_ref, v_ref,
-               send_ref, place_ref, count_ref, list_ref):
+               send_ref, place_ref, v_out_ref, count_ref, list_ref):
     tokens, width = k_ref.shape
     glob = pos_ref.shape[1]
     query_blocks = tokens // BLK
@@ -63,6 +63,7 @@
     owned = jnp.where(here == pos_ref[...], 1.0, 0.0).astype(BF16)
     send_ref[:, :width] = dot(owned, k_ref[...], 0, 0).astype(BF16)
     send_ref[:, width : 2 * width] = dot(owned, v_ref[...], 0, 0).astype(BF16)
+    v_out_ref[...] = v_ref[...]
     lane = lax.broadcasted_iota(jnp.int32, (rows, LANES), 1)
     for member in range(half):
         listed = jnp.full((rows, LANES), -1, jnp.int32)
@@ -165,7 +166,7 @@
                 ].astype(BF16)
         return carry
 
-    lax.fori_loop(0, query_blocks, one_block, 0)
+    lax.fori_loop(0, query_blocks, one_block, 0, unroll=4)
     inner_k_ref[...] = acc_ref[BLK : BLK + tokens, :width]
     inner_v_ref[...] = acc_ref[BLK : BLK + tokens, width:]
     elow_ref[...] = acc_ref[:BLK].astype(BF16)
@@ -180,10 +181,10 @@
             ].astype(BF16)
 
 
-def fold_kernel(half, capacity, asked_ref, back_ref, inner_ref, own_ref, mirror_ref, *rest):
+def fold_kernel(half, capacity, asked_ref, back_ref, inner_ref, own_ref, give_ref, mirror_acc):
+    tokens = own_ref.shape[0]
     stride = back_ref.shape[0] // half
     skip = 2 * capacity * BLK
-    mirror_acc = rest[-1]
     own_ref[...] = inner_ref[...]
     mirror_acc[...] = jnp.zeros_like(mirror_acc)
     for member in range(half):
@@ -197,31 +198,37 @@
                 rows = pl.ds(pl.multiple_of(block * BLK, BLK), BLK)
                 acc_ref[rows, :] += back_ref[at : at + BLK, :].astype(F32)
 
-    mirror_ref[...] = mirror_acc[...].astype(BF16)
-    if len(rest) > 1:
-        share_ref = rest[0]
-        rows, wide = share_ref.shape
-        width = back_ref.shape[1]
+    give_ref[:tokens] = mirror_acc[...].astype(BF16)
+    if stride > skip:
         total = back_ref[skip:stride, :].astype(F32)
         for member in range(1, half):
             total += back_ref[member * stride + skip : (member + 1) * stride, :].astype(F32)
-        for part in range(wide // width):
-            share_ref[:, part * width : (part + 1) * width] = total[
-                part * rows : (part + 1) * rows
-            ].astype(BF16)
-
-
-def finish_kernel(here_ref, pos_ref, own_k_ref, own_v_ref, far_k_ref, far_v_ref, from_low_ref,
-                  from_high_ref, glob_ref, dk_ref, dv_ref, acc_ref):
+        give_ref[tokens:] = total.astype(BF16)
+
+
+def finish_kernel(half, here_ref, pos_ref, own_k_ref, own_v_ref, far_k_ref, far_v_ref, from_low_ref,
+                  from_high_ref, total_ref, dk_ref, dv_ref, weight_ref, acc_ref, glob_ref):
     tokens, width = dk_ref.shape
-    glob = glob_ref.shape[0]
+    glob = pos_ref.shape[1]
+    rows = glob // half
+    stride = total_ref.shape[0] // half
     here = here_ref[0] * tokens + lax.broadcasted_iota(jnp.int32, (tokens, glob), 0)
     owned = jnp.where(here == pos_ref[...], 1.0, 0.0).astype(BF16)
+    for member in range(half):
+        mine = slice(member * rows, (member + 1) * rows)
+        for part in range(stride // rows):
+            at = member * stride + part * rows
+            if part < 2:
+                glob_ref[mine, part * width : (part + 1) * width] = total_ref[at : at + rows, :]
+            else:
+                weight_ref[mine, (part - 2) * width : (part - 1) * width] = total_ref[
+                    at : at + rows, :
+                ].astype(F32)
     for part, own_ref, far_ref, out_ref in (
         (slice(0, width), own_k_ref, far_k_ref, dk_ref),
         (slice(width, 2 * width), own_v_ref, far_v_ref, dv_ref),
     ):
-        acc_ref[...] = own_ref[...] + far_ref[...].astype(F32) + dot(owned, glob_ref[:, part], 1, 0)
+        acc_ref[...] = own_ref[...] + far_ref[:tokens].astype(F32) + dot(owned, glob_ref[:, part], 1, 0)
         acc_ref[:BLK] += from_low_ref[:, part].astype(F32)
         acc_ref[tokens - BLK :] += from_high_ref[:, part].astype(F32)
         out_ref[...] = acc_ref[...].astype(BF16)
@@ -255,17 +262,21 @@
         )
 
     mirror_k = lax.ppermute(k, "ctx", mirror)
-    mirror_v = lax.ppermute(v, "ctx", mirror)
-    send, places = pl.pallas_call(
+    send, places, v_after = pl.pallas_call(
         functools.partial(ask_kernel, half, capacity, strides),
         name="ask",
-        out_shape=(shape((glob, 2 * width + LANES), BF16), shape((3 * requests,), jnp.int32)),
+        out_shape=(
+            shape((glob, 2 * width + LANES), BF16),
+            shape((3 * requests,), jnp.int32),
+            shape((tokens, width), BF16),
+        ),
         in_specs=[SMEM, SMEM, VMEM, VMEM, VMEM],
-        out_specs=(VMEM, SMEM),
+        out_specs=(VMEM, SMEM, VMEM),
         scratch_shapes=[pltpu.SMEM((span,), jnp.int32), pltpu.SMEM((span * capacity,), jnp.int32)],
-        compiler_params=params(16),
+        compiler_params=params(60),
     )(here, rand_blocks.reshape(requests), glob_pos, k, v)
     got = swap(send)
+    mirror_v = lax.ppermute(v_after, "ctx", mirror)
     key_value_edges = [
         jnp.concatenate([k[edge], v[edge]], axis=1)
         for edge in (slice(tokens - BLK, tokens), slice(0, BLK))
@@ -289,7 +300,7 @@
         out_shape=shape((half * strides[0], 2 * width), BF16),
         in_specs=[SMEM] + [VMEM] * 6,
         out_specs=VMEM,
-        compiler_params=params(16),
+        compiler_params=params(60),
     )(asked, k, v, mirror_k, mirror_v, glob_here, glob_there)
     reply, low, high = lax.optimization_barrier((reply, low, high))
     arrived = swap(reply)
@@ -330,19 +341,19 @@
         return pl.pallas_call(
             functools.partial(fold_kernel, half, capacity),
             name=name,
-            out_shape=(shape((tokens, width), F32), shape((tokens, width), BF16)) + more,
+            out_shape=(shape((tokens, width), F32), shape((tokens + more, width), BF16)),
             in_specs=[SMEM, VMEM, VMEM],
-            out_specs=(VMEM,) * (2 + len(more)),
+            out_specs=(VMEM,) * 2,
             scratch_shapes=[pltpu.VMEM((tokens, width), F32)],
             compiler_params=params(16),
         )(asked, back, inner)
 
-    own_v, give_v, share = fold("fold_values", dv_back, inner_v, (shape((rows, wide), BF16),))
-    weight_share = share[:, 2 * width :]
-    glob_sum = share[:, : 2 * width].astype(F32) + lax.ppermute(
-        share[:, : 2 * width], "ctx", mirror
-    ).astype(F32)
-    weight_sum = weight_share.astype(F32) + lax.ppermute(weight_share, "ctx", mirror).astype(F32)
+    own_v, give_v = fold("fold_values", dv_back, inner_v, strides[1] - skip)
+    far_v = lax.ppermute(give_v, "ctx", mirror)
+    far_v, from_high, from_low = lax.optimization_barrier((far_v, from_high, from_low))
+    weight_at = tokens + 2 * rows
+    weight_share = give_v[weight_at:]
+    weight_sum = weight_share.astype(F32) + far_v[weight_at:].astype(F32)
     for step in range(1, batch):
         same, crossed = (
             lax.ppermute(
@@ -357,23 +368,28 @@
             for shift in (0, half)
         )
         weight_sum += same + crossed
-    far_v = lax.ppermute(give_v, "ctx", mirror)
-    dk_back, far_v = lax.optimization_barrier((dk_back, far_v))
-    own_k, give_k = fold("fold_keys", dk_back, inner_k, ())
+    glob_sum = give_v[tokens:weight_at].astype(F32) + far_v[tokens:weight_at].astype(F32)
+    share = jnp.concatenate([glob_sum, weight_sum], axis=0).astype(BF16)
+    own_k, give_k = fold("fold_keys", dk_back, inner_k, 0)
     far_k = lax.ppermute(give_k, "ctx", mirror)
-    share = jnp.concatenate([glob_sum, weight_sum], axis=1).astype(BF16)
     share, own_k = lax.optimization_barrier((share, own_k))
     totals = swap(jnp.tile(share, (half, 1)))
-    grad_weight = totals[:, 2 * width :].astype(F32)
     attended = dot(attention_rows, output_weight, 1, 0).astype(BF16)
 
-    grad_keys, grad_values = pl.pallas_call(
-        finish_kernel,
+    grad_keys, grad_values, grad_weight = pl.pallas_call(
+        functools.partial(finish_kernel, half),
         name="finish",
-        out_shape=(shape((tokens, width), BF16), shape((tokens, width), BF16)),
+        out_shape=(
+            shape((tokens, width), BF16),
+            shape((tokens, width), BF16),
+            shape((width, model), F32),
+        ),
         in_specs=[SMEM] + [VMEM] * 8,
-        out_specs=(VMEM,) * 2,
-        scratch_shapes=[pltpu.VMEM((tokens, width), F32)],
+        out_specs=(VMEM,) * 3,
+        scratch_shapes=[
+            pltpu.VMEM((tokens, width), F32),
+            pltpu.VMEM((glob, 2 * width), BF16),
+        ],
         compiler_params=params(24),
     )(here, glob_pos, own_k, own_v, far_k, far_v, from_low, from_high, totals)
     return (

time: 164 us -> 152 us (0.927)
  waiting for transfers between devices: 67.6 us -> 62 us
  starting transfers between devices: 37.8 us -> 33.5 us
  local copies, waits for them, and re-layouts: 13.3 us -> 9.55 us
    all_to_all x4, waiting for transfers between devices: 45.1 us -> 32.6 us  [swap(): lax.all_to_all(x, 'ctx', split_axis=0, concat_axis=0, axis_index_groups=h...]
    ppermute x1, waiting for transfers between devices: 10.5 us -> 0.01 us  [shards(): far_v = lax.ppermute(give_v, 'ctx', mirror)]
    ppermute x1, waiting for transfers between devices: 0.01 us -> 9.89 us  [shards(): from_high = lax.ppermute(edge_low, 'ctx', backward)]
    ppermute x1, waiting for transfers between devices: 3.71 us -> 8.69 us  [shards(): far_k = lax.ppermute(give_k, 'ctx', mirror)]
    ppermute x1, waiting for transfers between devices: 0.01 us -> 4.46 us  [shards(): from_low = lax.ppermute(edge_high, 'ctx', forward)]
    unnamed x47 -> x53, local copies, waits for them, and re-layouts: 10.8 us -> 6.57 us
    ppermute x3 -> x1, starting transfers between devices: 3.07 us -> 0.33 us  [shards(): mirror_v = lax.ppermute(v_after, 'ctx', mirror)]
    ppermute x1, waiting for transfers between devices: 3.2 us -> 1.14 us  [shards(): glob_there = lax.ppermute(glob_here, 'ctx', mirror)]
  transfers between devices with their start and end apart: 17 -> 15, of which waited for: 9 -> 8; matrix products, arithmetic and copies ran while one was open for 4% -> 4% of each run, Pallas kernels for 2% -> 4%
where the time goes in v3:
time: 152 us; the launch traced here: 151 us
  waiting for transfers between devices  62 us (41%)
  starting transfers between devices  33.5 us (22%)
  blocking collectives  22.9 us (15%)
  Pallas kernels  18.4 us (12%)
  local copies, waits for them, and re-layouts  9.55 us (6%)
  matrix products  3.41 us (2%)
    all_to_all x4, waiting for transfers between devices, swap(): lax.all_to_all(x, 'ctx', split_axis=0, concat_axis=0, axis_index_groups=h...  32.6 us
    all_to_all x1, blocking collectives, swap(): lax.all_to_all(x, 'ctx', split_axis=0, concat_axis=0, axis_index_groups=h...  22.9 us
    all_to_all x4, starting transfers between devices, swap(): lax.all_to_all(x, 'ctx', split_axis=0, concat_axis=0, axis_index_groups=h...  14.7 us
    ppermute x1, waiting for transfers between devices, shards(): from_high = lax.ppermute(edge_low, 'ctx', backward)  9.89 us
    pallas_call x1, Pallas kernels, shards(): pl.pallas_call(functools.partial(attend_kernel, half, capacity), name='at...  9.38 us
    ppermute x1, waiting for transfers between devices, shards(): far_k = lax.ppermute(give_k, 'ctx', mirror)  8.69 us
    unnamed x53, local copies, waits for them, and re-layouts  6.57 us
    ppermute x1, waiting for transfers between devices, shards(): mirror_v = lax.ppermute(v_after, 'ctx', mirror)  5.18 us
  transfers between devices with their start and end apart: 15, of which 8 were waited for; matrix products, arithmetic and copies ran while one was open for 4% of the time, Pallas kernels for 4%

profile of v3, /device:TPU:0, one launch (start us, length us, event | category | flops | bytes accessed | tf_op | source)
XLA Modules:
  0.0 150.7 jit_solution(11702943637494278073)
XLA Ops:
  0.6 4.1 %collective-permute-start = (bf16[512,256]{1,0:T(8,128)(2,1)}, bf16[512,256]{1,0:T(8,128)(2,1)S(1)}, u32[]{:S(2)}, u32[]{:S(2)}) collective-permute-start(bf16[512,256]{1,0:T(8,128)(2,1)} %bitcast.35), channel_id=1, source_target_pairs={{0,16},{2,18},{4,20},{6,22},{8,24},{10,26},{12,28},{14,30},{16,0},... | collective-permute-start | bytes 786440 | tf_op jit(solution)/shard_map/ppermute | solution.py:264
  6.1 2.6 %ask.1 = (bf16[256,640]{1,0:T(8,128)(2,1)}, s32[72]{0:T(128)}, bf16[512,256]{1,0:T(8,128)(2,1)}) custom-call(s32[1]{0:T(128)} %bitcast.here_ref, s32[24]{0:T(128)} %reshape.36.want_ref, s32[1,256]{1,0:T(1,128)} %pos_ref.3, bf16[512,256]{1,0:T(8,128)(2,1)} %bitcast.36, bf16[512,256]{1,0:T(8,128)(2,1)} %bitcast.39), custom_call_target="tpu_custom_call" | custom-call | tf_op jit(solution)/shard_map/ask/pallas_call | solution.py:265
  8.7 3.8 %all-to-all-start = ((bf16[8,32,640]{2,1,0:T(8,128)(2,1)}), bf16[8,32,640]{2,1,0:T(8,128)(2,1)S(1)}, u32[]{:S(2)}, u32[]{:S(2)}) async-start(bf16[8,32,640]{2,1,0:T(8,128)(2,1)} %bitcast.49), calls=%async_computation | async-start | bytes 655360 | tf_op jit(solution)/shard_map/all_to_all | solution.py:260
  14.7 4.3 %collective-permute-start.4 = (bf16[64,512]{1,0:T(8,128)(2,1)S(1)}, bf16[64,512]{1,0:T(8,128)(2,1)S(1)}, u32[]{:S(2)}, u32[]{:S(2)}) collective-permute-start(bf16[64,512]{1,0:T(8,128)(2,1)S(1)} %pad_maximum_fusion.1), channel_id=1, source_target_pairs={{2,0},{4,2},{6,4},{8,6},{10,8},{12,10},{14,12},{16,14},{18,16},{20... | collective-permute-start | bytes 196616 | tf_op jit(solution)/shard_map/ppermute | solution.py:285
  18.9 3.7 %all-to-all-done = bf16[8,32,640]{2,1,0:T(8,128)(2,1)S(1)} async-done(((bf16[8,32,640]{2,1,0:T(8,128)(2,1)}), bf16[8,32,640]{2,1,0:T(8,128)(2,1)S(1)}, u32[]{:S(2)}, u32[]{:S(2)}) %all-to-all-start) | async-done | bytes 327712 | tf_op jit(solution)/shard_map/all_to_all | solution.py:260
  23.9 5.2 %collective-permute-done.1.mv_ref = bf16[512,256]{1,0:T(8,128)(2,1)S(1)} collective-permute-done((bf16[512,256]{1,0:T(8,128)(2,1)}, bf16[512,256]{1,0:T(8,128)(2,1)S(1)}, u32[]{:S(2)}, u32[]{:S(2)}) %collective-permute-start.1) | collective-permute-done | bytes 262176 | tf_op jit(solution)/shard_map/ppermute | solution.py:279
  30.9 2.8 %reply.1 = bf16[2304,512]{1,0:T(8,128)(2,1)} custom-call(s32[8,128]{1,0:T(8,128)} %copy-done.13, bf16[512,256]{1,0:T(8,128)(2,1)} %bitcast.37, bf16[512,256]{1,0:T(8,128)(2,1)} %bitcast.40, bf16[512,256]{1,0:T(8,128)(2,1)} %copy-done.23, bf16[512,256]{1,0:T(8,128)(2,1)} %copy-done.24, bf16[32,512]{1,0:T(8,128)(2,1)} %copy-done.15, bf16[32,512]{1,0:T(8,128)(2,1)} %copy-done.25), custom_call_target="tpu_custom_call" | custom-call | tf_op jit(solution)/shard_map/reply/pallas_call | solution.py:297
  33.7 3.8 %all-to-all-start.1 = ((bf16[8,288,512]{2,1,0:T(8,128)(2,1)}), bf16[8,288,512]{2,1,0:T(8,128)(2,1)S(1)}, u32[]{:S(2)}, u32[]{:S(2)}) async-start(bf16[8,288,512]{2,1,0:T(8,128)(2,1)} %bitcast.48), calls=%async_computation.1 | async-start | bytes 4718592 | tf_op jit(solution)/shard_map/all_to_all | solution.py:260
  37.5 1.4 convolution_convert_fusion.1.ga_ref
  38.9 27.0 %all-to-all-done.1 = bf16[8,288,512]{2,1,0:T(8,128)(2,1)S(1)} async-done(((bf16[8,288,512]{2,1,0:T(8,128)(2,1)}), bf16[8,288,512]{2,1,0:T(8,128)(2,1)S(1)}, u32[]{:S(2)}, u32[]{:S(2)}) %all-to-all-start.1) | async-done | bytes 2359328 | tf_op jit(solution)/shard_map/all_to_all | solution.py:260
  67.9 9.4 %attend.1 = (bf16[2048,256]{1,0:T(8,128)(2,1)S(1)}, bf16[3072,256]{1,0:T(8,128)(2,1)S(1)}, f32[512,256]{1,0:T(8,128)S(1)}, f32[512,256]{1,0:T(8,128)S(1)}, bf16[...) custom-call(s32[72]{0:T(128)S(1)} %copy-done.17, ...), custom_call_target="tpu_custom_call" | custom-call | tf_op jit(solution)/shard_map/attend/pallas_call | solution.py:309
  77.3 22.9 %all_to_all.53 = bf16[8,384,256]{2,1,0:T(8,128)(2,1)S(1)} all-to-all(bf16[8,384,256]{2,1,0:T(8,128)(2,1)S(1)} %bitcast.44), channel_id=1, replica_groups={{0,2,4,6,8,10,12,14},{16,18,20,22,24,26,28,30},{1,3,5,7,9,11,13,15},{17..., dimensions={0} | all-to-all | bytes 3145728 | tf_op jit(solution)/shard_map/all_to_all | solution.py:260
  100.3 3.7 %all-to-all-start.3 = ((bf16[8,256,256]{2,1,0:T(8,128)(2,1)}), bf16[8,256,256]{2,1,0:T(8,128)(2,1)S(1)}, u32[]{:S(2)}, u32[]{:S(2)}) async-start(bf16[8,256,256]{2,1,0:T(8,128)(2,1)} %bitcast.46), calls=%async_computation.3 | async-start | bytes 2097152 | tf_op jit(solution)/shard_map/all_to_all | solution.py:260
  107.0 2.2 %collective-permute-start.5 = (bf16[640,256]{1,0:T(8,128)(2,1)S(1)}, bf16[640,256]{1,0:T(8,128)(2,1)S(1)}, u32[]{:S(2)}, u32[]{:S(2)}) collective-permute-start(bf16[640,256]{1,0:T(8,128)(2,1)S(1)} %get-tuple-element.49), channel_id=1, source_target_pairs={{0,16},{2,18},{4,20},{6,22},{8,24},{10,26},{12,28},{14,30},{16,0},... | collective-permute-start | bytes 983048 | tf_op jit(solution)/shard_map/ppermute | solution.py:352
  109.2 2.4 %collective-permute-start.6 = (bf16[64,512]{1,0:T(8,128)(2,1)S(1)}, bf16[64,512]{1,0:T(8,128)(2,1)S(1)}, u32[]{:S(2)}, u32[]{:S(2)}) collective-permute-start(bf16[64,512]{1,0:T(8,128)(2,1)S(1)} %copy-done.22), channel_id=1, source_target_pairs={{2,0},{4,2},{6,4},{8,6},{10,8},{12,10},{14,12},{16,14},{18,16},{20... | collective-permute-start | bytes 196616 | tf_op jit(solution)/shard_map/ppermute | solution.py:334
  111.6 1.6 %collective-permute-start.8 = (bf16[64,256]{1,0:T(8,128)(2,1)S(1)}, bf16[64,256]{1,0:T(8,128)(2,1)S(1)}, u32[]{:S(2)}, u32[]{:S(2)}) collective-permute-start(bf16[64,256]{1,0:T(8,128)(2,1)S(1)} %slice.46), channel_id=1, source_target_pairs={{0,1},{1,0},{2,3},{3,2},{4,5},{5,4},{6,7},{7,6},{8,9},{9,8},{10,11... | collective-permute-start | bytes 98312 | tf_op jit(solution)/shard_map/ppermute | solution.py:359
  114.5 9.9 %collective-permute-done.6.from_high_ref = bf16[64,512]{1,0:T(8,128)(2,1)S(1)} collective-permute-done((bf16[64,512]{1,0:T(8,128)(2,1)S(1)}, bf16[64,512]{1,0:T(8,128)(2,1)S(1)}, u32[]{:S(2)}, u32[]{:S(2)}) %collective-permute-start.6) | collective-permute-done | bytes 65568 | tf_op jit(solution)/shard_map/ppermute | solution.py:334
  124.4 4.5 %collective-permute-done.7.from_low_ref = bf16[64,512]{1,0:T(8,128)(2,1)S(1)} collective-permute-done((bf16[64,512]{1,0:T(8,128)(2,1)S(1)}, bf16[64,512]{1,0:T(8,128)(2,1)S(1)}, u32[]{:S(2)}, u32[]{:S(2)}) %collective-permute-start.7) | collective-permute-done | bytes 65568 | tf_op jit(solution)/shard_map/ppermute | solution.py:335
  131.5 3.5 %all-to-all-start.4 = ((bf16[8,128,256]{2,1,0:T(8,128)(2,1)}), bf16[8,128,256]{2,1,0:T(8,128)(2,1)S(1)}, u32[]{:S(2)}, u32[]{:S(2)}) async-start(bf16[8,128,256]{2,1,0:T(8,128)(2,1)} %tile.2), calls=%async_computation.4 | async-start | bytes 1048576 | tf_op jit(solution)/shard_map/all_to_all | solution.py:260
  135.0 1.7 %collective-permute-start.10 = (bf16[512,256]{1,0:T(8,128)(2,1)}, bf16[512,256]{1,0:T(8,128)(2,1)S(1)}, u32[]{:S(2)}, u32[]{:S(2)}) collective-permute-start(bf16[512,256]{1,0:T(8,128)(2,1)} %copy-done.18), channel_id=1, source_target_pairs={{0,16},{2,18},{4,20},{6,22},{8,24},{10,26},{12,28},{14,30},{16,0},... | collective-permute-start | bytes 786440 | tf_op jit(solution)/shard_map/ppermute | solution.py:374
  136.7 2.0 %fusion = bf16[1,512,512]{2,1,0:T(8,128)(2,1)} fusion(bf16[512,256]{1,0:T(8,128)(2,1)} %copy-done.12, bf16[256,512]{1,0:T(8,128)(2,1)S(1)} %copy-done), kind=kOutput, calls=%fused_computation.1 | convolution fusion | flops 134479872 | bytes 1048576 | tf_op jit(solution)/shard_map/dot_general | solution.py:28
  138.8 8.7 %collective-permute-done.10.far_k_ref = bf16[512,256]{1,0:T(8,128)(2,1)S(1)} collective-permute-done((bf16[512,256]{1,0:T(8,128)(2,1)}, bf16[512,256]{1,0:T(8,128)(2,1)S(1)}, u32[]{:S(2)}, u32[]{:S(2)}) %collective-permute-start.10) | collective-permute-done | bytes 262176 | tf_op jit(solution)/shard_map/ppermute | solution.py:374
  147.5 1.9 %all-to-all-done.4 = bf16[8,128,256]{2,1,0:T(8,128)(2,1)S(1)} async-done(((bf16[8,128,256]{2,1,0:T(8,128)(2,1)}), bf16[8,128,256]{2,1,0:T(8,128)(2,1)S(1)}, u32[]{:S(2)}, u32[]{:S(2)}) %all-to-all-start.4) | async-done | bytes 524320 | tf_op jit(solution)/shard_map/all_to_all | solution.py:260
  149.4 1.3 finish.1
  (78 shorter events, 15.5 us)
Async XLA Ops:
  0.6 36.8 %copy-start = (bf16[256,512]{1,0:T(8,128)(2,1)S(1)}, bf16[256,512]{1,0:T(8,128)(2,1)}, u32[]{:S(2)}) copy-start(bf16[256,512]{1,0:T(8,128)(2,1)} %param.10) | copy-start | bytes 786436
  0.6 23.3 %collective-permute-start = (bf16[512,256]{1,0:T(8,128)(2,1)}, bf16[512,256]{1,0:T(8,128)(2,1)S(1)}, u32[]{:S(2)}, u32[]{:S(2)}) collective-permute-start(bf16[512,256]{1,0:T(8,128)(2,1)} %bitcast.35), channel_id=1, source_target_pairs={{0,16},{2,18},{4,20},{6,22},{8,24},{10,26},{12,28},{14,30},{16,0},... | collective-permute-start | bytes 786440 | tf_op jit(solution)/shard_map/ppermute | solution.py:264
  8.7 13.9 %all-to-all-start = ((bf16[8,32,640]{2,1,0:T(8,128)(2,1)}), bf16[8,32,640]{2,1,0:T(8,128)(2,1)S(1)}, u32[]{:S(2)}, u32[]{:S(2)}) async-start(bf16[8,32,640]{2,1,0:T(8,128)(2,1)} %bitcast.49), calls=%async_computation | async-start | bytes 655360 | tf_op jit(solution)/shard_map/all_to_all | solution.py:260
  12.5 16.7 %collective-permute-start.1 = (bf16[512,256]{1,0:T(8,128)(2,1)}, bf16[512,256]{1,0:T(8,128)(2,1)S(1)}, u32[]{:S(2)}, u32[]{:S(2)}) collective-permute-start(bf16[512,256]{1,0:T(8,128)(2,1)} %get-tuple-element.38), channel_id=1, source_target_pairs={{0,16},{2,18},{4,20},{6,22},{8,24},{10,26},{12,28},{14,30},{16,0},... | collective-permute-start | bytes 786440 | tf_op jit(solution)/shard_map/ppermute | solution.py:279
  14.4 19.3 %collective-permute-start.3 = (bf16[64,512]{1,0:T(8,128)(2,1)S(1)}, bf16[64,512]{1,0:T(8,128)(2,1)S(1)}, u32[]{:S(2)}, u32[]{:S(2)}) collective-permute-start(bf16[64,512]{1,0:T(8,128)(2,1)S(1)} %pad_maximum_fusion), channel_id=1, source_target_pairs={{0,2},{2,4},{4,6},{6,8},{8,10},{10,12},{12,14},{14,16},{16,18},{18... | collective-permute-start | bytes 196616 | tf_op jit(solution)/shard_map/ppermute | solution.py:284
  14.7 19.0 %collective-permute-start.4 = (bf16[64,512]{1,0:T(8,128)(2,1)S(1)}, bf16[64,512]{1,0:T(8,128)(2,1)S(1)}, u32[]{:S(2)}, u32[]{:S(2)}) collective-permute-start(bf16[64,512]{1,0:T(8,128)(2,1)S(1)} %pad_maximum_fusion.1), channel_id=1, source_target_pairs={{2,0},{4,2},{6,4},{8,6},{10,8},{12,10},{14,12},{16,14},{18,16},{20... | collective-permute-start | bytes 196616 | tf_op jit(solution)/shard_map/ppermute | solution.py:285
  23.4 6.9 %collective-permute-start.2 = (bf16[32,512]{1,0:T(8,128)(2,1)S(1)}, bf16[32,512]{1,0:T(8,128)(2,1)S(1)}, u32[]{:S(2)}, u32[]{:S(2)}) collective-permute-start(bf16[32,512]{1,0:T(8,128)(2,1)S(1)} %get-tuple-element.39.glob_ref), channel_id=1, source_target_pairs={{0,16},{2,18},{4,20},{6,22},{8,24},{10,26},{12,28},{14,30},{16,0},... | collective-permute-start | bytes 98312 | tf_op jit(solution)/shard_map/ppermute | solution.py:296
  33.7 32.2 %copy-start.1 = (bf16[1,512,256]{2,1,0:T(8,128)(2,1)S(1)}, bf16[1,512,256]{2,1,0:T(8,128)(2,1)}, u32[]{:S(2)}) copy-start(bf16[1,512,256]{2,1,0:T(8,128)(2,1)} %param.8) | copy-start | bytes 786436
  33.7 32.2 %copy-start.2 = (bf16[1,512,256]{2,1,0:T(8,128)(2,1)S(1)}, bf16[1,512,256]{2,1,0:T(8,128)(2,1)}, u32[]{:S(2)}) copy-start(bf16[1,512,256]{2,1,0:T(8,128)(2,1)} %param.9) | copy-start | bytes 786436
  33.7 32.2 %copy-start.17 = (s32[72]{0:T(128)S(1)}, s32[72]{0:T(128)}, u32[]{:S(2)}) copy-start(s32[72]{0:T(128)} %get-tuple-element.35.place_ref) | copy-start | bytes 868
  33.7 32.2 %all-to-all-start.1 = ((bf16[8,288,512]{2,1,0:T(8,128)(2,1)}), bf16[8,288,512]{2,1,0:T(8,128)(2,1)S(1)}, u32[]{:S(2)}, u32[]{:S(2)}) async-start(bf16[8,288,512]{2,1,0:T(8,128)(2,1)} %bitcast.48), calls=%async_computation.1 | async-start | bytes 4718592 | tf_op jit(solution)/shard_map/all_to_all | solution.py:260
  77.3 22.9 %copy-start.19 = (bf16[64,512]{1,0:T(8,128)(2,1)}, bf16[64,512]{1,0:T(8,128)(2,1)S(1)}, u32[]{:S(2)}) copy-start(bf16[64,512]{1,0:T(8,128)(2,1)S(1)} %get-tuple-element.51) | copy-start | bytes 196612
  77.3 26.6 %copy-start.14 = (s32[8,128]{1,0:T(8,128)S(1)}, s32[8,128]{1,0:T(8,128)}, u32[]{:S(2)}) copy-start(s32[8,128]{1,0:T(8,128)} %copy-done.13) | copy-start | bytes 12292
  100.2 28.7 %copy-start.6 = (f32[512,256]{1,0:T(8,128)S(1)}, f32[512,256]{1,0:T(8,128)}, u32[]{:S(2)}) copy-start(f32[512,256]{1,0:T(8,128)} %copy-done.5) | copy-start | bytes 1572868
  100.3 28.6 %all-to-all-start.3 = ((bf16[8,256,256]{2,1,0:T(8,128)(2,1)}), bf16[8,256,256]{2,1,0:T(8,128)(2,1)S(1)}, u32[]{:S(2)}, u32[]{:S(2)}) async-start(bf16[8,256,256]{2,1,0:T(8,128)(2,1)} %bitcast.46), calls=%async_computation.3 | async-start | bytes 2097152 | tf_op jit(solution)/shard_map/all_to_all | solution.py:260
  107.0 21.9 %collective-permute-start.5 = (bf16[640,256]{1,0:T(8,128)(2,1)S(1)}, bf16[640,256]{1,0:T(8,128)(2,1)S(1)}, u32[]{:S(2)}, u32[]{:S(2)}) collective-permute-start(bf16[640,256]{1,0:T(8,128)(2,1)S(1)} %get-tuple-element.49), channel_id=1, source_target_pairs={{0,16},{2,18},{4,20},{6,22},{8,24},{10,26},{12,28},{14,30},{16,0},... | collective-permute-start | bytes 983048 | tf_op jit(solution)/shard_map/ppermute | solution.py:352
  109.2 15.2 %collective-permute-start.6 = (bf16[64,512]{1,0:T(8,128)(2,1)S(1)}, bf16[64,512]{1,0:T(8,128)(2,1)S(1)}, u32[]{:S(2)}, u32[]{:S(2)}) collective-permute-start(bf16[64,512]{1,0:T(8,128)(2,1)S(1)} %copy-done.22), channel_id=1, source_target_pairs={{2,0},{4,2},{6,4},{8,6},{10,8},{12,10},{14,12},{16,14},{18,16},{20... | collective-permute-start | bytes 196616 | tf_op jit(solution)/shard_map/ppermute | solution.py:334
  111.6 37.8 %copy-start.8 = (f32[512,256]{1,0:T(8,128)S(1)}, f32[512,256]{1,0:T(8,128)}, u32[]{:S(2)}) copy-start(f32[512,256]{1,0:T(8,128)} %copy-done.7) | copy-start | bytes 1572868
  111.6 37.8 %copy-start.16 = (s32[1,256]{1,0:T(1,128)S(1)}, s32[1,256]{1,0:T(1,128)}, u32[]{:S(2)}) copy-start(s32[1,256]{1,0:T(1,128)} %pos_ref.3) | copy-start | bytes 3076
  111.6 17.2 %collective-permute-start.7 = (bf16[64,512]{1,0:T(8,128)(2,1)S(1)}, bf16[64,512]{1,0:T(8,128)(2,1)S(1)}, u32[]{:S(2)}, u32[]{:S(2)}) collective-permute-start(bf16[64,512]{1,0:T(8,128)(2,1)S(1)} %copy-done.20), channel_id=1, source_target_pairs={{0,2},{2,4},{4,6},{6,8},{8,10},{10,12},{12,14},{14,16},{16,18},{18... | collective-permute-start | bytes 196616 | tf_op jit(solution)/shard_map/ppermute | solution.py:335
  111.6 17.2 %collective-permute-start.8 = (bf16[64,256]{1,0:T(8,128)(2,1)S(1)}, bf16[64,256]{1,0:T(8,128)(2,1)S(1)}, u32[]{:S(2)}, u32[]{:S(2)}) collective-permute-start(bf16[64,256]{1,0:T(8,128)(2,1)S(1)} %slice.46), channel_id=1, source_target_pairs={{0,1},{1,0},{2,3},{3,2},{4,5},{5,4},{6,7},{7,6},{8,9},{9,8},{10,11... | collective-permute-start | bytes 98312 | tf_op jit(solution)/shard_map/ppermute | solution.py:359
  113.3 15.6 %collective-permute-start.9 = (bf16[64,256]{1,0:T(8,128)(2,1)S(1)}, bf16[64,256]{1,0:T(8,128)(2,1)S(1)}, u32[]{:S(2)}, u32[]{:S(2)}) collective-permute-start(bf16[64,256]{1,0:T(8,128)(2,1)S(1)} %slice.46), channel_id=1, source_target_pairs={{0,17},{1,16},{2,19},{3,18},{4,21},{5,20},{6,23},{7,22},{8,25},{9,... | collective-permute-start | bytes 98312 | tf_op jit(solution)/shard_map/ppermute | solution.py:359
  131.5 17.9 %all-to-all-start.4 = ((bf16[8,128,256]{2,1,0:T(8,128)(2,1)}), bf16[8,128,256]{2,1,0:T(8,128)(2,1)S(1)}, u32[]{:S(2)}, u32[]{:S(2)}) async-start(bf16[8,128,256]{2,1,0:T(8,128)(2,1)} %tile.2), calls=%async_computation.4 | async-start | bytes 1048576 | tf_op jit(solution)/shard_map/all_to_all | solution.py:260
  135.0 12.4 %collective-permute-start.10 = (bf16[512,256]{1,0:T(8,128)(2,1)}, bf16[512,256]{1,0:T(8,128)(2,1)S(1)}, u32[]{:S(2)}, u32[]{:S(2)}) collective-permute-start(bf16[512,256]{1,0:T(8,128)(2,1)} %copy-done.18), channel_id=1, source_target_pairs={{0,16},{2,18},{4,20},{6,22},{8,24},{10,26},{12,28},{14,30},{16,0},... | collective-permute-start | bytes 786440 | tf_op jit(solution)/shard_map/ppermute | solution.py:374
  (17 other events, 155.0 us)

commit v4 on v3

--- a/solution.py
+++ b/solution.py
@@ -166,7 +166,7 @@
                 ].astype(BF16)
         return carry
 
-    lax.fori_loop(0, query_blocks, one_block, 0, unroll=4)
+    lax.fori_loop(0, query_blocks, one_block, 0, unroll=8)
     inner_k_ref[...] = acc_ref[BLK : BLK + tokens, :width]
     inner_v_ref[...] = acc_ref[BLK : BLK + tokens, width:]
     elow_ref[...] = acc_ref[:BLK].astype(BF16)
@@ -373,7 +373,7 @@
     own_k, give_k = fold("fold_keys", dk_back, inner_k, 0)
     far_k = lax.ppermute(give_k, "ctx", mirror)
     share, own_k = lax.optimization_barrier((share, own_k))
-    totals = swap(jnp.tile(share, (half, 1)))
+    totals = lax.all_gather(share, "ctx", axis=0, axis_index_groups=halves, tiled=True)
     attended = dot(attention_rows, output_weight, 1, 0).astype(BF16)
 
     grad_keys, grad_values, grad_weight = pl.pallas_call(

time: 152 us -> 148 us (0.974)
  blocking collectives: 22.9 us -> 39 us
  waiting for transfers between devices: 62 us -> 50.1 us
  starting transfers between devices: 33.5 us -> 28.7 us
  local copies, waits for them, and re-layouts: 9.55 us -> 7.22 us
    all_gather x0 -> x1, blocking collectives: none -> 16.1 us  [shards(): lax.all_gather(share, 'ctx', axis=0, axis_index_groups=halves, tiled=True)]
    ppermute x1, waiting for transfers between devices: 8.69 us -> 0.01 us  [shards(): far_k = lax.ppermute(give_k, 'ctx', mirror)]
    all_to_all x4 -> x3, starting transfers between devices: 14.7 us -> 11.3 us  [swap(): lax.all_to_all(x, 'ctx', split_axis=0, concat_axis=0, axis_index_groups=h...]
    all_to_all x4 -> x3, waiting for transfers between devices: 32.6 us -> 30.7 us  [swap(): lax.all_to_all(x, 'ctx', split_axis=0, concat_axis=0, axis_index_groups=h...]
    unnamed x53 -> x51, local copies, waits for them, and re-layouts: 6.57 us -> 5.07 us
  transfers between devices with their start and end apart: 15 -> 14, of which waited for: 8 -> 6; matrix products, arithmetic and copies ran while one was open for 4% -> 4% of each run, Pallas kernels for 4% -> 5%
where the time goes in v4:
time: 148 us; the launch traced here: 147 us
  waiting for transfers between devices  50.1 us (34%)
  blocking collectives  39 us (26%)
  starting transfers between devices  28.7 us (19%)
  Pallas kernels  17.4 us (12%)
  local copies, waits for them, and re-layouts  7.22 us (5%)
  matrix products  3.4 us (2%)
    all_to_all x3, waiting for transfers between devices, swap(): lax.all_to_all(x, 'ctx', split_axis=0, concat_axis=0, axis_index_groups=h...  30.7 us
    all_to_all x1, blocking collectives, swap(): lax.all_to_all(x, 'ctx', split_axis=0, concat_axis=0, axis_index_groups=h...  22.9 us
    all_gather x1, blocking collectives, shards(): lax.all_gather(share, 'ctx', axis=0, axis_index_groups=halves, tiled=True)  16.1 us
    all_to_all x3, starting transfers between devices, swap(): lax.all_to_all(x, 'ctx', split_axis=0, concat_axis=0, axis_index_groups=h...  11.3 us
    ppermute x1, waiting for transfers between devices, shards(): from_high = lax.ppermute(edge_low, 'ctx', backward)  8.61 us
    pallas_call x1, Pallas kernels, shards(): pl.pallas_call(functools.partial(attend_kernel, half, capacity), name='at...  8.47 us
    ppermute x1, waiting for transfers between devices, shards(): mirror_v = lax.ppermute(v_after, 'ctx', mirror)  5.18 us
    unnamed x51, local copies, waits for them, and re-layouts  5.07 us
  transfers between devices with their start and end apart: 14, of which 6 were waited for; matrix products, arithmetic and copies ran while one was open for 4% of the time, Pallas kernels for 5%

profile of v4, /device:TPU:0, one launch (start us, length us, event | category | flops | bytes accessed | tf_op | source)
XLA Modules:
  0.0 146.8 jit_solution(15470600954274175628)
XLA Ops:
  0.6 4.1 %collective-permute-start = (bf16[512,256]{1,0:T(8,128)(2,1)}, bf16[512,256]{1,0:T(8,128)(2,1)S(1)}, u32[]{:S(2)}, u32[]{:S(2)}) collective-permute-start(bf16[512,256]{1,0:T(8,128)(2,1)} %bitcast.34), channel_id=1, source_target_pairs={{0,16},{2,18},{4,20},{6,22},{8,24},{10,26},{12,28},{14,30},{16,0},... | collective-permute-start | bytes 786440 | tf_op jit(solution)/shard_map/ppermute | solution.py:264
  6.1 2.6 %ask.1 = (bf16[256,640]{1,0:T(8,128)(2,1)}, s32[72]{0:T(128)}, bf16[512,256]{1,0:T(8,128)(2,1)}) custom-call(s32[1]{0:T(128)} %bitcast.here_ref, s32[24]{0:T(128)} %reshape.29.want_ref, s32[1,256]{1,0:T(1,128)} %pos_ref.3, bf16[512,256]{1,0:T(8,128)(2,1)} %bitcast.35, bf16[512,256]{1,0:T(8,128)(2,1)} %bitcast.38), custom_call_target="tpu_custom_call" | custom-call | tf_op jit(solution)/shard_map/ask/pallas_call | solution.py:265
  8.7 3.8 %all-to-all-start = ((bf16[8,32,640]{2,1,0:T(8,128)(2,1)}), bf16[8,32,640]{2,1,0:T(8,128)(2,1)S(1)}, u32[]{:S(2)}, u32[]{:S(2)}) async-start(bf16[8,32,640]{2,1,0:T(8,128)(2,1)} %bitcast.47), calls=%async_computation | async-start | bytes 655360 | tf_op jit(solution)/shard_map/all_to_all | solution.py:260
  14.7 4.3 %collective-permute-start.4 = (bf16[64,512]{1,0:T(8,128)(2,1)S(1)}, bf16[64,512]{1,0:T(8,128)(2,1)S(1)}, u32[]{:S(2)}, u32[]{:S(2)}) collective-permute-start(bf16[64,512]{1,0:T(8,128)(2,1)S(1)} %pad_maximum_fusion.1), channel_id=1, source_target_pairs={{2,0},{4,2},{6,4},{8,6},{10,8},{12,10},{14,12},{16,14},{18,16},{20... | collective-permute-start | bytes 196616 | tf_op jit(solution)/shard_map/ppermute | solution.py:285
  18.9 3.7 %all-to-all-done = bf16[8,32,640]{2,1,0:T(8,128)(2,1)S(1)} async-done(((bf16[8,32,640]{2,1,0:T(8,128)(2,1)}), bf16[8,32,640]{2,1,0:T(8,128)(2,1)S(1)}, u32[]{:S(2)}, u32[]{:S(2)}) %all-to-all-start) | async-done | bytes 327712 | tf_op jit(solution)/shard_map/all_to_all | solution.py:260
  23.9 5.2 %collective-permute-done.1.mv_ref = bf16[512,256]{1,0:T(8,128)(2,1)S(1)} collective-permute-done((bf16[512,256]{1,0:T(8,128)(2,1)}, bf16[512,256]{1,0:T(8,128)(2,1)S(1)}, u32[]{:S(2)}, u32[]{:S(2)}) %collective-permute-start.1) | collective-permute-done | bytes 262176 | tf_op jit(solution)/shard_map/ppermute | solution.py:279
  29.1 1.1 collective-permute-done.2.mglob_ref
  30.9 2.8 %reply.1 = bf16[2304,512]{1,0:T(8,128)(2,1)} custom-call(s32[8,128]{1,0:T(8,128)} %copy-done.13, bf16[512,256]{1,0:T(8,128)(2,1)} %bitcast.36, bf16[512,256]{1,0:T(8,128)(2,1)} %bitcast.39, bf16[512,256]{1,0:T(8,128)(2,1)} %copy-done.22, bf16[512,256]{1,0:T(8,128)(2,1)} %copy-done.23, bf16[32,512]{1,0:T(8,128)(2,1)} %copy-done.15, bf16[32,512]{1,0:T(8,128)(2,1)} %copy-done.24), custom_call_target="tpu_custom_call" | custom-call | tf_op jit(solution)/shard_map/reply/pallas_call | solution.py:297
  33.7 3.8 %all-to-all-start.1 = ((bf16[8,288,512]{2,1,0:T(8,128)(2,1)}), bf16[8,288,512]{2,1,0:T(8,128)(2,1)S(1)}, u32[]{:S(2)}, u32[]{:S(2)}) async-start(bf16[8,288,512]{2,1,0:T(8,128)(2,1)} %bitcast.46), calls=%async_computation.1 | async-start | bytes 4718592 | tf_op jit(solution)/shard_map/all_to_all | solution.py:260
  37.5 1.4 convolution_convert_fusion.1.ga_ref
  38.9 27.0 %all-to-all-done.1 = bf16[8,288,512]{2,1,0:T(8,128)(2,1)S(1)} async-done(((bf16[8,288,512]{2,1,0:T(8,128)(2,1)}), bf16[8,288,512]{2,1,0:T(8,128)(2,1)S(1)}, u32[]{:S(2)}, u32[]{:S(2)}) %all-to-all-start.1) | async-done | bytes 2359328 | tf_op jit(solution)/shard_map/all_to_all | solution.py:260
  67.9 8.5 %attend.1 = (bf16[2048,256]{1,0:T(8,128)(2,1)S(1)}, bf16[3072,256]{1,0:T(8,128)(2,1)S(1)}, f32[512,256]{1,0:T(8,128)S(1)}, f32[512,256]{1,0:T(8,128)S(1)}, bf16[...) custom-call(s32[72]{0:T(128)S(1)} %copy-done.17, ...), custom_call_target="tpu_custom_call" | custom-call | tf_op jit(solution)/shard_map/attend/pallas_call | solution.py:309
  76.4 22.9 %all_to_all.45 = bf16[8,384,256]{2,1,0:T(8,128)(2,1)S(1)} all-to-all(bf16[8,384,256]{2,1,0:T(8,128)(2,1)S(1)} %bitcast.42), channel_id=1, replica_groups={{0,2,4,6,8,10,12,14},{16,18,20,22,24,26,28,30},{1,3,5,7,9,11,13,15},{17..., dimensions={0} | all-to-all | bytes 3145728 | tf_op jit(solution)/shard_map/all_to_all | solution.py:260
  99.3 3.7 %all-to-all-start.3 = ((bf16[8,256,256]{2,1,0:T(8,128)(2,1)}), bf16[8,256,256]{2,1,0:T(8,128)(2,1)S(1)}, u32[]{:S(2)}, u32[]{:S(2)}) async-start(bf16[8,256,256]{2,1,0:T(8,128)(2,1)} %bitcast.44), calls=%async_computation.3 | async-start | bytes 2097152 | tf_op jit(solution)/shard_map/all_to_all | solution.py:260
  104.1 1.1 fold_values.1
  105.2 2.3 %collective-permute-start.5 = (bf16[640,256]{1,0:T(8,128)(2,1)S(1)}, bf16[640,256]{1,0:T(8,128)(2,1)S(1)}, u32[]{:S(2)}, u32[]{:S(2)}) collective-permute-start(bf16[640,256]{1,0:T(8,128)(2,1)S(1)} %get-tuple-element.49), channel_id=1, source_target_pairs={{0,16},{2,18},{4,20},{6,22},{8,24},{10,26},{12,28},{14,30},{16,0},... | collective-permute-start | bytes 983048 | tf_op jit(solution)/shard_map/ppermute | solution.py:352
  107.5 2.5 %collective-permute-start.6 = (bf16[64,512]{1,0:T(8,128)(2,1)S(1)}, bf16[64,512]{1,0:T(8,128)(2,1)S(1)}, u32[]{:S(2)}, u32[]{:S(2)}) collective-permute-start(bf16[64,512]{1,0:T(8,128)(2,1)S(1)} %copy-done.21), channel_id=1, source_target_pairs={{2,0},{4,2},{6,4},{8,6},{10,8},{12,10},{14,12},{16,14},{18,16},{20... | collective-permute-start | bytes 196616 | tf_op jit(solution)/shard_map/ppermute | solution.py:334
  110.0 1.7 %collective-permute-start.8 = (bf16[64,256]{1,0:T(8,128)(2,1)S(1)}, bf16[64,256]{1,0:T(8,128)(2,1)S(1)}, u32[]{:S(2)}, u32[]{:S(2)}) collective-permute-start(bf16[64,256]{1,0:T(8,128)(2,1)S(1)} %slice.46), channel_id=1, source_target_pairs={{0,1},{1,0},{2,3},{3,2},{4,5},{5,4},{6,7},{7,6},{8,9},{9,8},{10,11... | collective-permute-start | bytes 98312 | tf_op jit(solution)/shard_map/ppermute | solution.py:359
  111.7 1.2 collective-permute-start.9
  112.8 2.0 %fusion = bf16[1,512,512]{2,1,0:T(8,128)(2,1)} fusion(bf16[512,256]{1,0:T(8,128)(2,1)} %copy-done.12, bf16[256,512]{1,0:T(8,128)(2,1)S(1)} %copy-done), kind=kOutput, calls=%fused_computation.1 | convolution fusion | flops 134479872 | bytes 1048576 | tf_op jit(solution)/shard_map/dot_general | solution.py:28
  114.9 8.6 %collective-permute-done.6.from_high_ref = bf16[64,512]{1,0:T(8,128)(2,1)S(1)} collective-permute-done((bf16[64,512]{1,0:T(8,128)(2,1)S(1)}, bf16[64,512]{1,0:T(8,128)(2,1)S(1)}, u32[]{:S(2)}, u32[]{:S(2)}) %collective-permute-start.6) | collective-permute-done | bytes 65568 | tf_op jit(solution)/shard_map/ppermute | solution.py:334
  123.5 4.5 %collective-permute-done.7.from_low_ref = bf16[64,512]{1,0:T(8,128)(2,1)S(1)} collective-permute-done((bf16[64,512]{1,0:T(8,128)(2,1)S(1)}, bf16[64,512]{1,0:T(8,128)(2,1)S(1)}, u32[]{:S(2)}, u32[]{:S(2)}) %collective-permute-start.7) | collective-permute-done | bytes 65568 | tf_op jit(solution)/shard_map/ppermute | solution.py:335
  129.4 16.1 %all_gather.3.total_ref = bf16[1024,256]{1,0:T(8,128)(2,1)S(1)} all-gather(bf16[128,256]{1,0:T(8,128)(2,1)S(1)} %pad_maximum_fusion.2), channel_id=1, replica_groups={{0,2,4,6,8,10,12,14},{16,18,20,22,24,26,28,30},{1,3,5,7,9,11,13,15},{17..., dimensions={0}, use_global_device_ids=true | all-gather | bytes 589824 | tf_op jit(solution)/shard_map/all_gather | solution.py:376
  145.6 1.3 finish.1
  (74 shorter events, 10.1 us)
Async XLA Ops:
  0.6 36.8 %copy-start = (bf16[256,512]{1,0:T(8,128)(2,1)S(1)}, bf16[256,512]{1,0:T(8,128)(2,1)}, u32[]{:S(2)}) copy-start(bf16[256,512]{1,0:T(8,128)(2,1)} %param.10) | copy-start | bytes 786436
  0.6 23.3 %collective-permute-start = (bf16[512,256]{1,0:T(8,128)(2,1)}, bf16[512,256]{1,0:T(8,128)(2,1)S(1)}, u32[]{:S(2)}, u32[]{:S(2)}) collective-permute-start(bf16[512,256]{1,0:T(8,128)(2,1)} %bitcast.34), channel_id=1, source_target_pairs={{0,16},{2,18},{4,20},{6,22},{8,24},{10,26},{12,28},{14,30},{16,0},... | collective-permute-start | bytes 786440 | tf_op jit(solution)/shard_map/ppermute | solution.py:264
  8.7 13.9 %all-to-all-start = ((bf16[8,32,640]{2,1,0:T(8,128)(2,1)}), bf16[8,32,640]{2,1,0:T(8,128)(2,1)S(1)}, u32[]{:S(2)}, u32[]{:S(2)}) async-start(bf16[8,32,640]{2,1,0:T(8,128)(2,1)} %bitcast.47), calls=%async_computation | async-start | bytes 655360 | tf_op jit(solution)/shard_map/all_to_all | solution.py:260
  12.5 16.7 %collective-permute-start.1 = (bf16[512,256]{1,0:T(8,128)(2,1)}, bf16[512,256]{1,0:T(8,128)(2,1)S(1)}, u32[]{:S(2)}, u32[]{:S(2)}) collective-permute-start(bf16[512,256]{1,0:T(8,128)(2,1)} %get-tuple-element.38), channel_id=1, source_target_pairs={{0,16},{2,18},{4,20},{6,22},{8,24},{10,26},{12,28},{14,30},{16,0},... | collective-permute-start | bytes 786440 | tf_op jit(solution)/shard_map/ppermute | solution.py:279
  14.4 19.3 %collective-permute-start.3 = (bf16[64,512]{1,0:T(8,128)(2,1)S(1)}, bf16[64,512]{1,0:T(8,128)(2,1)S(1)}, u32[]{:S(2)}, u32[]{:S(2)}) collective-permute-start(bf16[64,512]{1,0:T(8,128)(2,1)S(1)} %pad_maximum_fusion), channel_id=1, source_target_pairs={{0,2},{2,4},{4,6},{6,8},{8,10},{10,12},{12,14},{14,16},{16,18},{18... | collective-permute-start | bytes 196616 | tf_op jit(solution)/shard_map/ppermute | solution.py:284
  14.7 19.0 %collective-permute-start.4 = (bf16[64,512]{1,0:T(8,128)(2,1)S(1)}, bf16[64,512]{1,0:T(8,128)(2,1)S(1)}, u32[]{:S(2)}, u32[]{:S(2)}) collective-permute-start(bf16[64,512]{1,0:T(8,128)(2,1)S(1)} %pad_maximum_fusion.1), channel_id=1, source_target_pairs={{2,0},{4,2},{6,4},{8,6},{10,8},{12,10},{14,12},{16,14},{18,16},{20... | collective-permute-start | bytes 196616 | tf_op jit(solution)/shard_map/ppermute | solution.py:285
  23.4 6.9 %collective-permute-start.2 = (bf16[32,512]{1,0:T(8,128)(2,1)S(1)}, bf16[32,512]{1,0:T(8,128)(2,1)S(1)}, u32[]{:S(2)}, u32[]{:S(2)}) collective-permute-start(bf16[32,512]{1,0:T(8,128)(2,1)S(1)} %get-tuple-element.39.glob_ref), channel_id=1, source_target_pairs={{0,16},{2,18},{4,20},{6,22},{8,24},{10,26},{12,28},{14,30},{16,0},... | collective-permute-start | bytes 98312 | tf_op jit(solution)/shard_map/ppermute | solution.py:296
  33.7 32.2 %copy-start.1 = (bf16[1,512,256]{2,1,0:T(8,128)(2,1)S(1)}, bf16[1,512,256]{2,1,0:T(8,128)(2,1)}, u32[]{:S(2)}) copy-start(bf16[1,512,256]{2,1,0:T(8,128)(2,1)} %param.8) | copy-start | bytes 786436
  33.7 32.2 %copy-start.2 = (bf16[1,512,256]{2,1,0:T(8,128)(2,1)S(1)}, bf16[1,512,256]{2,1,0:T(8,128)(2,1)}, u32[]{:S(2)}) copy-start(bf16[1,512,256]{2,1,0:T(8,128)(2,1)} %param.9) | copy-start | bytes 786436
  33.7 32.2 %copy-start.17 = (s32[72]{0:T(128)S(1)}, s32[72]{0:T(128)}, u32[]{:S(2)}) copy-start(s32[72]{0:T(128)} %get-tuple-element.35.place_ref) | copy-start | bytes 868
  33.7 32.2 %all-to-all-start.1 = ((bf16[8,288,512]{2,1,0:T(8,128)(2,1)}), bf16[8,288,512]{2,1,0:T(8,128)(2,1)S(1)}, u32[]{:S(2)}, u32[]{:S(2)}) async-start(bf16[8,288,512]{2,1,0:T(8,128)(2,1)} %bitcast.46), calls=%async_computation.1 | async-start | bytes 4718592 | tf_op jit(solution)/shard_map/all_to_all | solution.py:260
  76.4 22.9 %copy-start.12 = (bf16[512,256]{1,0:T(8,128)(2,1)}, bf16[512,256]{1,0:T(8,128)(2,1)S(1)}, u32[]{:S(2)}) copy-start(bf16[512,256]{1,0:T(8,128)(2,1)S(1)} %get-tuple-element.43) | copy-start | bytes 786436
  76.4 22.9 %copy-start.18 = (bf16[64,512]{1,0:T(8,128)(2,1)}, bf16[64,512]{1,0:T(8,128)(2,1)S(1)}, u32[]{:S(2)}) copy-start(bf16[64,512]{1,0:T(8,128)(2,1)S(1)} %get-tuple-element.51) | copy-start | bytes 196612
  76.4 22.9 %copy-start.20 = (bf16[64,512]{1,0:T(8,128)(2,1)}, bf16[64,512]{1,0:T(8,128)(2,1)S(1)}, u32[]{:S(2)}) copy-start(bf16[64,512]{1,0:T(8,128)(2,1)S(1)} %get-tuple-element.50) | copy-start | bytes 196612
  76.4 26.6 %copy-start.14 = (s32[8,128]{1,0:T(8,128)S(1)}, s32[8,128]{1,0:T(8,128)}, u32[]{:S(2)}) copy-start(s32[8,128]{1,0:T(8,128)} %copy-done.13) | copy-start | bytes 12292
  99.3 28.7 %copy-start.6 = (f32[512,256]{1,0:T(8,128)S(1)}, f32[512,256]{1,0:T(8,128)}, u32[]{:S(2)}) copy-start(f32[512,256]{1,0:T(8,128)} %copy-done.5) | copy-start | bytes 1572868
  99.3 28.6 %all-to-all-start.3 = ((bf16[8,256,256]{2,1,0:T(8,128)(2,1)}), bf16[8,256,256]{2,1,0:T(8,128)(2,1)S(1)}, u32[]{:S(2)}, u32[]{:S(2)}) async-start(bf16[8,256,256]{2,1,0:T(8,128)(2,1)} %bitcast.44), calls=%async_computation.3 | async-start | bytes 2097152 | tf_op jit(solution)/shard_map/all_to_all | solution.py:260
  105.2 40.3 %copy-start.16 = (s32[1,256]{1,0:T(1,128)S(1)}, s32[1,256]{1,0:T(1,128)}, u32[]{:S(2)}) copy-start(s32[1,256]{1,0:T(1,128)} %pos_ref.3) | copy-start | bytes 3076
  105.2 22.7 %collective-permute-start.5 = (bf16[640,256]{1,0:T(8,128)(2,1)S(1)}, bf16[640,256]{1,0:T(8,128)(2,1)S(1)}, u32[]{:S(2)}, u32[]{:S(2)}) collective-permute-start(bf16[640,256]{1,0:T(8,128)(2,1)S(1)} %get-tuple-element.49), channel_id=1, source_target_pairs={{0,16},{2,18},{4,20},{6,22},{8,24},{10,26},{12,28},{14,30},{16,0},... | collective-permute-start | bytes 983048 | tf_op jit(solution)/shard_map/ppermute | solution.py:352
  107.5 16.0 %collective-permute-start.6 = (bf16[64,512]{1,0:T(8,128)(2,1)S(1)}, bf16[64,512]{1,0:T(8,128)(2,1)S(1)}, u32[]{:S(2)}, u32[]{:S(2)}) collective-permute-start(bf16[64,512]{1,0:T(8,128)(2,1)S(1)} %copy-done.21), channel_id=1, source_target_pairs={{2,0},{4,2},{6,4},{8,6},{10,8},{12,10},{14,12},{16,14},{18,16},{20... | collective-permute-start | bytes 196616 | tf_op jit(solution)/shard_map/ppermute | solution.py:334
  110.0 17.9 %collective-permute-start.7 = (bf16[64,512]{1,0:T(8,128)(2,1)S(1)}, bf16[64,512]{1,0:T(8,128)(2,1)S(1)}, u32[]{:S(2)}, u32[]{:S(2)}) collective-permute-start(bf16[64,512]{1,0:T(8,128)(2,1)S(1)} %copy-done.19), channel_id=1, source_target_pairs={{0,2},{2,4},{4,6},{6,8},{8,10},{10,12},{12,14},{14,16},{16,18},{18... | collective-permute-start | bytes 196616 | tf_op jit(solution)/shard_map/ppermute | solution.py:335
  110.0 17.9 %collective-permute-start.8 = (bf16[64,256]{1,0:T(8,128)(2,1)S(1)}, bf16[64,256]{1,0:T(8,128)(2,1)S(1)}, u32[]{:S(2)}, u32[]{:S(2)}) collective-permute-start(bf16[64,256]{1,0:T(8,128)(2,1)S(1)} %slice.46), channel_id=1, source_target_pairs={{0,1},{1,0},{2,3},{3,2},{4,5},{5,4},{6,7},{7,6},{8,9},{9,8},{10,11... | collective-permute-start | bytes 98312 | tf_op jit(solution)/shard_map/ppermute | solution.py:359
  111.7 16.3 %collective-permute-start.9 = (bf16[64,256]{1,0:T(8,128)(2,1)S(1)}, bf16[64,256]{1,0:T(8,128)(2,1)S(1)}, u32[]{:S(2)}, u32[]{:S(2)}) collective-permute-start(bf16[64,256]{1,0:T(8,128)(2,1)S(1)} %slice.46), channel_id=1, source_target_pairs={{0,17},{1,16},{2,19},{3,18},{4,21},{5,20},{6,23},{7,22},{8,25},{9,... | collective-permute-start | bytes 98312 | tf_op jit(solution)/shard_map/ppermute | solution.py:359
  129.1 16.5 %collective-permute-start.10 = (bf16[512,256]{1,0:T(8,128)(2,1)S(1)}, bf16[512,256]{1,0:T(8,128)(2,1)S(1)}, u32[]{:S(2)}, u32[]{:S(2)}) collective-permute-start(bf16[512,256]{1,0:T(8,128)(2,1)S(1)} %get-tuple-element.58), channel_id=1, source_target_pairs={{0,16},{2,18},{4,20},{6,22},{8,24},{10,26},{12,28},{14,30},{16,0},... | collective-permute-start | bytes 786440 | tf_op jit(solution)/shard_map/ppermute | solution.py:374
  (15 other events, 146.5 us)

commit v5 on v4

--- a/solution.py
+++ b/solution.py
@@ -13,6 +13,7 @@
 LANES = 128
 MIB = 1024 * 1024
 LOG2E = 1.4426950408889634
+MASKS = (0, 6, 2, 4, 7, 3, 5, 1)
 
 F32 = jnp.float32
 BF16 = jnp.bfloat16
@@ -28,6 +29,20 @@
     return lax.dot_general(
         left, right, (((over_left,), (over_right,)), ((), ())), preferred_element_type=F32
     )
+
+
+def masks_of(half):
+    return MASKS if half == len(MASKS) else tuple(range(half))
+
+
+def member_of(here_ref, direct, half, j):
+    return here_ref[1] ^ masks_of(half)[j] if direct else j
+
+
+def rows_of(member, rows):
+    if isinstance(member, int):
+        return slice(member * rows, (member + 1) * rows)
+    return pl.ds(pl.multiple_of(member * rows, rows), rows)
 
 
 def ask_kernel(half, capacity, strides, here_ref, want_ref, pos_ref, k_ref, v_ref,
@@ -39,6 +54,7 @@
     rows = glob // half
     lists = 2 * capacity
     me = here_ref[0]
+    turn = here_ref[1]
     my_half = lax.div(me, half)
     for entry in range(2 * half):
         count_ref[entry] = 0
@@ -54,8 +70,10 @@
         member = owner - owner_half * half
         slot = jnp.where(owner_half == my_half, 0, capacity) + rank
         list_ref[member * lists + slot] = wanted - owner * query_blocks
-        for use in range(3):
-            place_ref[use * requests + at] = member * strides[use] + slot * BLK
+        piece = member ^ turn
+        piece = sum(jnp.where(piece == mask, j, 0) for j, mask in enumerate(masks_of(half)))
+        for use, stride in enumerate(strides):
+            place_ref[use * requests + at] = piece * stride + slot * BLK
         return carry
 
     lax.fori_loop(0, requests, request, 0)
@@ -86,24 +104,29 @@
     glob_ref[...] = dot(total, got_ref[:, :wide], 1, 0).astype(BF16)
 
 
-def reply_kernel(half, capacity, asked_ref, k_ref, v_ref, mk_ref, mv_ref, glob_ref, mglob_ref, out_ref):
+def reply_kernel(half, capacity, direct, here_ref, asked_ref, k_ref, v_ref, mk_ref, mv_ref, glob_ref, mglob_ref,
+                 *out_refs):
     tokens, width = k_ref.shape
-    stride = out_ref.shape[0] // half
+    rows = glob_ref.shape[0]
+    skip = 2 * capacity * BLK
     share = (glob_ref[...].astype(F32) + mglob_ref[...].astype(F32)).astype(BF16)
-    for member in range(half):
+    for j, out_ref in enumerate(out_refs):
+        member = member_of(here_ref, direct, half, j)
         for slot in range(2 * capacity):
             block = jnp.maximum(asked_ref[member, slot], 0)
             source = pl.ds(pl.multiple_of(block * BLK, BLK), BLK)
-            target = pl.ds(member * stride + slot * BLK, BLK)
+            target = slice(slot * BLK, (slot + 1) * BLK)
             own = slot < capacity
             out_ref[target, :width] = (k_ref if own else mk_ref)[source, :]
             out_ref[target, width:] = (v_ref if own else mv_ref)[source, :]
-        out_ref[member * stride + 2 * capacity * BLK : (member + 1) * stride, :] = share
-
-
-def attend_kernel(half, capacity, place_ref, q_ref, ga_ref, og_ref, k_ref, v_ref, low_ref, high_ref, arr_ref,
-                  dk_out_ref, dv_out_ref, inner_k_ref, inner_v_ref, elow_ref, ehigh_ref, att_ref, dq_ref,
-                  pad_ref, kc_ref, vc_ref, acc_ref, gacc_ref):
+        out_ref[skip : skip + rows, :] = share
+
+
+def attend_kernel(half, capacity, direct, place_ref, here_ref, q_ref, ga_ref, og_ref, k_ref, v_ref, low_ref, high_ref,
+                  *refs):
+    pieces, dk_pieces, dv_pieces = (refs[at : at + half] for at in range(0, 3 * half, half))
+    inner_k_ref, inner_v_ref, elow_ref, ehigh_ref, att_ref, dq_ref = refs[3 * half : 3 * half + 6]
+    pad_ref, kc_ref, vc_ref, acc_ref, gacc_ref, arr_ref, dk_out_ref, dv_out_ref = refs[3 * half + 6 :]
     tokens, width = q_ref.shape
     query_blocks = tokens // BLK
     head_size = width // HEADS
@@ -116,10 +139,12 @@
     pad_ref[BLK + tokens :] = high_ref[...]
     skip = 2 * capacity * BLK
     rows = gacc_ref.shape[0] // half
-    for member in range(half):
-        at = member * (arr_ref.shape[0] // half) + skip
-        kc_ref[local + member * rows : local + (member + 1) * rows] = arr_ref[at : at + rows, :width]
-        vc_ref[local + member * rows : local + (member + 1) * rows] = arr_ref[at : at + rows, width:]
+    for j, piece in enumerate(pieces):
+        stride = piece.shape[0]
+        mine = slice(local + j * rows, local + (j + 1) * rows)
+        arr_ref[j * stride : (j + 1) * stride] = piece[...]
+        kc_ref[mine] = piece[skip : skip + rows, :width]
+        vc_ref[mine] = piece[skip : skip + rows, width:]
     acc_ref[...] = jnp.zeros_like(acc_ref)
     gacc_ref[...] = jnp.zeros_like(gacc_ref)
     row_head = lax.broadcasted_iota(jnp.int32, (HEADS * BLK, width), 0) // BLK
@@ -153,14 +178,14 @@
         dscores = (probs * (dprobs - delta) * scale).astype(BF16)
         att_ref[pl.ds(base, BLK), :] = own_head(dot(probs16, vc_ref[...], 0, 0)).astype(BF16)
         dq_ref[pl.ds(base, BLK), :] = own_head(dot(dscores, kc_ref[...], 0, 0)).astype(BF16)
-        for out_ref, at, part, terms in (
-            (dv_out_ref, 1, slice(width, 2 * width), dot(probs16, ga_by_head, 1, 0)),
-            (dk_out_ref, 2, slice(0, width), dot(dscores, q_by_head, 1, 0)),
+        for out_ref, part, terms in (
+            (dv_out_ref, slice(width, 2 * width), dot(probs16, ga_by_head, 1, 0)),
+            (dk_out_ref, slice(0, width), dot(dscores, q_by_head, 1, 0)),
         ):
             acc_ref[pl.ds(base, win), part] += terms[:win]
             gacc_ref[:, part] += terms[local:]
             for j in range(RAND):
-                slot = place_ref[at * requests + i * RAND + j]
+                slot = place_ref[requests + i * RAND + j]
                 out_ref[pl.ds(pl.multiple_of(slot, 16), BLK), :] = terms[
                     win + j * BLK : win + (j + 1) * BLK
                 ].astype(BF16)
@@ -172,41 +197,46 @@
     elow_ref[...] = acc_ref[:BLK].astype(BF16)
     ehigh_ref[...] = acc_ref[BLK + tokens :].astype(BF16)
     gacc_ref[:, 2 * width :] = dot(att_ref[...], og_ref[...], 0, 0)
-    stride = dv_out_ref.shape[0] // half
-    for member in range(half):
+    for j in range(half):
+        dk_pieces[j][...] = dk_out_ref[j * skip : (j + 1) * skip]
+        dv_pieces[j][:skip] = dv_out_ref[j * skip : (j + 1) * skip]
+        member_rows = rows_of(member_of(here_ref, direct, half, j), rows)
         for part in range(gacc_ref.shape[1] // width):
-            at = member * stride + skip + part * rows
-            dv_out_ref[at : at + rows, :] = gacc_ref[
-                member * rows : (member + 1) * rows, part * width : (part + 1) * width
+            at = skip + part * rows
+            mine = slice(j * rows, (j + 1) * rows) if part < 2 else member_rows
+            dv_pieces[j][at : at + rows, :] = gacc_ref[
+                mine, part * width : (part + 1) * width
             ].astype(BF16)
 
 
-def fold_kernel(half, capacity, asked_ref, back_ref, inner_ref, own_ref, give_ref, mirror_acc):
+def fold_kernel(half, capacity, direct, here_ref, asked_ref, inner_ref, *refs):
+    pieces = refs[:half]
+    own_ref, give_ref, mirror_acc = refs[half:]
     tokens = own_ref.shape[0]
-    stride = back_ref.shape[0] // half
     skip = 2 * capacity * BLK
     own_ref[...] = inner_ref[...]
     mirror_acc[...] = jnp.zeros_like(mirror_acc)
-    for member in range(half):
+    for j, piece in enumerate(pieces):
+        member = member_of(here_ref, direct, half, j)
         for slot in range(2 * capacity):
             block = asked_ref[member, slot]
             acc_ref = own_ref if slot < capacity else mirror_acc
-            at = member * stride + slot * BLK
+            at = slot * BLK
 
             @pl.when(block >= 0)
             def _():
                 rows = pl.ds(pl.multiple_of(block * BLK, BLK), BLK)
-                acc_ref[rows, :] += back_ref[at : at + BLK, :].astype(F32)
+                acc_ref[rows, :] += piece[at : at + BLK, :].astype(F32)
 
     give_ref[:tokens] = mirror_acc[...].astype(BF16)
-    if stride > skip:
-        total = back_ref[skip:stride, :].astype(F32)
-        for member in range(1, half):
-            total += back_ref[member * stride + skip : (member + 1) * stride, :].astype(F32)
+    if pieces[0].shape[0] > skip:
+        total = pieces[0][skip:, :].astype(F32)
+        for piece in pieces[1:]:
+            total += piece[skip:, :].astype(F32)
         give_ref[tokens:] = total.astype(BF16)
 
 
-def finish_kernel(half, here_ref, pos_ref, own_k_ref, own_v_ref, far_k_ref, far_v_ref, from_low_ref,
+def finish_kernel(half, direct, here_ref, pos_ref, own_k_ref, own_v_ref, far_k_ref, far_v_ref, from_low_ref,
                   from_high_ref, total_ref, dk_ref, dv_ref, weight_ref, acc_ref, glob_ref):
     tokens, width = dk_ref.shape
     glob = pos_ref.shape[1]
@@ -214,21 +244,20 @@
     stride = total_ref.shape[0] // half
     here = here_ref[0] * tokens + lax.broadcasted_iota(jnp.int32, (tokens, glob), 0)
     owned = jnp.where(here == pos_ref[...], 1.0, 0.0).astype(BF16)
-    for member in range(half):
-        mine = slice(member * rows, (member + 1) * rows)
+    for j in range(half):
+        mine = rows_of(j, rows)
         for part in range(stride // rows):
-            at = member * stride + part * rows
+            at = j * stride + part * rows
+            piece = total_ref[at : at + rows, :].astype(F32)
             if part < 2:
-                glob_ref[mine, part * width : (part + 1) * width] = total_ref[at : at + rows, :]
+                glob_ref[mine, part * width : (part + 1) * width] = piece
             else:
-                weight_ref[mine, (part - 2) * width : (part - 1) * width] = total_ref[
-                    at : at + rows, :
-                ].astype(F32)
+                weight_ref[mine, (part - 2) * width : (part - 1) * width] = piece
     for part, own_ref, far_ref, out_ref in (
         (slice(0, width), own_k_ref, far_k_ref, dk_ref),
         (slice(width, 2 * width), own_v_ref, far_v_ref, dv_ref),
     ):
-        acc_ref[...] = own_ref[...] + far_ref[:tokens].astype(F32) + dot(owned, glob_ref[:, part], 1, 0)
+        acc_ref[...] = own_ref[...] + far_ref[:tokens].astype(F32) + dot(owned, glob_ref[:, part].astype(BF16), 1, 0)
         acc_ref[:BLK] += from_low_ref[:, part].astype(F32)
         acc_ref[tokens - BLK :] += from_high_ref[:, part].astype(F32)
         out_ref[...] = acc_ref[...].astype(BF16)
@@ -248,8 +277,11 @@
     rows = glob // half
     wide = 2 * width + model
     skip = 2 * capacity * BLK
-    strides = (skip + rows, skip + rows * wide // width, skip)
-    here = lax.axis_index("ctx").astype(jnp.int32).reshape(1)
+    strides = (skip + -(-rows // 16) * 16, skip)
+    more = rows * wide // width
+    me = lax.axis_index("ctx").astype(jnp.int32)
+    direct = half <= 8
+    here = jnp.stack([me, me % half if direct else jnp.zeros_like(me)])
     shape = jax.ShapeDtypeStruct
     forward = [(i, (i + 1) % span) for i in range(span)]
     backward = [(target, source) for source, target in forward]
@@ -260,6 +292,16 @@
         return lax.all_to_all(
             x, "ctx", split_axis=0, concat_axis=0, axis_index_groups=halves, tiled=True
         )
+
+    def flip(x, mask):
+        return lax.ppermute(x, "ctx", [(i, i ^ mask) for i in range(span)])
+
+    def trade(pieces):
+        if not direct:
+            return [piece[0] for piece in jnp.split(swap(jnp.stack(pieces)), half)]
+        return [pieces[0]] + [
+            flip(pieces[j], mask) for j, mask in enumerate(masks_of(half)) if mask
+        ]
 
     mirror_k = lax.ppermute(k, "ctx", mirror)
     send, places, v_after = pl.pallas_call(
@@ -267,7 +309,7 @@
         name="ask",
         out_shape=(
             shape((glob, 2 * width + LANES), BF16),
-            shape((3 * requests,), jnp.int32),
+            shape((2 * requests,), jnp.int32),
             shape((tokens, width), BF16),
         ),
         in_specs=[SMEM, SMEM, VMEM, VMEM, VMEM],
@@ -295,60 +337,62 @@
     )(got)
     glob_there = lax.ppermute(glob_here, "ctx", mirror)
     reply = pl.pallas_call(
-        functools.partial(reply_kernel, half, capacity),
+        functools.partial(reply_kernel, half, capacity, direct),
         name="reply",
-        out_shape=shape((half * strides[0], 2 * width), BF16),
-        in_specs=[SMEM] + [VMEM] * 6,
-        out_specs=VMEM,
-        compiler_params=params(60),
-    )(asked, k, v, mirror_k, mirror_v, glob_here, glob_there)
+        out_shape=[shape((strides[0], 2 * width), BF16)] * half,
+        in_specs=[SMEM, SMEM] + [VMEM] * 6,
+        out_specs=[VMEM] * half,
+        compiler_params=params(16),
+    )(here, asked, k, v, mirror_k, mirror_v, glob_here, glob_there)
     reply, low, high = lax.optimization_barrier((reply, low, high))
-    arrived = swap(reply)
+    arrived = trade(reply)
 
     block = (3 + RAND) * BLK + glob
-    dk_out, dv_out, inner_k, inner_v, edge_low, edge_high, attention_rows, grad_queries = pl.pallas_call(
-        functools.partial(attend_kernel, half, capacity),
+    *gives, inner_k, inner_v, edge_low, edge_high, attention_rows, grad_queries = pl.pallas_call(
+        functools.partial(attend_kernel, half, capacity, direct),
         name="attend",
-        out_shape=(
-            shape((half * strides[2], width), BF16),
-            shape((half * strides[1], width), BF16),
+        out_shape=[shape((skip, width), BF16)] * half
+        + [shape((skip + more, width), BF16)] * half
+        + [
             shape((tokens, width), F32),
             shape((tokens, width), F32),
             shape((BLK, 2 * width), BF16),
             shape((BLK, 2 * width), BF16),
             shape((tokens, width), BF16),
             shape((tokens, width), BF16),
-        ),
-        in_specs=[SMEM] + [VMEM] * 8,
-        out_specs=(VMEM,) * 8,
+        ],
+        in_specs=[SMEM, SMEM] + [VMEM] * (7 + half),
+        out_specs=[VMEM] * (2 * half + 6),
         scratch_shapes=[
             pltpu.VMEM((tokens + 2 * BLK, 2 * width), BF16),
             pltpu.VMEM((block, width), BF16),
             pltpu.VMEM((block, width), BF16),
             pltpu.VMEM((tokens + 2 * BLK, 2 * width), F32),
             pltpu.VMEM((glob, wide), F32),
+            pltpu.VMEM((half * strides[0], 2 * width), BF16),
+            pltpu.VMEM((half * skip, width), BF16),
+            pltpu.VMEM((half * skip, width), BF16),
         ],
         compiler_params=params(32),
-    )(places, q, grad_attn, og, k, v, low, high, arrived)
+    )(places, here, q, grad_attn, og, k, v, low, high, *arrived)
 
     from_high = lax.ppermute(edge_low, "ctx", backward)
     from_low = lax.ppermute(edge_high, "ctx", forward)
-    dv_back = swap(dv_out)
-    dk_out, dv_back = lax.optimization_barrier((dk_out, dv_back))
-    dk_back = swap(dk_out)
+    dv_back = trade(gives[half:])
+    dk_back = trade(gives[:half])
 
     def fold(name, back, inner, more):
         return pl.pallas_call(
-            functools.partial(fold_kernel, half, capacity),
+            functools.partial(fold_kernel, half, capacity, direct),
             name=name,
             out_shape=(shape((tokens, width), F32), shape((tokens + more, width), BF16)),
-            in_specs=[SMEM, VMEM, VMEM],
+            in_specs=[SMEM, SMEM, VMEM] + [VMEM] * half,
             out_specs=(VMEM,) * 2,
             scratch_shapes=[pltpu.VMEM((tokens, width), F32)],
             compiler_params=params(16),
-        )(asked, back, inner)
-
-    own_v, give_v = fold("fold_values", dv_back, inner_v, strides[1] - skip)
+        )(here, asked, inner, *back)
+
+    own_v, give_v = fold("fold_values", dv_back, inner_v, more)
     far_v = lax.ppermute(give_v, "ctx", mirror)
     far_v, from_high, from_low = lax.optimization_barrier((far_v, from_high, from_low))
     weight_at = tokens + 2 * rows
@@ -377,7 +421,7 @@
     attended = dot(attention_rows, output_weight, 1, 0).astype(BF16)
 
     grad_keys, grad_values, grad_weight = pl.pallas_call(
-        functools.partial(finish_kernel, half),
+        functools.partial(finish_kernel, half, direct),
         name="finish",
         out_shape=(
             shape((tokens, width), BF16),
@@ -388,7 +432,7 @@
         out_specs=(VMEM,) * 3,
         scratch_shapes=[
             pltpu.VMEM((tokens, width), F32),
-            pltpu.VMEM((glob, 2 * width), BF16),
+            pltpu.VMEM((glob, 2 * width), F32),
         ],
         compiler_params=params(24),
     )(here, glob_pos, own_k, own_v, far_k, far_v, from_low, from_high, totals)

time: 148 us -> 135 us (0.912)
  blocking collectives: 39 us -> 17.7 us
  starting transfers between devices: 28.7 us -> 39.4 us
  waiting for transfers between devices: 50.1 us -> 55.4 us
  local copies, waits for them, and re-layouts: 7.22 us -> 2.73 us
  matrix products: 3.4 us -> 1.41 us
    ppermute x0 -> x21, waiting for transfers between devices: none -> 43.7 us  [flip(): return lax.ppermute(x, 'ctx', [(i, i ^ mask) for i in range(span)])]
    all_to_all x3 -> x1, waiting for transfers between devices: 30.7 us -> 4.4 us  [swap(): lax.all_to_all(x, 'ctx', split_axis=0, concat_axis=0, axis_index_groups=h...]
    all_to_all x1 -> x0, blocking collectives: 22.9 us -> none  [swap(): lax.all_to_all(x, 'ctx', split_axis=0, concat_axis=0, axis_index_groups=h...]
    ppermute x0 -> x21, starting transfers between devices: none -> 17.7 us  [flip(): return lax.ppermute(x, 'ctx', [(i, i ^ mask) for i in range(span)])]
    ppermute x1, waiting for transfers between devices: 8.61 us -> 0.01 us  [shards(): from_high = lax.ppermute(edge_low, 'ctx', backward)]
    all_to_all x3 -> x1, starting transfers between devices: 11.3 us -> 3.92 us  [swap(): lax.all_to_all(x, 'ctx', split_axis=0, concat_axis=0, axis_index_groups=h...]
    ppermute x1, waiting for transfers between devices: 4.46 us -> 0.01 us  [shards(): from_low = lax.ppermute(edge_high, 'ctx', forward)]
    unnamed x51 -> x19, local copies, waits for them, and re-layouts: 5.07 us -> 2.12 us
  transfers between devices with their start and end apart: 14 -> 33, of which waited for: 6 -> 15; matrix products, arithmetic and copies ran while one was open for 4% -> 2% of each run, Pallas kernels for 5% -> 4%
where the time goes in v5:
time: 135 us; the launch traced here: 134 us
  waiting for transfers between devices  55.4 us (41%)
  starting transfers between devices  39.4 us (29%)
  blocking collectives  17.7 us (13%)
  Pallas kernels  16.5 us (12%)
  local copies, waits for them, and re-layouts  2.73 us (2%)
  matrix products  1.41 us (1%)
    ppermute x21, waiting for transfers between devices, flip(): return lax.ppermute(x, 'ctx', [(i, i ^ mask) for i in range(span)])  43.7 us
    ppermute x21, starting transfers between devices, flip(): return lax.ppermute(x, 'ctx', [(i, i ^ mask) for i in range(span)])  17.7 us
    all_gather x1, blocking collectives, shards(): lax.all_gather(share, 'ctx', axis=0, axis_index_groups=halves, tiled=True)  17.7 us
    pallas_call x1, Pallas kernels, shards(): pl.pallas_call(functools.partial(attend_kernel, half, capacity, direct),...  8.65 us
    ppermute x1, waiting for transfers between devices, shards(): mirror_v = lax.ppermute(v_after, 'ctx', mirror)  5.59 us
    all_to_all x1, waiting for transfers between devices, swap(): lax.all_to_all(x, 'ctx', split_axis=0, concat_axis=0, axis_index_groups=h...  4.4 us
    ppermute x1, starting transfers between devices, shards(): high = lax.ppermute(key_value_edges[1], 'ctx', backward)  4.27 us
    ppermute x2, starting transfers between devices, shards(): lax.ppermute(weight_share, ('ctx', 'batch'), [(i * batch + b, (i + shift)...  4.26 us
  transfers between devices with their start and end apart: 33, of which 15 were waited for; matrix products, arithmetic and copies ran while one was open for 2% of the time, Pallas kernels for 4%

profile of v5, /device:TPU:0, one launch (start us, length us, event | category | flops | bytes accessed | tf_op | source)
XLA Modules:
  0.0 134.5 jit_solution(16351684879495832066)
XLA Ops:
  0.6 4.1 %collective-permute-start = (bf16[512,256]{1,0:T(8,128)(2,1)}, bf16[512,256]{1,0:T(8,128)(2,1)S(1)}, u32[]{:S(2)}, u32[]{:S(2)}) collective-permute-start(bf16[512,256]{1,0:T(8,128)(2,1)} %bitcast.26), channel_id=1, source_target_pairs={{0,16},{2,18},{4,20},{6,22},{8,24},{10,26},{12,28},{14,30},{16,0},... | collective-permute-start | bytes 786440 | tf_op jit(solution)/shard_map/ppermute | solution.py:306
  6.7 2.8 %ask.1 = (bf16[256,640]{1,0:T(8,128)(2,1)}, s32[48]{0:T(128)}, bf16[512,256]{1,0:T(8,128)(2,1)}) custom-call(s32[2]{0:T(128)} %pad_add_fusion.here_ref, s32[24]{0:T(128)} %reshape.19.want_ref, s32[1,256]{1,0:T(1,128)} %pos_ref.3, bf16[512,256]{1,0:T(8,128)(2,1)} %bitcast.27, bf16[512,256]{1,0:T(8,128)(2,1)} %bitcast.30), custom_call_target="tpu_custom_call" | custom-call | tf_op jit(solution)/shard_map/ask/pallas_call | solution.py:307
  9.5 3.9 %all-to-all-start = ((bf16[8,32,640]{2,1,0:T(8,128)(2,1)}), bf16[8,32,640]{2,1,0:T(8,128)(2,1)S(1)}, u32[]{:S(2)}, u32[]{:S(2)}) async-start(bf16[8,32,640]{2,1,0:T(8,128)(2,1)} %bitcast.36), calls=%async_computation | async-start | bytes 655360 | tf_op jit(solution)/shard_map/all_to_all | solution.py:292
  14.1 4.3 %collective-permute-start.4 = (bf16[64,512]{1,0:T(8,128)(2,1)S(1)}, bf16[64,512]{1,0:T(8,128)(2,1)S(1)}, u32[]{:S(2)}, u32[]{:S(2)}) collective-permute-start(bf16[64,512]{1,0:T(8,128)(2,1)S(1)} %pad_maximum_fusion.1), channel_id=1, source_target_pairs={{2,0},{4,2},{6,4},{8,6},{10,8},{12,10},{14,12},{16,14},{18,16},{20... | collective-permute-start | bytes 196616 | tf_op jit(solution)/shard_map/ppermute | solution.py:327
  18.4 4.4 %all-to-all-done = bf16[8,32,640]{2,1,0:T(8,128)(2,1)S(1)} async-done(((bf16[8,32,640]{2,1,0:T(8,128)(2,1)}), bf16[8,32,640]{2,1,0:T(8,128)(2,1)S(1)}, u32[]{:S(2)}, u32[]{:S(2)}) %all-to-all-start) | async-done | bytes 327712 | tf_op jit(solution)/shard_map/all_to_all | solution.py:292
  24.4 5.6 %collective-permute-done.1.mv_ref = bf16[512,256]{1,0:T(8,128)(2,1)S(1)} collective-permute-done((bf16[512,256]{1,0:T(8,128)(2,1)}, bf16[512,256]{1,0:T(8,128)(2,1)S(1)}, u32[]{:S(2)}, u32[]{:S(2)}) %collective-permute-start.1) | collective-permute-done | bytes 262176 | tf_op jit(solution)/shard_map/ppermute | solution.py:321
  33.7 1.7 %collective-permute-start.7 = (bf16[288,512]{1,0:T(8,128)(2,1)S(1)}, bf16[288,512]{1,0:T(8,128)(2,1)S(1)}, u32[]{:S(2)}, u32[]{:S(2)}) collective-permute-start(bf16[288,512]{1,0:T(8,128)(2,1)S(1)} %get-tuple-element.80), channel_id=1, source_target_pairs={{0,8},{2,10},{4,12},{6,14},{8,0},{10,2},{12,4},{14,6},{16,24},{18,... | collective-permute-start | bytes 884744 | tf_op jit(solution)/shard_map/ppermute | solution.py:297
  36.9 5.9 %collective-permute-done.5.refs_1_ = bf16[288,512]{1,0:T(8,128)(2,1)S(1)} collective-permute-done((bf16[288,512]{1,0:T(8,128)(2,1)S(1)}, bf16[288,512]{1,0:T(8,128)(2,1)S(1)}, u32[]{:S(2)}, u32[]{:S(2)}) %collective-permute-start.5) | collective-permute-done | bytes 294944 | tf_op jit(solution)/shard_map/ppermute | solution.py:297
  42.8 6.3 %collective-permute-done.6.refs_2_ = bf16[288,512]{1,0:T(8,128)(2,1)S(1)} collective-permute-done((bf16[288,512]{1,0:T(8,128)(2,1)S(1)}, bf16[288,512]{1,0:T(8,128)(2,1)S(1)}, u32[]{:S(2)}, u32[]{:S(2)}) %collective-permute-start.6) | collective-permute-done | bytes 294944 | tf_op jit(solution)/shard_map/ppermute | solution.py:297
  49.5 2.8 %collective-permute-done.8.refs_4_ = bf16[288,512]{1,0:T(8,128)(2,1)S(1)} collective-permute-done((bf16[288,512]{1,0:T(8,128)(2,1)S(1)}, bf16[288,512]{1,0:T(8,128)(2,1)S(1)}, u32[]{:S(2)}, u32[]{:S(2)}) %collective-permute-start.8) | collective-permute-done | bytes 294944 | tf_op jit(solution)/shard_map/ppermute | solution.py:297
  52.3 7.4 %collective-permute-done.9.refs_5_ = bf16[288,512]{1,0:T(8,128)(2,1)S(1)} collective-permute-done((bf16[288,512]{1,0:T(8,128)(2,1)S(1)}, bf16[288,512]{1,0:T(8,128)(2,1)S(1)}, u32[]{:S(2)}, u32[]{:S(2)}) %collective-permute-start.9) | collective-permute-done | bytes 294944 | tf_op jit(solution)/shard_map/ppermute | solution.py:297
  60.3 8.7 %attend.1 = (bf16[256,256]{1,0:T(8,128)(2,1)S(1)}, bf16[256,256]{1,0:T(8,128)(2,1)S(1)}, bf16[256,256]{1,0:T(8,128)(2,1)S(1)}, bf16[256,256]{1,0:T(8,128)(2,1)S(...) custom-call(s32[48]{0:T(128)S(1)} %copy-done.7, ...), custom_call_target="tpu_custom_call" | custom-call | tf_op jit(solution)/shard_map/attend/pallas_call | solution.py:351
  69.0 1.9 %collective-permute-start.12 = (bf16[384,256]{1,0:T(8,128)(2,1)S(1)}, bf16[384,256]{1,0:T(8,128)(2,1)S(1)}, u32[]{:S(2)}, u32[]{:S(2)}) collective-permute-start(bf16[384,256]{1,0:T(8,128)(2,1)S(1)} %get-tuple-element.89), channel_id=1, source_target_pairs={{0,12},{2,14},{4,8},{6,10},{8,4},{10,6},{12,0},{14,2},{16,28},{18,... | collective-permute-start | bytes 589832 | tf_op jit(solution)/shard_map/ppermute | solution.py:297
  74.6 3.0 %collective-permute-done.12.refs_1_ = bf16[384,256]{1,0:T(8,128)(2,1)S(1)} collective-permute-done((bf16[384,256]{1,0:T(8,128)(2,1)S(1)}, bf16[384,256]{1,0:T(8,128)(2,1)S(1)}, u32[]{:S(2)}, u32[]{:S(2)}) %collective-permute-start.12) | collective-permute-done | bytes 196640 | tf_op jit(solution)/shard_map/ppermute | solution.py:297
  77.6 4.3 %collective-permute-done.13.refs_2_ = bf16[384,256]{1,0:T(8,128)(2,1)S(1)} collective-permute-done((bf16[384,256]{1,0:T(8,128)(2,1)S(1)}, bf16[384,256]{1,0:T(8,128)(2,1)S(1)}, u32[]{:S(2)}, u32[]{:S(2)}) %collective-permute-start.13) | collective-permute-done | bytes 196640 | tf_op jit(solution)/shard_map/ppermute | solution.py:297
  81.9 1.9 %collective-permute-start.24 = (bf16[256,256]{1,0:T(8,128)(2,1)S(1)}, bf16[256,256]{1,0:T(8,128)(2,1)S(1)}, u32[]{:S(2)}, u32[]{:S(2)}) collective-permute-start(bf16[256,256]{1,0:T(8,128)(2,1)S(1)} %get-tuple-element.102), channel_id=1, source_target_pairs={{0,12},{2,14},{4,8},{6,10},{8,4},{10,6},{12,0},{14,2},{16,28},{18,... | collective-permute-start | bytes 393224 | tf_op jit(solution)/shard_map/ppermute | solution.py:297
  86.1 3.8 %collective-permute-done.16.refs_5_ = bf16[384,256]{1,0:T(8,128)(2,1)S(1)} collective-permute-done((bf16[384,256]{1,0:T(8,128)(2,1)S(1)}, bf16[384,256]{1,0:T(8,128)(2,1)S(1)}, u32[]{:S(2)}, u32[]{:S(2)}) %collective-permute-start.16) | collective-permute-done | bytes 196640 | tf_op jit(solution)/shard_map/ppermute | solution.py:297
  92.2 1.5 %collective-permute-start.19 = (bf16[640,256]{1,0:T(8,128)(2,1)S(1)}, bf16[640,256]{1,0:T(8,128)(2,1)S(1)}, u32[]{:S(2)}, u32[]{:S(2)}) collective-permute-start(bf16[640,256]{1,0:T(8,128)(2,1)S(1)} %get-tuple-element.96), channel_id=1, source_target_pairs={{0,16},{2,18},{4,20},{6,22},{8,24},{10,26},{12,28},{14,30},{16,0},... | collective-permute-start | bytes 983048 | tf_op jit(solution)/shard_map/ppermute | solution.py:396
  95.0 1.9 %collective-permute-start.28 = (bf16[256,256]{1,0:T(8,128)(2,1)S(1)}, bf16[256,256]{1,0:T(8,128)(2,1)S(1)}, u32[]{:S(2)}, u32[]{:S(2)}) collective-permute-start(bf16[256,256]{1,0:T(8,128)(2,1)S(1)} %get-tuple-element.106), channel_id=1, source_target_pairs={{0,6},{2,4},{4,2},{6,0},{8,14},{10,12},{12,10},{14,8},{16,22},{18,... | collective-permute-start | bytes 393224 | tf_op jit(solution)/shard_map/ppermute | solution.py:297
  97.1 7.5 %collective-permute-done.27.refs_4_ = bf16[256,256]{1,0:T(8,128)(2,1)S(1)} collective-permute-done((bf16[256,256]{1,0:T(8,128)(2,1)S(1)}, bf16[256,256]{1,0:T(8,128)(2,1)S(1)}, u32[]{:S(2)}, u32[]{:S(2)}) %collective-permute-start.27) | collective-permute-done | bytes 131104 | tf_op jit(solution)/shard_map/ppermute | solution.py:297
  107.0 1.5 %collective-permute-start.22 = (bf16[64,256]{1,0:T(8,128)(2,1)S(1)}, bf16[64,256]{1,0:T(8,128)(2,1)S(1)}, u32[]{:S(2)}, u32[]{:S(2)}) collective-permute-start(bf16[64,256]{1,0:T(8,128)(2,1)S(1)} %slice.46), channel_id=1, source_target_pairs={{0,1},{1,0},{2,3},{3,2},{4,5},{5,4},{6,7},{7,6},{8,9},{9,8},{10,11... | collective-permute-start | bytes 98312 | tf_op jit(solution)/shard_map/ppermute | solution.py:403
  108.5 2.8 %collective-permute-start.23 = (bf16[64,256]{1,0:T(8,128)(2,1)S(1)}, bf16[64,256]{1,0:T(8,128)(2,1)S(1)}, u32[]{:S(2)}, u32[]{:S(2)}) collective-permute-start(bf16[64,256]{1,0:T(8,128)(2,1)S(1)} %slice.46), channel_id=1, source_target_pairs={{0,17},{1,16},{2,19},{3,18},{4,21},{5,20},{6,23},{7,22},{8,25},{9,... | collective-permute-start | bytes 98312 | tf_op jit(solution)/shard_map/ppermute | solution.py:403
  114.3 17.7 %all_gather.3.total_ref = bf16[1024,256]{1,0:T(8,128)(2,1)S(1)} all-gather(bf16[128,256]{1,0:T(8,128)(2,1)S(1)} %pad_maximum_fusion.2), channel_id=1, replica_groups={{0,2,4,6,8,10,12,14},{16,18,20,22,24,26,28,30},{1,3,5,7,9,11,13,15},{17..., dimensions={0}, use_global_device_ids=true | all-gather | bytes 589824 | tf_op jit(solution)/shard_map/all_gather | solution.py:420
  132.7 1.8 %finish.1 = (bf16[512,256]{1,0:T(8,128)(2,1)}, bf16[512,256]{1,0:T(8,128)(2,1)}, f32[256,512]{1,0:T(8,128)}) custom-call(s32[2]{0:T(128)S(1)} %copy-done.5, s32[1,256]{1,0:T(1,128)S(1)} %copy-done.6, f32[512,256]{1,0:T(8,128)S(1)} %get-tuple-element.110.own_k_ref, f32[512,256]{1,0:T(8,128)S(1)} %get-tuple-element.111.own_v_ref, ...), custom_call_target="tpu_custom_call" | custom-call | tf_op jit(solution)/shard_map/finish/pallas_call | solution.py:423
  (80 shorter events, 26.0 us)
Async XLA Ops:
  0.6 23.8 %collective-permute-start = (bf16[512,256]{1,0:T(8,128)(2,1)}, bf16[512,256]{1,0:T(8,128)(2,1)S(1)}, u32[]{:S(2)}, u32[]{:S(2)}) collective-permute-start(bf16[512,256]{1,0:T(8,128)(2,1)} %bitcast.26), channel_id=1, source_target_pairs={{0,16},{2,18},{4,20},{6,22},{8,24},{10,26},{12,28},{14,30},{16,0},... | collective-permute-start | bytes 786440 | tf_op jit(solution)/shard_map/ppermute | solution.py:306
  9.5 13.3 %all-to-all-start = ((bf16[8,32,640]{2,1,0:T(8,128)(2,1)}), bf16[8,32,640]{2,1,0:T(8,128)(2,1)S(1)}, u32[]{:S(2)}, u32[]{:S(2)}) async-start(bf16[8,32,640]{2,1,0:T(8,128)(2,1)} %bitcast.36), calls=%async_computation | async-start | bytes 655360 | tf_op jit(solution)/shard_map/all_to_all | solution.py:292
  13.5 16.5 %collective-permute-start.1 = (bf16[512,256]{1,0:T(8,128)(2,1)}, bf16[512,256]{1,0:T(8,128)(2,1)S(1)}, u32[]{:S(2)}, u32[]{:S(2)}) collective-permute-start(bf16[512,256]{1,0:T(8,128)(2,1)} %get-tuple-element.65), channel_id=1, source_target_pairs={{0,16},{2,18},{4,20},{6,22},{8,24},{10,26},{12,28},{14,30},{16,0},... | collective-permute-start | bytes 786440 | tf_op jit(solution)/shard_map/ppermute | solution.py:321
  13.8 18.0 %collective-permute-start.3 = (bf16[64,512]{1,0:T(8,128)(2,1)S(1)}, bf16[64,512]{1,0:T(8,128)(2,1)S(1)}, u32[]{:S(2)}, u32[]{:S(2)}) collective-permute-start(bf16[64,512]{1,0:T(8,128)(2,1)S(1)} %pad_maximum_fusion), channel_id=1, source_target_pairs={{0,2},{2,4},{4,6},{6,8},{8,10},{10,12},{12,14},{14,16},{16,18},{18... | collective-permute-start | bytes 196616 | tf_op jit(solution)/shard_map/ppermute | solution.py:326
  14.1 17.7 %collective-permute-start.4 = (bf16[64,512]{1,0:T(8,128)(2,1)S(1)}, bf16[64,512]{1,0:T(8,128)(2,1)S(1)}, u32[]{:S(2)}, u32[]{:S(2)}) collective-permute-start(bf16[64,512]{1,0:T(8,128)(2,1)S(1)} %pad_maximum_fusion.1), channel_id=1, source_target_pairs={{2,0},{4,2},{6,4},{8,6},{10,8},{12,10},{14,12},{16,14},{18,16},{20... | collective-permute-start | bytes 196616 | tf_op jit(solution)/shard_map/ppermute | solution.py:327
  31.9 11.0 %collective-permute-start.5 = (bf16[288,512]{1,0:T(8,128)(2,1)S(1)}, bf16[288,512]{1,0:T(8,128)(2,1)S(1)}, u32[]{:S(2)}, u32[]{:S(2)}) collective-permute-start(bf16[288,512]{1,0:T(8,128)(2,1)S(1)} %get-tuple-element.78), channel_id=1, source_target_pairs={{0,12},{2,14},{4,8},{6,10},{8,4},{10,6},{12,0},{14,2},{16,28},{18,... | collective-permute-start | bytes 884744 | tf_op jit(solution)/shard_map/ppermute | solution.py:297
  32.2 17.0 %collective-permute-start.6 = (bf16[288,512]{1,0:T(8,128)(2,1)S(1)}, bf16[288,512]{1,0:T(8,128)(2,1)S(1)}, u32[]{:S(2)}, u32[]{:S(2)}) collective-permute-start(bf16[288,512]{1,0:T(8,128)(2,1)S(1)} %get-tuple-element.79), channel_id=1, source_target_pairs={{0,4},{2,6},{4,0},{6,2},{8,12},{10,14},{12,8},{14,10},{16,20},{18,... | collective-permute-start | bytes 884744 | tf_op jit(solution)/shard_map/ppermute | solution.py:297
  33.7 15.8 %collective-permute-start.7 = (bf16[288,512]{1,0:T(8,128)(2,1)S(1)}, bf16[288,512]{1,0:T(8,128)(2,1)S(1)}, u32[]{:S(2)}, u32[]{:S(2)}) collective-permute-start(bf16[288,512]{1,0:T(8,128)(2,1)S(1)} %get-tuple-element.80), channel_id=1, source_target_pairs={{0,8},{2,10},{4,12},{6,14},{8,0},{10,2},{12,4},{14,6},{16,24},{18,... | collective-permute-start | bytes 884744 | tf_op jit(solution)/shard_map/ppermute | solution.py:297
  35.4 16.9 %collective-permute-start.8 = (bf16[288,512]{1,0:T(8,128)(2,1)S(1)}, bf16[288,512]{1,0:T(8,128)(2,1)S(1)}, u32[]{:S(2)}, u32[]{:S(2)}) collective-permute-start(bf16[288,512]{1,0:T(8,128)(2,1)S(1)} %get-tuple-element.81), channel_id=1, source_target_pairs={{0,14},{2,12},{4,10},{6,8},{8,6},{10,4},{12,2},{14,0},{16,30},{18,... | collective-permute-start | bytes 884744 | tf_op jit(solution)/shard_map/ppermute | solution.py:297
  35.4 24.3 %collective-permute-start.9 = (bf16[288,512]{1,0:T(8,128)(2,1)S(1)}, bf16[288,512]{1,0:T(8,128)(2,1)S(1)}, u32[]{:S(2)}, u32[]{:S(2)}) collective-permute-start(bf16[288,512]{1,0:T(8,128)(2,1)S(1)} %get-tuple-element.82), channel_id=1, source_target_pairs={{0,6},{2,4},{4,2},{6,0},{8,14},{10,12},{12,10},{14,8},{16,22},{18,... | collective-permute-start | bytes 884744 | tf_op jit(solution)/shard_map/ppermute | solution.py:297
  42.8 16.9 %collective-permute-start.10 = (bf16[288,512]{1,0:T(8,128)(2,1)S(1)}, bf16[288,512]{1,0:T(8,128)(2,1)S(1)}, u32[]{:S(2)}, u32[]{:S(2)}) collective-permute-start(bf16[288,512]{1,0:T(8,128)(2,1)S(1)} %get-tuple-element.83), channel_id=1, source_target_pairs={{0,10},{2,8},{4,14},{6,12},{8,2},{10,0},{12,6},{14,4},{16,26},{18,... | collective-permute-start | bytes 884744 | tf_op jit(solution)/shard_map/ppermute | solution.py:297
  49.1 10.5 %collective-permute-start.11 = (bf16[288,512]{1,0:T(8,128)(2,1)S(1)}, bf16[288,512]{1,0:T(8,128)(2,1)S(1)}, u32[]{:S(2)}, u32[]{:S(2)}) collective-permute-start(bf16[288,512]{1,0:T(8,128)(2,1)S(1)} %get-tuple-element.84), channel_id=1, source_target_pairs={{0,2},{2,0},{4,6},{6,4},{8,10},{10,8},{12,14},{14,12},{16,18},{18,... | collective-permute-start | bytes 884744 | tf_op jit(solution)/shard_map/ppermute | solution.py:297
  70.9 11.0 %collective-permute-start.13 = (bf16[384,256]{1,0:T(8,128)(2,1)S(1)}, bf16[384,256]{1,0:T(8,128)(2,1)S(1)}, u32[]{:S(2)}, u32[]{:S(2)}) collective-permute-start(bf16[384,256]{1,0:T(8,128)(2,1)S(1)} %get-tuple-element.90), channel_id=1, source_target_pairs={{0,4},{2,6},{4,0},{6,2},{8,12},{10,14},{12,8},{14,10},{16,20},{18,... | collective-permute-start | bytes 589832 | tf_op jit(solution)/shard_map/ppermute | solution.py:297
  71.4 10.5 %collective-permute-start.14 = (bf16[384,256]{1,0:T(8,128)(2,1)S(1)}, bf16[384,256]{1,0:T(8,128)(2,1)S(1)}, u32[]{:S(2)}, u32[]{:S(2)}) collective-permute-start(bf16[384,256]{1,0:T(8,128)(2,1)S(1)} %get-tuple-element.91), channel_id=1, source_target_pairs={{0,8},{2,10},{4,12},{6,14},{8,0},{10,2},{12,4},{14,6},{16,24},{18,... | collective-permute-start | bytes 589832 | tf_op jit(solution)/shard_map/ppermute | solution.py:297
  72.5 12.8 %collective-permute-start.15 = (bf16[384,256]{1,0:T(8,128)(2,1)S(1)}, bf16[384,256]{1,0:T(8,128)(2,1)S(1)}, u32[]{:S(2)}, u32[]{:S(2)}) collective-permute-start(bf16[384,256]{1,0:T(8,128)(2,1)S(1)} %get-tuple-element.92), channel_id=1, source_target_pairs={{0,14},{2,12},{4,10},{6,8},{8,6},{10,4},{12,2},{14,0},{16,30},{18,... | collective-permute-start | bytes 589832 | tf_op jit(solution)/shard_map/ppermute | solution.py:297
  73.3 16.7 %collective-permute-start.16 = (bf16[384,256]{1,0:T(8,128)(2,1)S(1)}, bf16[384,256]{1,0:T(8,128)(2,1)S(1)}, u32[]{:S(2)}, u32[]{:S(2)}) collective-permute-start(bf16[384,256]{1,0:T(8,128)(2,1)S(1)} %get-tuple-element.93), channel_id=1, source_target_pairs={{0,6},{2,4},{4,2},{6,0},{8,14},{10,12},{12,10},{14,8},{16,22},{18,... | collective-permute-start | bytes 589832 | tf_op jit(solution)/shard_map/ppermute | solution.py:297
  77.6 13.4 %collective-permute-start.17 = (bf16[384,256]{1,0:T(8,128)(2,1)S(1)}, bf16[384,256]{1,0:T(8,128)(2,1)S(1)}, u32[]{:S(2)}, u32[]{:S(2)}) collective-permute-start(bf16[384,256]{1,0:T(8,128)(2,1)S(1)} %get-tuple-element.94), channel_id=1, source_target_pairs={{0,10},{2,8},{4,14},{6,12},{8,2},{10,0},{12,6},{14,4},{16,26},{18,... | collective-permute-start | bytes 589832 | tf_op jit(solution)/shard_map/ppermute | solution.py:297
  81.9 13.1 %collective-permute-start.24 = (bf16[256,256]{1,0:T(8,128)(2,1)S(1)}, bf16[256,256]{1,0:T(8,128)(2,1)S(1)}, u32[]{:S(2)}, u32[]{:S(2)}) collective-permute-start(bf16[256,256]{1,0:T(8,128)(2,1)S(1)} %get-tuple-element.102), channel_id=1, source_target_pairs={{0,12},{2,14},{4,8},{6,10},{8,4},{10,6},{12,0},{14,2},{16,28},{18,... | collective-permute-start | bytes 393224 | tf_op jit(solution)/shard_map/ppermute | solution.py:297
  85.3 11.7 %collective-permute-start.25 = (bf16[256,256]{1,0:T(8,128)(2,1)S(1)}, bf16[256,256]{1,0:T(8,128)(2,1)S(1)}, u32[]{:S(2)}, u32[]{:S(2)}) collective-permute-start(bf16[256,256]{1,0:T(8,128)(2,1)S(1)} %get-tuple-element.103), channel_id=1, source_target_pairs={{0,4},{2,6},{4,0},{6,2},{8,12},{10,14},{12,8},{14,10},{16,20},{18,... | collective-permute-start | bytes 393224 | tf_op jit(solution)/shard_map/ppermute | solution.py:297
  92.2 21.5 %collective-permute-start.19 = (bf16[640,256]{1,0:T(8,128)(2,1)S(1)}, bf16[640,256]{1,0:T(8,128)(2,1)S(1)}, u32[]{:S(2)}, u32[]{:S(2)}) collective-permute-start(bf16[640,256]{1,0:T(8,128)(2,1)S(1)} %get-tuple-element.96), channel_id=1, source_target_pairs={{0,16},{2,18},{4,20},{6,22},{8,24},{10,26},{12,28},{14,30},{16,0},... | collective-permute-start | bytes 983048 | tf_op jit(solution)/shard_map/ppermute | solution.py:396
  93.7 10.9 %collective-permute-start.27 = (bf16[256,256]{1,0:T(8,128)(2,1)S(1)}, bf16[256,256]{1,0:T(8,128)(2,1)S(1)}, u32[]{:S(2)}, u32[]{:S(2)}) collective-permute-start(bf16[256,256]{1,0:T(8,128)(2,1)S(1)} %get-tuple-element.105), channel_id=1, source_target_pairs={{0,14},{2,12},{4,10},{6,8},{8,6},{10,4},{12,2},{14,0},{16,30},{18,... | collective-permute-start | bytes 393224 | tf_op jit(solution)/shard_map/ppermute | solution.py:297
  95.0 10.9 %collective-permute-start.28 = (bf16[256,256]{1,0:T(8,128)(2,1)S(1)}, bf16[256,256]{1,0:T(8,128)(2,1)S(1)}, u32[]{:S(2)}, u32[]{:S(2)}) collective-permute-start(bf16[256,256]{1,0:T(8,128)(2,1)S(1)} %get-tuple-element.106), channel_id=1, source_target_pairs={{0,6},{2,4},{4,2},{6,0},{8,14},{10,12},{12,10},{14,8},{16,22},{18,... | collective-permute-start | bytes 393224 | tf_op jit(solution)/shard_map/ppermute | solution.py:297
  97.0 11.5 %collective-permute-start.30 = (bf16[256,256]{1,0:T(8,128)(2,1)S(1)}, bf16[256,256]{1,0:T(8,128)(2,1)S(1)}, u32[]{:S(2)}, u32[]{:S(2)}) collective-permute-start(bf16[256,256]{1,0:T(8,128)(2,1)S(1)} %get-tuple-element.108), channel_id=1, source_target_pairs={{0,2},{2,0},{4,6},{6,4},{8,10},{10,8},{12,14},{14,12},{16,18},{18,... | collective-permute-start | bytes 393224 | tf_op jit(solution)/shard_map/ppermute | solution.py:297
  113.5 18.5 %collective-permute-start.31 = (bf16[512,256]{1,0:T(8,128)(2,1)S(1)}, bf16[512,256]{1,0:T(8,128)(2,1)S(1)}, u32[]{:S(2)}, u32[]{:S(2)}) collective-permute-start(bf16[512,256]{1,0:T(8,128)(2,1)S(1)} %get-tuple-element.112), channel_id=1, source_target_pairs={{0,16},{2,18},{4,20},{6,22},{8,24},{10,26},{12,28},{14,30},{16,0},... | collective-permute-start | bytes 786440 | tf_op jit(solution)/shard_map/ppermute | solution.py:418
  (18 other events, 185.1 us)

commit v6 on v5

--- a/solution.py
+++ b/solution.py
@@ -236,18 +236,21 @@
         give_ref[tokens:] = total.astype(BF16)
 
 
-def finish_kernel(half, direct, here_ref, pos_ref, own_k_ref, own_v_ref, far_k_ref, far_v_ref, from_low_ref,
-                  from_high_ref, total_ref, dk_ref, dv_ref, weight_ref, acc_ref, glob_ref):
+def finish_kernel(masks, here_ref, pos_ref, own_k_ref, own_v_ref, far_k_ref, far_v_ref, from_low_ref,
+                  from_high_ref, *refs):
+    dk_ref, dv_ref, weight_ref, acc_ref, glob_ref = refs[-5:]
+    half = len(masks)
     tokens, width = dk_ref.shape
     glob = pos_ref.shape[1]
     rows = glob // half
-    stride = total_ref.shape[0] // half
+    stride = sum(ref.shape[0] for ref in refs[:-5]) // half
     here = here_ref[0] * tokens + lax.broadcasted_iota(jnp.int32, (tokens, glob), 0)
     owned = jnp.where(here == pos_ref[...], 1.0, 0.0).astype(BF16)
-    for j in range(half):
-        mine = rows_of(j, rows)
+    places = [(ref, at) for ref in refs[:-5] for at in range(0, ref.shape[0], stride)]
+    for mask, (total_ref, first) in zip(masks, places):
+        mine = rows_of(here_ref[1] ^ mask if len(refs) > 6 else mask, rows)
         for part in range(stride // rows):
-            at = j * stride + part * rows
+            at = first + part * rows
             piece = total_ref[at : at + rows, :].astype(F32)
             if part < 2:
                 glob_ref[mine, part * width : (part + 1) * width] = piece
@@ -280,7 +283,7 @@
     strides = (skip + -(-rows // 16) * 16, skip)
     more = rows * wide // width
     me = lax.axis_index("ctx").astype(jnp.int32)
-    direct = half <= 8
+    direct = half == 8
     here = jnp.stack([me, me % half if direct else jnp.zeros_like(me)])
     shape = jax.ShapeDtypeStruct
     forward = [(i, (i + 1) % span) for i in range(span)]
@@ -393,49 +396,46 @@
         )(here, asked, inner, *back)
 
     own_v, give_v = fold("fold_values", dv_back, inner_v, more)
-    far_v = lax.ppermute(give_v, "ctx", mirror)
-    far_v, from_high, from_low = lax.optimization_barrier((far_v, from_high, from_low))
+    far_share = lax.ppermute(give_v[tokens:], "ctx", mirror)
+    far_v = lax.ppermute(give_v[:tokens], "ctx", mirror)
     weight_at = tokens + 2 * rows
-    weight_share = give_v[weight_at:]
-    weight_sum = weight_share.astype(F32) + far_v[weight_at:].astype(F32)
+    weight_pair = (give_v[weight_at:].astype(F32) + far_share[2 * rows :].astype(F32)).astype(BF16)
+    weight_sum = weight_pair.astype(F32)
     for step in range(1, batch):
-        same, crossed = (
-            lax.ppermute(
-                weight_share,
-                ("ctx", "batch"),
-                [
-                    (i * batch + b, (i + shift) % span * batch + (b + step) % batch)
-                    for i in range(span)
-                    for b in range(batch)
-                ],
-            ).astype(F32)
-            for shift in (0, half)
-        )
-        weight_sum += same + crossed
-    glob_sum = give_v[tokens:weight_at].astype(F32) + far_v[tokens:weight_at].astype(F32)
+        weight_sum += lax.ppermute(
+            weight_pair, "batch", [(i, (i + step) % batch) for i in range(batch)]
+        ).astype(F32)
+    weight_sum, far_v = lax.optimization_barrier((weight_sum, far_v))
+    glob_sum = give_v[tokens:weight_at].astype(F32) + far_share[: 2 * rows].astype(F32)
     share = jnp.concatenate([glob_sum, weight_sum], axis=0).astype(BF16)
     own_k, give_k = fold("fold_keys", dk_back, inner_k, 0)
     far_k = lax.ppermute(give_k, "ctx", mirror)
     share, own_k = lax.optimization_barrier((share, own_k))
-    totals = lax.all_gather(share, "ctx", axis=0, axis_index_groups=halves, tiled=True)
+    if direct:
+        pair = jnp.concatenate([share, flip(share, 1)], axis=0)
+        totals = [pair] + [flip(pair, mask) for mask in (6, 2, 4)]
+        masks = (0, 1, 6, 7, 2, 3, 4, 5)
+    else:
+        totals = [lax.all_gather(share, "ctx", axis=0, axis_index_groups=halves, tiled=True)]
+        masks = tuple(range(half))
     attended = dot(attention_rows, output_weight, 1, 0).astype(BF16)
 
     grad_keys, grad_values, grad_weight = pl.pallas_call(
-        functools.partial(finish_kernel, half, direct),
+        functools.partial(finish_kernel, masks),
         name="finish",
         out_shape=(
             shape((tokens, width), BF16),
             shape((tokens, width), BF16),
             shape((width, model), F32),
         ),
-        in_specs=[SMEM] + [VMEM] * 8,
+        in_specs=[SMEM] + [VMEM] * (7 + len(totals)),
         out_specs=(VMEM,) * 3,
         scratch_shapes=[
             pltpu.VMEM((tokens, width), F32),
             pltpu.VMEM((glob, 2 * width), F32),
         ],
         compiler_params=params(24),
-    )(here, glob_pos, own_k, own_v, far_k, far_v, from_low, from_high, totals)
+    )(here, glob_pos, own_k, own_v, far_k, far_v, from_low, from_high, *totals)
     return (
         attended[None],
         grad_queries[None],

time: 135 us -> 133 us (0.985)
  blocking collectives: 17.7 us -> 0 us
  waiting for transfers between devices: 55.4 us -> 68 us
  starting transfers between devices: 39.4 us -> 43.1 us
    all_gather x1 -> x0, blocking collectives: 17.7 us -> none  [shards(): lax.all_gather(share, 'ctx', axis=0, axis_index_groups=halves, tiled=True)]
    ppermute x3, waiting for transfers between devices: 0.55 us -> 9.78 us  [the longest x1 8.88 us: shards(): far_v = lax.ppermute(give_v[:tokens], 'ctx', mirror)]
    ppermute x21 -> x25, starting transfers between devices: 17.7 us -> 21.9 us  [flip(): return lax.ppermute(x, 'ctx', [(i, i ^ mask) for i in range(span)])]
    ppermute x21 -> x25, waiting for transfers between devices: 43.7 us -> 47.2 us  [flip(): return lax.ppermute(x, 'ctx', [(i, i ^ mask) for i in range(span)])]
    ppermute x3, starting transfers between devices: 5.78 us -> 4.21 us  [the longest x1 1.53 us: shards(): far_share = lax.ppermute(give_v[tokens:], 'ctx', mirror)]
  transfers between devices with their start and end apart: 33 -> 37, of which waited for: 15 -> 19; matrix products, arithmetic and copies ran while one was open for 2% -> 2% of each run, Pallas kernels for 4% -> 5%
where the time goes in v6:
time: 133 us
  waiting for transfers between devices  68 us (51%)
  starting transfers between devices  43.1 us (32%)
  Pallas kernels  16.5 us (12%)
  local copies, waits for them, and re-layouts  2.09 us (2%)
  matrix products  1.41 us (1%)
    ppermute x25, waiting for transfers between devices, flip(): return lax.ppermute(x, 'ctx', [(i, i ^ mask) for i in range(span)])  47.2 us
    ppermute x25, starting transfers between devices, flip(): return lax.ppermute(x, 'ctx', [(i, i ^ mask) for i in range(span)])  21.9 us
    ppermute x1, waiting for transfers between devices, shards(): far_v = lax.ppermute(give_v[:tokens], 'ctx', mirror)  8.88 us
    pallas_call x1, Pallas kernels, shards(): pl.pallas_call(functools.partial(attend_kernel, half, capacity, direct),...  8.65 us
    ppermute x1, waiting for transfers between devices, shards(): mirror_v = lax.ppermute(v_after, 'ctx', mirror)  5.59 us
    all_to_all x1, waiting for transfers between devices, swap(): lax.all_to_all(x, 'ctx', split_axis=0, concat_axis=0, axis_index_groups=h...  4.4 us
    ppermute x1, starting transfers between devices, shards(): high = lax.ppermute(key_value_edges[1], 'ctx', backward)  4.27 us
    ppermute x1, starting transfers between devices, shards(): mirror_k = lax.ppermute(k, 'ctx', mirror)  4.1 us
  transfers between devices with their start and end apart: 37, of which 19 were waited for; matrix products, arithmetic and copies ran while one was open for 2% of the time, Pallas kernels for 5%

profile of v6, /device:TPU:0, one launch (start us, length us, event | category | flops | bytes accessed | tf_op | source)
XLA Modules:
  0.0 132.6 jit_solution(9220935496449081788)
XLA Ops:
  0.6 4.1 %collective-permute-start = (bf16[512,256]{1,0:T(8,128)(2,1)}, bf16[512,256]{1,0:T(8,128)(2,1)S(1)}, u32[]{:S(2)}, u32[]{:S(2)}) collective-permute-start(bf16[512,256]{1,0:T(8,128)(2,1)} %bitcast.26), channel_id=1, source_target_pairs={{0,16},{2,18},{4,20},{6,22},{8,24},{10,26},{12,28},{14,30},{16,0},... | collective-permute-start | bytes 786440 | tf_op jit(solution)/shard_map/ppermute | solution.py:309
  6.7 2.8 %ask.1 = (bf16[256,640]{1,0:T(8,128)(2,1)}, s32[48]{0:T(128)}, bf16[512,256]{1,0:T(8,128)(2,1)}) custom-call(s32[2]{0:T(128)} %pad_add_fusion.here_ref, s32[24]{0:T(128)} %reshape.19.want_ref, s32[1,256]{1,0:T(1,128)} %pos_ref.3, bf16[512,256]{1,0:T(8,128)(2,1)} %bitcast.27, bf16[512,256]{1,0:T(8,128)(2,1)} %bitcast.30), custom_call_target="tpu_custom_call" | custom-call | tf_op jit(solution)/shard_map/ask/pallas_call | solution.py:310
  9.5 3.9 %all-to-all-start = ((bf16[8,32,640]{2,1,0:T(8,128)(2,1)}), bf16[8,32,640]{2,1,0:T(8,128)(2,1)S(1)}, u32[]{:S(2)}, u32[]{:S(2)}) async-start(bf16[8,32,640]{2,1,0:T(8,128)(2,1)} %bitcast.36), calls=%async_computation | async-start | bytes 655360 | tf_op jit(solution)/shard_map/all_to_all | solution.py:295
  14.1 4.3 %collective-permute-start.4 = (bf16[64,512]{1,0:T(8,128)(2,1)S(1)}, bf16[64,512]{1,0:T(8,128)(2,1)S(1)}, u32[]{:S(2)}, u32[]{:S(2)}) collective-permute-start(bf16[64,512]{1,0:T(8,128)(2,1)S(1)} %pad_maximum_fusion.1), channel_id=1, source_target_pairs={{2,0},{4,2},{6,4},{8,6},{10,8},{12,10},{14,12},{16,14},{18,16},{20... | collective-permute-start | bytes 196616 | tf_op jit(solution)/shard_map/ppermute | solution.py:330
  18.4 4.4 %all-to-all-done = bf16[8,32,640]{2,1,0:T(8,128)(2,1)S(1)} async-done(((bf16[8,32,640]{2,1,0:T(8,128)(2,1)}), bf16[8,32,640]{2,1,0:T(8,128)(2,1)S(1)}, u32[]{:S(2)}, u32[]{:S(2)}) %all-to-all-start) | async-done | bytes 327712 | tf_op jit(solution)/shard_map/all_to_all | solution.py:295
  24.4 5.6 %collective-permute-done.1.mv_ref = bf16[512,256]{1,0:T(8,128)(2,1)S(1)} collective-permute-done((bf16[512,256]{1,0:T(8,128)(2,1)}, bf16[512,256]{1,0:T(8,128)(2,1)S(1)}, u32[]{:S(2)}, u32[]{:S(2)}) %collective-permute-start.1) | collective-permute-done | bytes 262176 | tf_op jit(solution)/shard_map/ppermute | solution.py:324
  33.7 1.7 %collective-permute-start.7 = (bf16[288,512]{1,0:T(8,128)(2,1)S(1)}, bf16[288,512]{1,0:T(8,128)(2,1)S(1)}, u32[]{:S(2)}, u32[]{:S(2)}) collective-permute-start(bf16[288,512]{1,0:T(8,128)(2,1)S(1)} %get-tuple-element.79), channel_id=1, source_target_pairs={{0,8},{2,10},{4,12},{6,14},{8,0},{10,2},{12,4},{14,6},{16,24},{18,... | collective-permute-start | bytes 884744 | tf_op jit(solution)/shard_map/ppermute | solution.py:300
  36.9 5.9 %collective-permute-done.5.refs_1_ = bf16[288,512]{1,0:T(8,128)(2,1)S(1)} collective-permute-done((bf16[288,512]{1,0:T(8,128)(2,1)S(1)}, bf16[288,512]{1,0:T(8,128)(2,1)S(1)}, u32[]{:S(2)}, u32[]{:S(2)}) %collective-permute-start.5) | collective-permute-done | bytes 294944 | tf_op jit(solution)/shard_map/ppermute | solution.py:300
  42.8 6.3 %collective-permute-done.6.refs_2_ = bf16[288,512]{1,0:T(8,128)(2,1)S(1)} collective-permute-done((bf16[288,512]{1,0:T(8,128)(2,1)S(1)}, bf16[288,512]{1,0:T(8,128)(2,1)S(1)}, u32[]{:S(2)}, u32[]{:S(2)}) %collective-permute-start.6) | collective-permute-done | bytes 294944 | tf_op jit(solution)/shard_map/ppermute | solution.py:300
  49.5 2.8 %collective-permute-done.8.refs_4_ = bf16[288,512]{1,0:T(8,128)(2,1)S(1)} collective-permute-done((bf16[288,512]{1,0:T(8,128)(2,1)S(1)}, bf16[288,512]{1,0:T(8,128)(2,1)S(1)}, u32[]{:S(2)}, u32[]{:S(2)}) %collective-permute-start.8) | collective-permute-done | bytes 294944 | tf_op jit(solution)/shard_map/ppermute | solution.py:300
  52.3 7.4 %collective-permute-done.9.refs_5_ = bf16[288,512]{1,0:T(8,128)(2,1)S(1)} collective-permute-done((bf16[288,512]{1,0:T(8,128)(2,1)S(1)}, bf16[288,512]{1,0:T(8,128)(2,1)S(1)}, u32[]{:S(2)}, u32[]{:S(2)}) %collective-permute-start.9) | collective-permute-done | bytes 294944 | tf_op jit(solution)/shard_map/ppermute | solution.py:300
  60.3 8.7 %attend.1 = (bf16[256,256]{1,0:T(8,128)(2,1)S(1)}, bf16[256,256]{1,0:T(8,128)(2,1)S(1)}, bf16[256,256]{1,0:T(8,128)(2,1)S(1)}, bf16[256,256]{1,0:T(8,128)(2,1)S(...) custom-call(s32[48]{0:T(128)S(1)} %copy-done.7, ...), custom_call_target="tpu_custom_call" | custom-call | tf_op jit(solution)/shard_map/attend/pallas_call | solution.py:354
  69.0 1.9 %collective-permute-start.12 = (bf16[384,256]{1,0:T(8,128)(2,1)S(1)}, bf16[384,256]{1,0:T(8,128)(2,1)S(1)}, u32[]{:S(2)}, u32[]{:S(2)}) collective-permute-start(bf16[384,256]{1,0:T(8,128)(2,1)S(1)} %get-tuple-element.88), channel_id=1, source_target_pairs={{0,12},{2,14},{4,8},{6,10},{8,4},{10,6},{12,0},{14,2},{16,28},{18,... | collective-permute-start | bytes 589832 | tf_op jit(solution)/shard_map/ppermute | solution.py:300
  74.6 3.0 %collective-permute-done.12.refs_1_ = bf16[384,256]{1,0:T(8,128)(2,1)S(1)} collective-permute-done((bf16[384,256]{1,0:T(8,128)(2,1)S(1)}, bf16[384,256]{1,0:T(8,128)(2,1)S(1)}, u32[]{:S(2)}, u32[]{:S(2)}) %collective-permute-start.12) | collective-permute-done | bytes 196640 | tf_op jit(solution)/shard_map/ppermute | solution.py:300
  77.6 4.3 %collective-permute-done.13.refs_2_ = bf16[384,256]{1,0:T(8,128)(2,1)S(1)} collective-permute-done((bf16[384,256]{1,0:T(8,128)(2,1)S(1)}, bf16[384,256]{1,0:T(8,128)(2,1)S(1)}, u32[]{:S(2)}, u32[]{:S(2)}) %collective-permute-start.13) | collective-permute-done | bytes 196640 | tf_op jit(solution)/shard_map/ppermute | solution.py:300
  81.9 1.9 %collective-permute-start.22 = (bf16[256,256]{1,0:T(8,128)(2,1)S(1)}, bf16[256,256]{1,0:T(8,128)(2,1)S(1)}, u32[]{:S(2)}, u32[]{:S(2)}) collective-permute-start(bf16[256,256]{1,0:T(8,128)(2,1)S(1)} %get-tuple-element.99), channel_id=1, source_target_pairs={{0,12},{2,14},{4,8},{6,10},{8,4},{10,6},{12,0},{14,2},{16,28},{18,... | collective-permute-start | bytes 393224 | tf_op jit(solution)/shard_map/ppermute | solution.py:300
  86.1 3.8 %collective-permute-done.16.refs_5_ = bf16[384,256]{1,0:T(8,128)(2,1)S(1)} collective-permute-done((bf16[384,256]{1,0:T(8,128)(2,1)S(1)}, bf16[384,256]{1,0:T(8,128)(2,1)S(1)}, u32[]{:S(2)}, u32[]{:S(2)}) %collective-permute-start.16) | collective-permute-done | bytes 196640 | tf_op jit(solution)/shard_map/ppermute | solution.py:300
  95.0 2.0 %collective-permute-start.26 = (bf16[256,256]{1,0:T(8,128)(2,1)S(1)}, bf16[256,256]{1,0:T(8,128)(2,1)S(1)}, u32[]{:S(2)}, u32[]{:S(2)}) collective-permute-start(bf16[256,256]{1,0:T(8,128)(2,1)S(1)} %get-tuple-element.103), channel_id=1, source_target_pairs={{0,6},{2,4},{4,2},{6,0},{8,14},{10,12},{12,10},{14,8},{16,22},{18,... | collective-permute-start | bytes 393224 | tf_op jit(solution)/shard_map/ppermute | solution.py:300
  99.3 1.8 %collective-permute-done.25.refs_4_ = bf16[256,256]{1,0:T(8,128)(2,1)S(1)} collective-permute-done((bf16[256,256]{1,0:T(8,128)(2,1)S(1)}, bf16[256,256]{1,0:T(8,128)(2,1)S(1)}, u32[]{:S(2)}, u32[]{:S(2)}) %collective-permute-start.25) | collective-permute-done | bytes 131104 | tf_op jit(solution)/shard_map/ppermute | solution.py:300
  103.7 3.3 %collective-permute-done.27.refs_6_ = bf16[256,256]{1,0:T(8,128)(2,1)S(1)} collective-permute-done((bf16[256,256]{1,0:T(8,128)(2,1)S(1)}, bf16[256,256]{1,0:T(8,128)(2,1)S(1)}, u32[]{:S(2)}, u32[]{:S(2)}) %collective-permute-start.27) | collective-permute-done | bytes 131104 | tf_op jit(solution)/shard_map/ppermute | solution.py:300
  106.9 2.1 %collective-permute-start.31 = (bf16[64,512]{1,0:T(8,128)(2,1)S(1)}, bf16[64,512]{1,0:T(8,128)(2,1)S(1)}, u32[]{:S(2)}, u32[]{:S(2)}) collective-permute-start(bf16[64,512]{1,0:T(8,128)(2,1)S(1)} %get-tuple-element.112), channel_id=1, source_target_pairs={{2,0},{4,2},{6,4},{8,6},{10,8},{12,10},{14,12},{16,14},{18,16},{20... | collective-permute-start | bytes 196616 | tf_op jit(solution)/shard_map/ppermute | solution.py:382
  110.2 8.9 %collective-permute-done.21.far_v_ref = bf16[512,256]{1,0:T(8,128)(2,1)S(1)} collective-permute-done((bf16[512,256]{1,0:T(8,128)(2,1)S(1)}, bf16[512,256]{1,0:T(8,128)(2,1)S(1)}, u32[]{:S(2)}, u32[]{:S(2)}) %collective-permute-start.21) | collective-permute-done | bytes 262176 | tf_op jit(solution)/shard_map/ppermute | solution.py:400
  127.2 3.5 %collective-permute-done.33.refs_1_ = bf16[256,256]{1,0:T(8,128)(2,1)S(1)} collective-permute-done((bf16[256,256]{1,0:T(8,128)(2,1)S(1)}, bf16[256,256]{1,0:T(8,128)(2,1)S(1)}, u32[]{:S(2)}, u32[]{:S(2)}) %collective-permute-start.33) | collective-permute-done | bytes 131104 | tf_op jit(solution)/shard_map/ppermute | solution.py:300
  130.7 1.9 %finish.1 = (bf16[512,256]{1,0:T(8,128)(2,1)}, bf16[512,256]{1,0:T(8,128)(2,1)}, f32[256,512]{1,0:T(8,128)}) custom-call(s32[2]{0:T(128)S(1)} %copy-done.5, s32[1,256]{1,0:T(1,128)S(1)} %copy-done.6, f32[512,256]{1,0:T(8,128)S(1)} %get-tuple-element.107.own_k_ref, f32[512,256]{1,0:T(8,128)S(1)} %get-tuple-element.108.own_v_ref, ...), custom_call_target="tpu_custom_call" | custom-call | tf_op jit(solution)/shard_map/finish/pallas_call | solution.py:423
  (91 shorter events, 35.5 us)
Async XLA Ops:
  0.6 23.8 %collective-permute-start = (bf16[512,256]{1,0:T(8,128)(2,1)}, bf16[512,256]{1,0:T(8,128)(2,1)S(1)}, u32[]{:S(2)}, u32[]{:S(2)}) collective-permute-start(bf16[512,256]{1,0:T(8,128)(2,1)} %bitcast.26), channel_id=1, source_target_pairs={{0,16},{2,18},{4,20},{6,22},{8,24},{10,26},{12,28},{14,30},{16,0},... | collective-permute-start | bytes 786440 | tf_op jit(solution)/shard_map/ppermute | solution.py:309
  9.5 13.3 %all-to-all-start = ((bf16[8,32,640]{2,1,0:T(8,128)(2,1)}), bf16[8,32,640]{2,1,0:T(8,128)(2,1)S(1)}, u32[]{:S(2)}, u32[]{:S(2)}) async-start(bf16[8,32,640]{2,1,0:T(8,128)(2,1)} %bitcast.36), calls=%async_computation | async-start | bytes 655360 | tf_op jit(solution)/shard_map/all_to_all | solution.py:295
  13.5 16.5 %collective-permute-start.1 = (bf16[512,256]{1,0:T(8,128)(2,1)}, bf16[512,256]{1,0:T(8,128)(2,1)S(1)}, u32[]{:S(2)}, u32[]{:S(2)}) collective-permute-start(bf16[512,256]{1,0:T(8,128)(2,1)} %get-tuple-element.64), channel_id=1, source_target_pairs={{0,16},{2,18},{4,20},{6,22},{8,24},{10,26},{12,28},{14,30},{16,0},... | collective-permute-start | bytes 786440 | tf_op jit(solution)/shard_map/ppermute | solution.py:324
  13.8 18.0 %collective-permute-start.3 = (bf16[64,512]{1,0:T(8,128)(2,1)S(1)}, bf16[64,512]{1,0:T(8,128)(2,1)S(1)}, u32[]{:S(2)}, u32[]{:S(2)}) collective-permute-start(bf16[64,512]{1,0:T(8,128)(2,1)S(1)} %pad_maximum_fusion), channel_id=1, source_target_pairs={{0,2},{2,4},{4,6},{6,8},{8,10},{10,12},{12,14},{14,16},{16,18},{18... | collective-permute-start | bytes 196616 | tf_op jit(solution)/shard_map/ppermute | solution.py:329
  14.1 17.7 %collective-permute-start.4 = (bf16[64,512]{1,0:T(8,128)(2,1)S(1)}, bf16[64,512]{1,0:T(8,128)(2,1)S(1)}, u32[]{:S(2)}, u32[]{:S(2)}) collective-permute-start(bf16[64,512]{1,0:T(8,128)(2,1)S(1)} %pad_maximum_fusion.1), channel_id=1, source_target_pairs={{2,0},{4,2},{6,4},{8,6},{10,8},{12,10},{14,12},{16,14},{18,16},{20... | collective-permute-start | bytes 196616 | tf_op jit(solution)/shard_map/ppermute | solution.py:330
  31.9 11.0 %collective-permute-start.5 = (bf16[288,512]{1,0:T(8,128)(2,1)S(1)}, bf16[288,512]{1,0:T(8,128)(2,1)S(1)}, u32[]{:S(2)}, u32[]{:S(2)}) collective-permute-start(bf16[288,512]{1,0:T(8,128)(2,1)S(1)} %get-tuple-element.77), channel_id=1, source_target_pairs={{0,12},{2,14},{4,8},{6,10},{8,4},{10,6},{12,0},{14,2},{16,28},{18,... | collective-permute-start | bytes 884744 | tf_op jit(solution)/shard_map/ppermute | solution.py:300
  32.2 17.0 %collective-permute-start.6 = (bf16[288,512]{1,0:T(8,128)(2,1)S(1)}, bf16[288,512]{1,0:T(8,128)(2,1)S(1)}, u32[]{:S(2)}, u32[]{:S(2)}) collective-permute-start(bf16[288,512]{1,0:T(8,128)(2,1)S(1)} %get-tuple-element.78), channel_id=1, source_target_pairs={{0,4},{2,6},{4,0},{6,2},{8,12},{10,14},{12,8},{14,10},{16,20},{18,... | collective-permute-start | bytes 884744 | tf_op jit(solution)/shard_map/ppermute | solution.py:300
  33.7 15.8 %collective-permute-start.7 = (bf16[288,512]{1,0:T(8,128)(2,1)S(1)}, bf16[288,512]{1,0:T(8,128)(2,1)S(1)}, u32[]{:S(2)}, u32[]{:S(2)}) collective-permute-start(bf16[288,512]{1,0:T(8,128)(2,1)S(1)} %get-tuple-element.79), channel_id=1, source_target_pairs={{0,8},{2,10},{4,12},{6,14},{8,0},{10,2},{12,4},{14,6},{16,24},{18,... | collective-permute-start | bytes 884744 | tf_op jit(solution)/shard_map/ppermute | solution.py:300
  35.4 16.9 %collective-permute-start.8 = (bf16[288,512]{1,0:T(8,128)(2,1)S(1)}, bf16[288,512]{1,0:T(8,128)(2,1)S(1)}, u32[]{:S(2)}, u32[]{:S(2)}) collective-permute-start(bf16[288,512]{1,0:T(8,128)(2,1)S(1)} %get-tuple-element.80), channel_id=1, source_target_pairs={{0,14},{2,12},{4,10},{6,8},{8,6},{10,4},{12,2},{14,0},{16,30},{18,... | collective-permute-start | bytes 884744 | tf_op jit(solution)/shard_map/ppermute | solution.py:300
  35.4 24.3 %collective-permute-start.9 = (bf16[288,512]{1,0:T(8,128)(2,1)S(1)}, bf16[288,512]{1,0:T(8,128)(2,1)S(1)}, u32[]{:S(2)}, u32[]{:S(2)}) collective-permute-start(bf16[288,512]{1,0:T(8,128)(2,1)S(1)} %get-tuple-element.81), channel_id=1, source_target_pairs={{0,6},{2,4},{4,2},{6,0},{8,14},{10,12},{12,10},{14,8},{16,22},{18,... | collective-permute-start | bytes 884744 | tf_op jit(solution)/shard_map/ppermute | solution.py:300
  42.8 16.9 %collective-permute-start.10 = (bf16[288,512]{1,0:T(8,128)(2,1)S(1)}, bf16[288,512]{1,0:T(8,128)(2,1)S(1)}, u32[]{:S(2)}, u32[]{:S(2)}) collective-permute-start(bf16[288,512]{1,0:T(8,128)(2,1)S(1)} %get-tuple-element.82), channel_id=1, source_target_pairs={{0,10},{2,8},{4,14},{6,12},{8,2},{10,0},{12,6},{14,4},{16,26},{18,... | collective-permute-start | bytes 884744 | tf_op jit(solution)/shard_map/ppermute | solution.py:300
  49.1 10.5 %collective-permute-start.11 = (bf16[288,512]{1,0:T(8,128)(2,1)S(1)}, bf16[288,512]{1,0:T(8,128)(2,1)S(1)}, u32[]{:S(2)}, u32[]{:S(2)}) collective-permute-start(bf16[288,512]{1,0:T(8,128)(2,1)S(1)} %get-tuple-element.83), channel_id=1, source_target_pairs={{0,2},{2,0},{4,6},{6,4},{8,10},{10,8},{12,14},{14,12},{16,18},{18,... | collective-permute-start | bytes 884744 | tf_op jit(solution)/shard_map/ppermute | solution.py:300
  70.9 11.0 %collective-permute-start.13 = (bf16[384,256]{1,0:T(8,128)(2,1)S(1)}, bf16[384,256]{1,0:T(8,128)(2,1)S(1)}, u32[]{:S(2)}, u32[]{:S(2)}) collective-permute-start(bf16[384,256]{1,0:T(8,128)(2,1)S(1)} %get-tuple-element.89), channel_id=1, source_target_pairs={{0,4},{2,6},{4,0},{6,2},{8,12},{10,14},{12,8},{14,10},{16,20},{18,... | collective-permute-start | bytes 589832 | tf_op jit(solution)/shard_map/ppermute | solution.py:300
  71.4 10.5 %collective-permute-start.14 = (bf16[384,256]{1,0:T(8,128)(2,1)S(1)}, bf16[384,256]{1,0:T(8,128)(2,1)S(1)}, u32[]{:S(2)}, u32[]{:S(2)}) collective-permute-start(bf16[384,256]{1,0:T(8,128)(2,1)S(1)} %get-tuple-element.90), channel_id=1, source_target_pairs={{0,8},{2,10},{4,12},{6,14},{8,0},{10,2},{12,4},{14,6},{16,24},{18,... | collective-permute-start | bytes 589832 | tf_op jit(solution)/shard_map/ppermute | solution.py:300
  72.5 12.8 %collective-permute-start.15 = (bf16[384,256]{1,0:T(8,128)(2,1)S(1)}, bf16[384,256]{1,0:T(8,128)(2,1)S(1)}, u32[]{:S(2)}, u32[]{:S(2)}) collective-permute-start(bf16[384,256]{1,0:T(8,128)(2,1)S(1)} %get-tuple-element.91), channel_id=1, source_target_pairs={{0,14},{2,12},{4,10},{6,8},{8,6},{10,4},{12,2},{14,0},{16,30},{18,... | collective-permute-start | bytes 589832 | tf_op jit(solution)/shard_map/ppermute | solution.py:300
  73.3 16.7 %collective-permute-start.16 = (bf16[384,256]{1,0:T(8,128)(2,1)S(1)}, bf16[384,256]{1,0:T(8,128)(2,1)S(1)}, u32[]{:S(2)}, u32[]{:S(2)}) collective-permute-start(bf16[384,256]{1,0:T(8,128)(2,1)S(1)} %get-tuple-element.92), channel_id=1, source_target_pairs={{0,6},{2,4},{4,2},{6,0},{8,14},{10,12},{12,10},{14,8},{16,22},{18,... | collective-permute-start | bytes 589832 | tf_op jit(solution)/shard_map/ppermute | solution.py:300
  77.6 13.4 %collective-permute-start.17 = (bf16[384,256]{1,0:T(8,128)(2,1)S(1)}, bf16[384,256]{1,0:T(8,128)(2,1)S(1)}, u32[]{:S(2)}, u32[]{:S(2)}) collective-permute-start(bf16[384,256]{1,0:T(8,128)(2,1)S(1)} %get-tuple-element.93), channel_id=1, source_target_pairs={{0,10},{2,8},{4,14},{6,12},{8,2},{10,0},{12,6},{14,4},{16,26},{18,... | collective-permute-start | bytes 589832 | tf_op jit(solution)/shard_map/ppermute | solution.py:300
  81.9 13.1 %collective-permute-start.22 = (bf16[256,256]{1,0:T(8,128)(2,1)S(1)}, bf16[256,256]{1,0:T(8,128)(2,1)S(1)}, u32[]{:S(2)}, u32[]{:S(2)}) collective-permute-start(bf16[256,256]{1,0:T(8,128)(2,1)S(1)} %get-tuple-element.99), channel_id=1, source_target_pairs={{0,12},{2,14},{4,8},{6,10},{8,4},{10,6},{12,0},{14,2},{16,28},{18,... | collective-permute-start | bytes 393224 | tf_op jit(solution)/shard_map/ppermute | solution.py:300
  85.3 11.8 %collective-permute-start.23 = (bf16[256,256]{1,0:T(8,128)(2,1)S(1)}, bf16[256,256]{1,0:T(8,128)(2,1)S(1)}, u32[]{:S(2)}, u32[]{:S(2)}) collective-permute-start(bf16[256,256]{1,0:T(8,128)(2,1)S(1)} %get-tuple-element.100), channel_id=1, source_target_pairs={{0,4},{2,6},{4,0},{6,2},{8,12},{10,14},{12,8},{14,10},{16,20},{18,... | collective-permute-start | bytes 393224 | tf_op jit(solution)/shard_map/ppermute | solution.py:300
  97.0 11.9 %collective-permute-start.28 = (bf16[256,256]{1,0:T(8,128)(2,1)S(1)}, bf16[256,256]{1,0:T(8,128)(2,1)S(1)}, u32[]{:S(2)}, u32[]{:S(2)}) collective-permute-start(bf16[256,256]{1,0:T(8,128)(2,1)S(1)} %get-tuple-element.105), channel_id=1, source_target_pairs={{0,2},{2,0},{4,6},{6,4},{8,10},{10,8},{12,14},{14,12},{16,18},{18,... | collective-permute-start | bytes 393224 | tf_op jit(solution)/shard_map/ppermute | solution.py:300
  98.1 21.0 %collective-permute-start.21 = (bf16[512,256]{1,0:T(8,128)(2,1)S(1)}, bf16[512,256]{1,0:T(8,128)(2,1)S(1)}, u32[]{:S(2)}, u32[]{:S(2)}) collective-permute-start(bf16[512,256]{1,0:T(8,128)(2,1)S(1)} %slice.55), channel_id=1, source_target_pairs={{0,16},{2,18},{4,20},{6,22},{8,24},{10,26},{12,28},{14,30},{16,0},... | collective-permute-start | bytes 786440 | tf_op jit(solution)/shard_map/ppermute | solution.py:400
  103.2 19.8 %collective-permute-start.30 = (bf16[64,512]{1,0:T(8,128)(2,1)S(1)}, bf16[64,512]{1,0:T(8,128)(2,1)S(1)}, u32[]{:S(2)}, u32[]{:S(2)}) collective-permute-start(bf16[64,512]{1,0:T(8,128)(2,1)S(1)} %get-tuple-element.111), channel_id=1, source_target_pairs={{0,2},{2,4},{4,6},{6,8},{8,10},{10,12},{12,14},{14,16},{16,18},{18... | collective-permute-start | bytes 196616 | tf_op jit(solution)/shard_map/ppermute | solution.py:383
  106.9 18.6 %collective-permute-start.31 = (bf16[64,512]{1,0:T(8,128)(2,1)S(1)}, bf16[64,512]{1,0:T(8,128)(2,1)S(1)}, u32[]{:S(2)}, u32[]{:S(2)}) collective-permute-start(bf16[64,512]{1,0:T(8,128)(2,1)S(1)} %get-tuple-element.112), channel_id=1, source_target_pairs={{2,0},{4,2},{6,4},{8,6},{10,8},{12,10},{14,12},{16,14},{18,16},{20... | collective-permute-start | bytes 196616 | tf_op jit(solution)/shard_map/ppermute | solution.py:382
  110.1 15.4 %collective-permute-start.29 = (bf16[512,256]{1,0:T(8,128)(2,1)S(1)}, bf16[512,256]{1,0:T(8,128)(2,1)S(1)}, u32[]{:S(2)}, u32[]{:S(2)}) collective-permute-start(bf16[512,256]{1,0:T(8,128)(2,1)S(1)} %get-tuple-element.109), channel_id=1, source_target_pairs={{0,16},{2,18},{4,20},{6,22},{8,24},{10,26},{12,28},{14,30},{16,0},... | collective-permute-start | bytes 786440 | tf_op jit(solution)/shard_map/ppermute | solution.py:412
  (22 other events, 212.1 us)

commit v7 on v6

--- a/solution.py
+++ b/solution.py
@@ -13,7 +13,7 @@
 LANES = 128
 MIB = 1024 * 1024
 LOG2E = 1.4426950408889634
-MASKS = (0, 6, 2, 4, 7, 3, 5, 1)
+MASKS = (0, 6, 2, 4, 3, 5, 7, 1)
 
 F32 = jnp.float32
 BF16 = jnp.bfloat16
@@ -409,6 +409,7 @@
     glob_sum = give_v[tokens:weight_at].astype(F32) + far_share[: 2 * rows].astype(F32)
     share = jnp.concatenate([glob_sum, weight_sum], axis=0).astype(BF16)
     own_k, give_k = fold("fold_keys", dk_back, inner_k, 0)
+    give_k, far_v = lax.optimization_barrier((give_k, far_v))
     far_k = lax.ppermute(give_k, "ctx", mirror)
     share, own_k = lax.optimization_barrier((share, own_k))
     if direct:

time: 133 us -> 131 us (0.985)
  waiting for transfers between devices: 68 us -> 57.3 us
  starting transfers between devices: 43.1 us -> 51.8 us
    ppermute x1, waiting for transfers between devices: 8.88 us -> 2.58 us  [shards(): far_v = lax.ppermute(give_v[:tokens], 'ctx', mirror)]
    ppermute x25, starting transfers between devices: 21.9 us -> 27.1 us  [flip(): return lax.ppermute(x, 'ctx', [(i, i ^ mask) for i in range(span)])]
    ppermute x25, waiting for transfers between devices: 47.2 us -> 43.6 us  [flip(): return lax.ppermute(x, 'ctx', [(i, i ^ mask) for i in range(span)])]
    ppermute x1, starting transfers between devices: 1.17 us -> 3.07 us  [shards(): far_v = lax.ppermute(give_v[:tokens], 'ctx', mirror)]
  transfers between devices with their start and end apart: 37 -> 37, of which waited for: 19 -> 18; matrix products, arithmetic and copies ran while one was open for 2% -> 2% of each run, Pallas kernels for 5% -> 5%
where the time goes in v7:
time: 131 us
  waiting for transfers between devices  57.3 us (44%)
  starting transfers between devices  51.8 us (40%)
  Pallas kernels  16.5 us (13%)
  local copies, waits for them, and re-layouts  2.1 us (2%)
  matrix products  1.42 us (1%)
    ppermute x25, waiting for transfers between devices, flip(): return lax.ppermute(x, 'ctx', [(i, i ^ mask) for i in range(span)])  43.6 us
    ppermute x25, starting transfers between devices, flip(): return lax.ppermute(x, 'ctx', [(i, i ^ mask) for i in range(span)])  27.1 us
    pallas_call x1, Pallas kernels, shards(): pl.pallas_call(functools.partial(attend_kernel, half, capacity, direct),...  8.65 us
    ppermute x1, waiting for transfers between devices, shards(): mirror_v = lax.ppermute(v_after, 'ctx', mirror)  5.59 us
    all_to_all x1, waiting for transfers between devices, swap(): lax.all_to_all(x, 'ctx', split_axis=0, concat_axis=0, axis_index_groups=h...  4.4 us
    ppermute x1, starting transfers between devices, shards(): high = lax.ppermute(key_value_edges[1], 'ctx', backward)  4.27 us
    ppermute x1, starting transfers between devices, shards(): mirror_k = lax.ppermute(k, 'ctx', mirror)  4.1 us
    all_to_all x1, starting transfers between devices, swap(): lax.all_to_all(x, 'ctx', split_axis=0, concat_axis=0, axis_index_groups=h...  3.92 us
  transfers between devices with their start and end apart: 37, of which 18 were waited for; matrix products, arithmetic and copies ran while one was open for 2% of the time, Pallas kernels for 5%

profile of v7, /device:TPU:0, one launch (start us, length us, event | category | flops | bytes accessed | tf_op | source)
XLA Modules:
  0.0 130.6 jit_solution(13824456125261352108)
XLA Ops:
  0.6 4.1 %collective-permute-start = (bf16[512,256]{1,0:T(8,128)(2,1)}, bf16[512,256]{1,0:T(8,128)(2,1)S(1)}, u32[]{:S(2)}, u32[]{:S(2)}) collective-permute-start(bf16[512,256]{1,0:T(8,128)(2,1)} %bitcast.26), channel_id=1, source_target_pairs={{0,16},{2,18},{4,20},{6,22},{8,24},{10,26},{12,28},{14,30},{16,0},... | collective-permute-start | bytes 786440 | tf_op jit(solution)/shard_map/ppermute | solution.py:309
  6.7 2.8 %ask.1 = (bf16[256,640]{1,0:T(8,128)(2,1)}, s32[48]{0:T(128)}, bf16[512,256]{1,0:T(8,128)(2,1)}) custom-call(s32[2]{0:T(128)} %pad_add_fusion.here_ref, s32[24]{0:T(128)} %reshape.19.want_ref, s32[1,256]{1,0:T(1,128)} %pos_ref.3, bf16[512,256]{1,0:T(8,128)(2,1)} %bitcast.27, bf16[512,256]{1,0:T(8,128)(2,1)} %bitcast.30), custom_call_target="tpu_custom_call" | custom-call | tf_op jit(solution)/shard_map/ask/pallas_call | solution.py:310
  9.5 3.9 %all-to-all-start = ((bf16[8,32,640]{2,1,0:T(8,128)(2,1)}), bf16[8,32,640]{2,1,0:T(8,128)(2,1)S(1)}, u32[]{:S(2)}, u32[]{:S(2)}) async-start(bf16[8,32,640]{2,1,0:T(8,128)(2,1)} %bitcast.36), calls=%async_computation | async-start | bytes 655360 | tf_op jit(solution)/shard_map/all_to_all | solution.py:295
  14.1 4.3 %collective-permute-start.4 = (bf16[64,512]{1,0:T(8,128)(2,1)S(1)}, bf16[64,512]{1,0:T(8,128)(2,1)S(1)}, u32[]{:S(2)}, u32[]{:S(2)}) collective-permute-start(bf16[64,512]{1,0:T(8,128)(2,1)S(1)} %pad_maximum_fusion.1), channel_id=1, source_target_pairs={{2,0},{4,2},{6,4},{8,6},{10,8},{12,10},{14,12},{16,14},{18,16},{20... | collective-permute-start | bytes 196616 | tf_op jit(solution)/shard_map/ppermute | solution.py:330
  18.4 4.4 %all-to-all-done = bf16[8,32,640]{2,1,0:T(8,128)(2,1)S(1)} async-done(((bf16[8,32,640]{2,1,0:T(8,128)(2,1)}), bf16[8,32,640]{2,1,0:T(8,128)(2,1)S(1)}, u32[]{:S(2)}, u32[]{:S(2)}) %all-to-all-start) | async-done | bytes 327712 | tf_op jit(solution)/shard_map/all_to_all | solution.py:295
  24.4 5.6 %collective-permute-done.1.mv_ref = bf16[512,256]{1,0:T(8,128)(2,1)S(1)} collective-permute-done((bf16[512,256]{1,0:T(8,128)(2,1)}, bf16[512,256]{1,0:T(8,128)(2,1)S(1)}, u32[]{:S(2)}, u32[]{:S(2)}) %collective-permute-start.1) | collective-permute-done | bytes 262176 | tf_op jit(solution)/shard_map/ppermute | solution.py:324
  36.8 6.0 %collective-permute-done.5.refs_1_ = bf16[288,512]{1,0:T(8,128)(2,1)S(1)} collective-permute-done((bf16[288,512]{1,0:T(8,128)(2,1)S(1)}, bf16[288,512]{1,0:T(8,128)(2,1)S(1)}, u32[]{:S(2)}, u32[]{:S(2)}) %collective-permute-start.5) | collective-permute-done | bytes 294944 | tf_op jit(solution)/shard_map/ppermute | solution.py:300
  42.8 4.3 %collective-permute-done.6.refs_2_ = bf16[288,512]{1,0:T(8,128)(2,1)S(1)} collective-permute-done((bf16[288,512]{1,0:T(8,128)(2,1)S(1)}, bf16[288,512]{1,0:T(8,128)(2,1)S(1)}, u32[]{:S(2)}, u32[]{:S(2)}) %collective-permute-start.6) | collective-permute-done | bytes 294944 | tf_op jit(solution)/shard_map/ppermute | solution.py:300
  49.3 6.0 %collective-permute-done.8.refs_4_ = bf16[288,512]{1,0:T(8,128)(2,1)S(1)} collective-permute-done((bf16[288,512]{1,0:T(8,128)(2,1)S(1)}, bf16[288,512]{1,0:T(8,128)(2,1)S(1)}, u32[]{:S(2)}, u32[]{:S(2)}) %collective-permute-start.8) | collective-permute-done | bytes 294944 | tf_op jit(solution)/shard_map/ppermute | solution.py:300
  55.3 3.1 %collective-permute-done.10.refs_6_ = bf16[288,512]{1,0:T(8,128)(2,1)S(1)} collective-permute-done((bf16[288,512]{1,0:T(8,128)(2,1)S(1)}, bf16[288,512]{1,0:T(8,128)(2,1)S(1)}, u32[]{:S(2)}, u32[]{:S(2)}) %collective-permute-start.10) | collective-permute-done | bytes 294944 | tf_op jit(solution)/shard_map/ppermute | solution.py:300
  59.0 8.7 %attend.1 = (bf16[256,256]{1,0:T(8,128)(2,1)S(1)}, bf16[256,256]{1,0:T(8,128)(2,1)S(1)}, bf16[256,256]{1,0:T(8,128)(2,1)S(1)}, bf16[256,256]{1,0:T(8,128)(2,1)S(...) custom-call(s32[48]{0:T(128)S(1)} %copy-done.7, ...), custom_call_target="tpu_custom_call" | custom-call | tf_op jit(solution)/shard_map/attend/pallas_call | solution.py:354
  67.6 3.1 %collective-permute-start.12 = (bf16[384,256]{1,0:T(8,128)(2,1)S(1)}, bf16[384,256]{1,0:T(8,128)(2,1)S(1)}, u32[]{:S(2)}, u32[]{:S(2)}) collective-permute-start(bf16[384,256]{1,0:T(8,128)(2,1)S(1)} %get-tuple-element.90), channel_id=1, source_target_pairs={{0,12},{2,14},{4,8},{6,10},{8,4},{10,6},{12,0},{14,2},{16,28},{18,... | collective-permute-start | bytes 589832 | tf_op jit(solution)/shard_map/ppermute | solution.py:300
  77.5 3.3 %collective-permute-done.13.refs_2_ = bf16[384,256]{1,0:T(8,128)(2,1)S(1)} collective-permute-done((bf16[384,256]{1,0:T(8,128)(2,1)S(1)}, bf16[384,256]{1,0:T(8,128)(2,1)S(1)}, u32[]{:S(2)}, u32[]{:S(2)}) %collective-permute-start.13) | collective-permute-done | bytes 196640 | tf_op jit(solution)/shard_map/ppermute | solution.py:300
  80.8 2.1 %collective-permute-start.22 = (bf16[256,256]{1,0:T(8,128)(2,1)S(1)}, bf16[256,256]{1,0:T(8,128)(2,1)S(1)}, u32[]{:S(2)}, u32[]{:S(2)}) collective-permute-start(bf16[256,256]{1,0:T(8,128)(2,1)S(1)} %get-tuple-element.101), channel_id=1, source_target_pairs={{0,12},{2,14},{4,8},{6,10},{8,4},{10,6},{12,0},{14,2},{16,28},{18,... | collective-permute-start | bytes 393224 | tf_op jit(solution)/shard_map/ppermute | solution.py:300
  85.9 2.4 %collective-permute-start.24 = (bf16[256,256]{1,0:T(8,128)(2,1)S(1)}, bf16[256,256]{1,0:T(8,128)(2,1)S(1)}, u32[]{:S(2)}, u32[]{:S(2)}) collective-permute-start(bf16[256,256]{1,0:T(8,128)(2,1)S(1)} %get-tuple-element.103), channel_id=1, source_target_pairs={{0,8},{2,10},{4,12},{6,14},{8,0},{10,2},{12,4},{14,6},{16,24},{18,... | collective-permute-start | bytes 393224 | tf_op jit(solution)/shard_map/ppermute | solution.py:300
  90.6 2.3 %collective-permute-start.19 = (bf16[128,256]{1,0:T(8,128)(2,1)S(1)}, bf16[128,256]{1,0:T(8,128)(2,1)S(1)}, u32[]{:S(2)}, u32[]{:S(2)}) collective-permute-start(bf16[128,256]{1,0:T(8,128)(2,1)S(1)} %slice.51), channel_id=1, source_target_pairs={{0,16},{2,18},{4,20},{6,22},{8,24},{10,26},{12,28},{14,30},{16,0},... | collective-permute-start | bytes 196616 | tf_op jit(solution)/shard_map/ppermute | solution.py:399
  97.0 3.1 %collective-permute-start.21 = (bf16[512,256]{1,0:T(8,128)(2,1)S(1)}, bf16[512,256]{1,0:T(8,128)(2,1)S(1)}, u32[]{:S(2)}, u32[]{:S(2)}) collective-permute-start(bf16[512,256]{1,0:T(8,128)(2,1)S(1)} %slice.55), channel_id=1, source_target_pairs={{0,16},{2,18},{4,20},{6,22},{8,24},{10,26},{12,28},{14,30},{16,0},... | collective-permute-start | bytes 786440 | tf_op jit(solution)/shard_map/ppermute | solution.py:400
  101.7 3.6 %collective-permute-done.27.refs_6_ = bf16[256,256]{1,0:T(8,128)(2,1)S(1)} collective-permute-done((bf16[256,256]{1,0:T(8,128)(2,1)S(1)}, bf16[256,256]{1,0:T(8,128)(2,1)S(1)}, u32[]{:S(2)}, u32[]{:S(2)}) %collective-permute-start.27) | collective-permute-done | bytes 131104 | tf_op jit(solution)/shard_map/ppermute | solution.py:300
  105.3 3.4 %collective-permute-start.31 = (bf16[64,512]{1,0:T(8,128)(2,1)S(1)}, bf16[64,512]{1,0:T(8,128)(2,1)S(1)}, u32[]{:S(2)}, u32[]{:S(2)}) collective-permute-start(bf16[64,512]{1,0:T(8,128)(2,1)S(1)} %get-tuple-element.116), channel_id=1, source_target_pairs={{2,0},{4,2},{6,4},{8,6},{10,8},{12,10},{14,12},{16,14},{18,16},{20... | collective-permute-start | bytes 196616 | tf_op jit(solution)/shard_map/ppermute | solution.py:382
  109.8 2.6 %collective-permute-done.21.far_v_ref = bf16[512,256]{1,0:T(8,128)(2,1)S(1)} collective-permute-done((bf16[512,256]{1,0:T(8,128)(2,1)S(1)}, bf16[512,256]{1,0:T(8,128)(2,1)S(1)}, u32[]{:S(2)}, u32[]{:S(2)}) %collective-permute-start.21) | collective-permute-done | bytes 262176 | tf_op jit(solution)/shard_map/ppermute | solution.py:400
  113.7 3.1 %collective-permute-start.35 = (bf16[256,256]{1,0:T(8,128)(2,1)S(1)}, bf16[256,256]{1,0:T(8,128)(2,1)S(1)}, u32[]{:S(2)}, u32[]{:S(2)}) collective-permute-start(bf16[256,256]{1,0:T(8,128)(2,1)S(1)} %constant_dynamic-update-slice_fusion.refs_0_), channel_id=1, source_target_pairs={{0,8},{2,10},{4,12},{6,14},{8,0},{10,2},{12,4},{14,6},{16,24},{18,... | collective-permute-start | bytes 393224 | tf_op jit(solution)/shard_map/ppermute | solution.py:300
  119.4 2.6 %collective-permute-done.35.refs_3_ = bf16[256,256]{1,0:T(8,128)(2,1)S(1)} collective-permute-done((bf16[256,256]{1,0:T(8,128)(2,1)S(1)}, bf16[256,256]{1,0:T(8,128)(2,1)S(1)}, u32[]{:S(2)}, u32[]{:S(2)}) %collective-permute-start.35) | collective-permute-done | bytes 131104 | tf_op jit(solution)/shard_map/ppermute | solution.py:300
  122.1 2.6 %collective-permute-done.34.refs_2_ = bf16[256,256]{1,0:T(8,128)(2,1)S(1)} collective-permute-done((bf16[256,256]{1,0:T(8,128)(2,1)S(1)}, bf16[256,256]{1,0:T(8,128)(2,1)S(1)}, u32[]{:S(2)}, u32[]{:S(2)}) %collective-permute-start.34) | collective-permute-done | bytes 131104 | tf_op jit(solution)/shard_map/ppermute | solution.py:300
  124.7 4.1 %collective-permute-done.33.refs_1_ = bf16[256,256]{1,0:T(8,128)(2,1)S(1)} collective-permute-done((bf16[256,256]{1,0:T(8,128)(2,1)S(1)}, bf16[256,256]{1,0:T(8,128)(2,1)S(1)}, u32[]{:S(2)}, u32[]{:S(2)}) %collective-permute-start.33) | collective-permute-done | bytes 131104 | tf_op jit(solution)/shard_map/ppermute | solution.py:300
  (91 shorter events, 38.4 us)
Async XLA Ops:
  0.6 23.8 %collective-permute-start = (bf16[512,256]{1,0:T(8,128)(2,1)}, bf16[512,256]{1,0:T(8,128)(2,1)S(1)}, u32[]{:S(2)}, u32[]{:S(2)}) collective-permute-start(bf16[512,256]{1,0:T(8,128)(2,1)} %bitcast.26), channel_id=1, source_target_pairs={{0,16},{2,18},{4,20},{6,22},{8,24},{10,26},{12,28},{14,30},{16,0},... | collective-permute-start | bytes 786440 | tf_op jit(solution)/shard_map/ppermute | solution.py:309
  9.5 13.3 %all-to-all-start = ((bf16[8,32,640]{2,1,0:T(8,128)(2,1)}), bf16[8,32,640]{2,1,0:T(8,128)(2,1)S(1)}, u32[]{:S(2)}, u32[]{:S(2)}) async-start(bf16[8,32,640]{2,1,0:T(8,128)(2,1)} %bitcast.36), calls=%async_computation | async-start | bytes 655360 | tf_op jit(solution)/shard_map/all_to_all | solution.py:295
  13.5 16.5 %collective-permute-start.1 = (bf16[512,256]{1,0:T(8,128)(2,1)}, bf16[512,256]{1,0:T(8,128)(2,1)S(1)}, u32[]{:S(2)}, u32[]{:S(2)}) collective-permute-start(bf16[512,256]{1,0:T(8,128)(2,1)} %get-tuple-element.66), channel_id=1, source_target_pairs={{0,16},{2,18},{4,20},{6,22},{8,24},{10,26},{12,28},{14,30},{16,0},... | collective-permute-start | bytes 786440 | tf_op jit(solution)/shard_map/ppermute | solution.py:324
  13.8 18.0 %collective-permute-start.3 = (bf16[64,512]{1,0:T(8,128)(2,1)S(1)}, bf16[64,512]{1,0:T(8,128)(2,1)S(1)}, u32[]{:S(2)}, u32[]{:S(2)}) collective-permute-start(bf16[64,512]{1,0:T(8,128)(2,1)S(1)} %pad_maximum_fusion), channel_id=1, source_target_pairs={{0,2},{2,4},{4,6},{6,8},{8,10},{10,12},{12,14},{14,16},{16,18},{18... | collective-permute-start | bytes 196616 | tf_op jit(solution)/shard_map/ppermute | solution.py:329
  14.1 17.7 %collective-permute-start.4 = (bf16[64,512]{1,0:T(8,128)(2,1)S(1)}, bf16[64,512]{1,0:T(8,128)(2,1)S(1)}, u32[]{:S(2)}, u32[]{:S(2)}) collective-permute-start(bf16[64,512]{1,0:T(8,128)(2,1)S(1)} %pad_maximum_fusion.1), channel_id=1, source_target_pairs={{2,0},{4,2},{6,4},{8,6},{10,8},{12,10},{14,12},{16,14},{18,16},{20... | collective-permute-start | bytes 196616 | tf_op jit(solution)/shard_map/ppermute | solution.py:330
  31.9 11.0 %collective-permute-start.5 = (bf16[288,512]{1,0:T(8,128)(2,1)S(1)}, bf16[288,512]{1,0:T(8,128)(2,1)S(1)}, u32[]{:S(2)}, u32[]{:S(2)}) collective-permute-start(bf16[288,512]{1,0:T(8,128)(2,1)S(1)} %get-tuple-element.79), channel_id=1, source_target_pairs={{0,12},{2,14},{4,8},{6,10},{8,4},{10,6},{12,0},{14,2},{16,28},{18,... | collective-permute-start | bytes 884744 | tf_op jit(solution)/shard_map/ppermute | solution.py:300
  32.2 14.9 %collective-permute-start.6 = (bf16[288,512]{1,0:T(8,128)(2,1)S(1)}, bf16[288,512]{1,0:T(8,128)(2,1)S(1)}, u32[]{:S(2)}, u32[]{:S(2)}) collective-permute-start(bf16[288,512]{1,0:T(8,128)(2,1)S(1)} %get-tuple-element.80), channel_id=1, source_target_pairs={{0,4},{2,6},{4,0},{6,2},{8,12},{10,14},{12,8},{14,10},{16,20},{18,... | collective-permute-start | bytes 884744 | tf_op jit(solution)/shard_map/ppermute | solution.py:300
  33.7 15.6 %collective-permute-start.7 = (bf16[288,512]{1,0:T(8,128)(2,1)S(1)}, bf16[288,512]{1,0:T(8,128)(2,1)S(1)}, u32[]{:S(2)}, u32[]{:S(2)}) collective-permute-start(bf16[288,512]{1,0:T(8,128)(2,1)S(1)} %get-tuple-element.81), channel_id=1, source_target_pairs={{0,8},{2,10},{4,12},{6,14},{8,0},{10,2},{12,4},{14,6},{16,24},{18,... | collective-permute-start | bytes 884744 | tf_op jit(solution)/shard_map/ppermute | solution.py:300
  35.4 19.9 %collective-permute-start.8 = (bf16[288,512]{1,0:T(8,128)(2,1)S(1)}, bf16[288,512]{1,0:T(8,128)(2,1)S(1)}, u32[]{:S(2)}, u32[]{:S(2)}) collective-permute-start(bf16[288,512]{1,0:T(8,128)(2,1)S(1)} %get-tuple-element.82), channel_id=1, source_target_pairs={{0,6},{2,4},{4,2},{6,0},{8,14},{10,12},{12,10},{14,8},{16,22},{18,... | collective-permute-start | bytes 884744 | tf_op jit(solution)/shard_map/ppermute | solution.py:300
  35.4 19.9 %collective-permute-start.9 = (bf16[288,512]{1,0:T(8,128)(2,1)S(1)}, bf16[288,512]{1,0:T(8,128)(2,1)S(1)}, u32[]{:S(2)}, u32[]{:S(2)}) collective-permute-start(bf16[288,512]{1,0:T(8,128)(2,1)S(1)} %get-tuple-element.83), channel_id=1, source_target_pairs={{0,10},{2,8},{4,14},{6,12},{8,2},{10,0},{12,6},{14,4},{16,26},{18,... | collective-permute-start | bytes 884744 | tf_op jit(solution)/shard_map/ppermute | solution.py:300
  42.8 15.5 %collective-permute-start.10 = (bf16[288,512]{1,0:T(8,128)(2,1)S(1)}, bf16[288,512]{1,0:T(8,128)(2,1)S(1)}, u32[]{:S(2)}, u32[]{:S(2)}) collective-permute-start(bf16[288,512]{1,0:T(8,128)(2,1)S(1)} %get-tuple-element.84), channel_id=1, source_target_pairs={{0,14},{2,12},{4,10},{6,8},{8,6},{10,4},{12,2},{14,0},{16,30},{18,... | collective-permute-start | bytes 884744 | tf_op jit(solution)/shard_map/ppermute | solution.py:300
  47.1 11.2 %collective-permute-start.11 = (bf16[288,512]{1,0:T(8,128)(2,1)S(1)}, bf16[288,512]{1,0:T(8,128)(2,1)S(1)}, u32[]{:S(2)}, u32[]{:S(2)}) collective-permute-start(bf16[288,512]{1,0:T(8,128)(2,1)S(1)} %get-tuple-element.85), channel_id=1, source_target_pairs={{0,2},{2,0},{4,6},{6,4},{8,10},{10,8},{12,14},{14,12},{16,18},{18,... | collective-permute-start | bytes 884744 | tf_op jit(solution)/shard_map/ppermute | solution.py:300
  71.4 13.5 %collective-permute-start.15 = (bf16[384,256]{1,0:T(8,128)(2,1)S(1)}, bf16[384,256]{1,0:T(8,128)(2,1)S(1)}, u32[]{:S(2)}, u32[]{:S(2)}) collective-permute-start(bf16[384,256]{1,0:T(8,128)(2,1)S(1)} %get-tuple-element.93), channel_id=1, source_target_pairs={{0,6},{2,4},{4,2},{6,0},{8,14},{10,12},{12,10},{14,8},{16,22},{18,... | collective-permute-start | bytes 589832 | tf_op jit(solution)/shard_map/ppermute | solution.py:300
  73.1 12.8 %collective-permute-start.16 = (bf16[384,256]{1,0:T(8,128)(2,1)S(1)}, bf16[384,256]{1,0:T(8,128)(2,1)S(1)}, u32[]{:S(2)}, u32[]{:S(2)}) collective-permute-start(bf16[384,256]{1,0:T(8,128)(2,1)S(1)} %get-tuple-element.94), channel_id=1, source_target_pairs={{0,10},{2,8},{4,14},{6,12},{8,2},{10,0},{12,6},{14,4},{16,26},{18,... | collective-permute-start | bytes 589832 | tf_op jit(solution)/shard_map/ppermute | solution.py:300
  76.6 12.8 %collective-permute-start.17 = (bf16[384,256]{1,0:T(8,128)(2,1)S(1)}, bf16[384,256]{1,0:T(8,128)(2,1)S(1)}, u32[]{:S(2)}, u32[]{:S(2)}) collective-permute-start(bf16[384,256]{1,0:T(8,128)(2,1)S(1)} %get-tuple-element.95), channel_id=1, source_target_pairs={{0,14},{2,12},{4,10},{6,8},{8,6},{10,4},{12,2},{14,0},{16,30},{18,... | collective-permute-start | bytes 589832 | tf_op jit(solution)/shard_map/ppermute | solution.py:300
  80.8 12.5 %collective-permute-start.22 = (bf16[256,256]{1,0:T(8,128)(2,1)S(1)}, bf16[256,256]{1,0:T(8,128)(2,1)S(1)}, u32[]{:S(2)}, u32[]{:S(2)}) collective-permute-start(bf16[256,256]{1,0:T(8,128)(2,1)S(1)} %get-tuple-element.101), channel_id=1, source_target_pairs={{0,12},{2,14},{4,8},{6,10},{8,4},{10,6},{12,0},{14,2},{16,28},{18,... | collective-permute-start | bytes 393224 | tf_op jit(solution)/shard_map/ppermute | solution.py:300
  84.9 10.6 %collective-permute-start.23 = (bf16[256,256]{1,0:T(8,128)(2,1)S(1)}, bf16[256,256]{1,0:T(8,128)(2,1)S(1)}, u32[]{:S(2)}, u32[]{:S(2)}) collective-permute-start(bf16[256,256]{1,0:T(8,128)(2,1)S(1)} %get-tuple-element.102), channel_id=1, source_target_pairs={{0,4},{2,6},{4,0},{6,2},{8,12},{10,14},{12,8},{14,10},{16,20},{18,... | collective-permute-start | bytes 393224 | tf_op jit(solution)/shard_map/ppermute | solution.py:300
  85.9 10.6 %collective-permute-start.24 = (bf16[256,256]{1,0:T(8,128)(2,1)S(1)}, bf16[256,256]{1,0:T(8,128)(2,1)S(1)}, u32[]{:S(2)}, u32[]{:S(2)}) collective-permute-start(bf16[256,256]{1,0:T(8,128)(2,1)S(1)} %get-tuple-element.103), channel_id=1, source_target_pairs={{0,8},{2,10},{4,12},{6,14},{8,0},{10,2},{12,4},{14,6},{16,24},{18,... | collective-permute-start | bytes 393224 | tf_op jit(solution)/shard_map/ppermute | solution.py:300
  96.5 12.2 %collective-permute-start.28 = (bf16[256,256]{1,0:T(8,128)(2,1)S(1)}, bf16[256,256]{1,0:T(8,128)(2,1)S(1)}, u32[]{:S(2)}, u32[]{:S(2)}) collective-permute-start(bf16[256,256]{1,0:T(8,128)(2,1)S(1)} %get-tuple-element.107), channel_id=1, source_target_pairs={{0,2},{2,0},{4,6},{6,4},{8,10},{10,8},{12,14},{14,12},{16,18},{18,... | collective-permute-start | bytes 393224 | tf_op jit(solution)/shard_map/ppermute | solution.py:300
  97.0 15.4 %collective-permute-start.21 = (bf16[512,256]{1,0:T(8,128)(2,1)S(1)}, bf16[512,256]{1,0:T(8,128)(2,1)S(1)}, u32[]{:S(2)}, u32[]{:S(2)}) collective-permute-start(bf16[512,256]{1,0:T(8,128)(2,1)S(1)} %slice.55), channel_id=1, source_target_pairs={{0,16},{2,18},{4,20},{6,22},{8,24},{10,26},{12,28},{14,30},{16,0},... | collective-permute-start | bytes 786440 | tf_op jit(solution)/shard_map/ppermute | solution.py:400
  101.7 15.9 %collective-permute-start.30 = (bf16[64,512]{1,0:T(8,128)(2,1)S(1)}, bf16[64,512]{1,0:T(8,128)(2,1)S(1)}, u32[]{:S(2)}, u32[]{:S(2)}) collective-permute-start(bf16[64,512]{1,0:T(8,128)(2,1)S(1)} %get-tuple-element.115), channel_id=1, source_target_pairs={{0,2},{2,4},{4,6},{6,8},{8,10},{10,12},{12,14},{14,16},{16,18},{18... | collective-permute-start | bytes 196616 | tf_op jit(solution)/shard_map/ppermute | solution.py:383
  105.3 14.1 %collective-permute-start.31 = (bf16[64,512]{1,0:T(8,128)(2,1)S(1)}, bf16[64,512]{1,0:T(8,128)(2,1)S(1)}, u32[]{:S(2)}, u32[]{:S(2)}) collective-permute-start(bf16[64,512]{1,0:T(8,128)(2,1)S(1)} %get-tuple-element.116), channel_id=1, source_target_pairs={{2,0},{4,2},{6,4},{8,6},{10,8},{12,10},{14,12},{16,14},{18,16},{20... | collective-permute-start | bytes 196616 | tf_op jit(solution)/shard_map/ppermute | solution.py:382
  112.4 16.3 %collective-permute-start.29 = (bf16[512,256]{1,0:T(8,128)(2,1)S(1)}, bf16[512,256]{1,0:T(8,128)(2,1)S(1)}, u32[]{:S(2)}, u32[]{:S(2)}) collective-permute-start(bf16[512,256]{1,0:T(8,128)(2,1)S(1)} %get-tuple-element.113), channel_id=1, source_target_pairs={{0,16},{2,18},{4,20},{6,22},{8,24},{10,26},{12,28},{14,30},{16,0},... | collective-permute-start | bytes 786440 | tf_op jit(solution)/shard_map/ppermute | solution.py:413
  117.6 11.2 %collective-permute-start.33 = (bf16[256,256]{1,0:T(8,128)(2,1)S(1)}, bf16[256,256]{1,0:T(8,128)(2,1)S(1)}, u32[]{:S(2)}, u32[]{:S(2)}) collective-permute-start(bf16[256,256]{1,0:T(8,128)(2,1)S(1)} %constant_dynamic-update-slice_fusion.refs_0_), channel_id=1, source_target_pairs={{0,12},{2,14},{4,8},{6,10},{8,4},{10,6},{12,0},{14,2},{16,28},{18,... | collective-permute-start | bytes 393224 | tf_op jit(solution)/shard_map/ppermute | solution.py:300
  (22 other events, 221.2 us)

commit v8 on v7

--- a/solution.py
+++ b/solution.py
@@ -13,7 +13,7 @@
 LANES = 128
 MIB = 1024 * 1024
 LOG2E = 1.4426950408889634
-MASKS = (0, 6, 2, 4, 3, 5, 7, 1)
+MASKS = (0, 6, 2, 4, 3, 5, 1, 7)
 
 F32 = jnp.float32
 BF16 = jnp.bfloat16
@@ -414,8 +414,8 @@
     share, own_k = lax.optimization_barrier((share, own_k))
     if direct:
         pair = jnp.concatenate([share, flip(share, 1)], axis=0)
-        totals = [pair] + [flip(pair, mask) for mask in (6, 2, 4)]
-        masks = (0, 1, 6, 7, 2, 3, 4, 5)
+        totals = [pair] + [flip(pair, mask) for mask in (2, 4, 6)]
+        masks = (0, 1, 2, 3, 4, 5, 6, 7)
     else:
         totals = [lax.all_gather(share, "ctx", axis=0, axis_index_groups=halves, tiled=True)]
         masks = tuple(range(half))

time: 131 us -> 130 us (level)
  waiting for transfers between devices: 57.3 us -> 55 us
  starting transfers between devices: 51.8 us -> 53.2 us
    ppermute x25, waiting for transfers between devices: 43.6 us -> 38.9 us  [flip(): return lax.ppermute(x, 'ctx', [(i, i ^ mask) for i in range(span)])]
    ppermute x1, waiting for transfers between devices: 2.58 us -> 5.01 us  [shards(): far_v = lax.ppermute(give_v[:tokens], 'ctx', mirror)]
  transfers between devices with their start and end apart: 37 -> 37, of which waited for: 18 -> 16; matrix products, arithmetic and copies ran while one was open for 2% -> 2% of each run, Pallas kernels for 5% -> 5%
where the time goes in v8:
time: 130 us
  waiting for transfers between devices  55 us (42%)
  starting transfers between devices  53.2 us (41%)
  Pallas kernels  16.5 us (13%)
  local copies, waits for them, and re-layouts  2.1 us (2%)
  matrix products  1.42 us (1%)
    ppermute x25, waiting for transfers between devices, flip(): return lax.ppermute(x, 'ctx', [(i, i ^ mask) for i in range(span)])  38.9 us
    ppermute x25, starting transfers between devices, flip(): return lax.ppermute(x, 'ctx', [(i, i ^ mask) for i in range(span)])  27.5 us
    pallas_call x1, Pallas kernels, shards(): pl.pallas_call(functools.partial(attend_kernel, half, capacity, direct),...  8.65 us
    ppermute x1, waiting for transfers between devices, shards(): mirror_v = lax.ppermute(v_after, 'ctx', mirror)  5.59 us
    ppermute x1, waiting for transfers between devices, shards(): far_v = lax.ppermute(give_v[:tokens], 'ctx', mirror)  5.01 us
    ppermute x1, starting transfers between devices, shards(): from_high = lax.ppermute(edge_low, 'ctx', backward)  4.44 us
    all_to_all x1, waiting for transfers between devices, swap(): lax.all_to_all(x, 'ctx', split_axis=0, concat_axis=0, axis_index_groups=h...  4.4 us
    ppermute x1, starting transfers between devices, shards(): high = lax.ppermute(key_value_edges[1], 'ctx', backward)  4.27 us
  transfers between devices with their start and end apart: 37, of which 16 were waited for; matrix products, arithmetic and copies ran while one was open for 2% of the time, Pallas kernels for 5%

profile of v8, /device:TPU:0, one launch (start us, length us, event | category | flops | bytes accessed | tf_op | source)
XLA Modules:
  0.0 129.7 jit_solution(13154921656567165556)
XLA Ops:
  0.6 4.1 %collective-permute-start = (bf16[512,256]{1,0:T(8,128)(2,1)}, bf16[512,256]{1,0:T(8,128)(2,1)S(1)}, u32[]{:S(2)}, u32[]{:S(2)}) collective-permute-start(bf16[512,256]{1,0:T(8,128)(2,1)} %bitcast.26), channel_id=1, source_target_pairs={{0,16},{2,18},{4,20},{6,22},{8,24},{10,26},{12,28},{14,30},{16,0},... | collective-permute-start | bytes 786440 | tf_op jit(solution)/shard_map/ppermute | solution.py:309
  6.7 2.8 %ask.1 = (bf16[256,640]{1,0:T(8,128)(2,1)}, s32[48]{0:T(128)}, bf16[512,256]{1,0:T(8,128)(2,1)}) custom-call(s32[2]{0:T(128)} %pad_add_fusion.here_ref, s32[24]{0:T(128)} %reshape.19.want_ref, s32[1,256]{1,0:T(1,128)} %pos_ref.3, bf16[512,256]{1,0:T(8,128)(2,1)} %bitcast.27, bf16[512,256]{1,0:T(8,128)(2,1)} %bitcast.30), custom_call_target="tpu_custom_call" | custom-call | tf_op jit(solution)/shard_map/ask/pallas_call | solution.py:310
  9.5 3.9 %all-to-all-start = ((bf16[8,32,640]{2,1,0:T(8,128)(2,1)}), bf16[8,32,640]{2,1,0:T(8,128)(2,1)S(1)}, u32[]{:S(2)}, u32[]{:S(2)}) async-start(bf16[8,32,640]{2,1,0:T(8,128)(2,1)} %bitcast.36), calls=%async_computation | async-start | bytes 655360 | tf_op jit(solution)/shard_map/all_to_all | solution.py:295
  14.1 4.3 %collective-permute-start.4 = (bf16[64,512]{1,0:T(8,128)(2,1)S(1)}, bf16[64,512]{1,0:T(8,128)(2,1)S(1)}, u32[]{:S(2)}, u32[]{:S(2)}) collective-permute-start(bf16[64,512]{1,0:T(8,128)(2,1)S(1)} %pad_maximum_fusion.1), channel_id=1, source_target_pairs={{2,0},{4,2},{6,4},{8,6},{10,8},{12,10},{14,12},{16,14},{18,16},{20... | collective-permute-start | bytes 196616 | tf_op jit(solution)/shard_map/ppermute | solution.py:330
  18.4 4.4 %all-to-all-done = bf16[8,32,640]{2,1,0:T(8,128)(2,1)S(1)} async-done(((bf16[8,32,640]{2,1,0:T(8,128)(2,1)}), bf16[8,32,640]{2,1,0:T(8,128)(2,1)S(1)}, u32[]{:S(2)}, u32[]{:S(2)}) %all-to-all-start) | async-done | bytes 327712 | tf_op jit(solution)/shard_map/all_to_all | solution.py:295
  24.4 5.6 %collective-permute-done.1.mv_ref = bf16[512,256]{1,0:T(8,128)(2,1)S(1)} collective-permute-done((bf16[512,256]{1,0:T(8,128)(2,1)}, bf16[512,256]{1,0:T(8,128)(2,1)S(1)}, u32[]{:S(2)}, u32[]{:S(2)}) %collective-permute-start.1) | collective-permute-done | bytes 262176 | tf_op jit(solution)/shard_map/ppermute | solution.py:324
  36.8 6.0 %collective-permute-done.5.refs_1_ = bf16[288,512]{1,0:T(8,128)(2,1)S(1)} collective-permute-done((bf16[288,512]{1,0:T(8,128)(2,1)S(1)}, bf16[288,512]{1,0:T(8,128)(2,1)S(1)}, u32[]{:S(2)}, u32[]{:S(2)}) %collective-permute-start.5) | collective-permute-done | bytes 294944 | tf_op jit(solution)/shard_map/ppermute | solution.py:300
  42.8 4.3 %collective-permute-done.6.refs_2_ = bf16[288,512]{1,0:T(8,128)(2,1)S(1)} collective-permute-done((bf16[288,512]{1,0:T(8,128)(2,1)S(1)}, bf16[288,512]{1,0:T(8,128)(2,1)S(1)}, u32[]{:S(2)}, u32[]{:S(2)}) %collective-permute-start.6) | collective-permute-done | bytes 294944 | tf_op jit(solution)/shard_map/ppermute | solution.py:300
  49.3 6.0 %collective-permute-done.8.refs_4_ = bf16[288,512]{1,0:T(8,128)(2,1)S(1)} collective-permute-done((bf16[288,512]{1,0:T(8,128)(2,1)S(1)}, bf16[288,512]{1,0:T(8,128)(2,1)S(1)}, u32[]{:S(2)}, u32[]{:S(2)}) %collective-permute-start.8) | collective-permute-done | bytes 294944 | tf_op jit(solution)/shard_map/ppermute | solution.py:300
  55.3 3.1 %collective-permute-done.11.refs_7_ = bf16[288,512]{1,0:T(8,128)(2,1)S(1)} collective-permute-done((bf16[288,512]{1,0:T(8,128)(2,1)S(1)}, bf16[288,512]{1,0:T(8,128)(2,1)S(1)}, u32[]{:S(2)}, u32[]{:S(2)}) %collective-permute-start.11) | collective-permute-done | bytes 294944 | tf_op jit(solution)/shard_map/ppermute | solution.py:300
  59.0 8.6 %attend.1 = (bf16[256,256]{1,0:T(8,128)(2,1)S(1)}, bf16[256,256]{1,0:T(8,128)(2,1)S(1)}, bf16[256,256]{1,0:T(8,128)(2,1)S(1)}, bf16[256,256]{1,0:T(8,128)(2,1)S(...) custom-call(s32[48]{0:T(128)S(1)} %copy-done.7, ...), custom_call_target="tpu_custom_call" | custom-call | tf_op jit(solution)/shard_map/attend/pallas_call | solution.py:354
  67.6 3.1 %collective-permute-start.12 = (bf16[384,256]{1,0:T(8,128)(2,1)S(1)}, bf16[384,256]{1,0:T(8,128)(2,1)S(1)}, u32[]{:S(2)}, u32[]{:S(2)}) collective-permute-start(bf16[384,256]{1,0:T(8,128)(2,1)S(1)} %get-tuple-element.90), channel_id=1, source_target_pairs={{0,12},{2,14},{4,8},{6,10},{8,4},{10,6},{12,0},{14,2},{16,28},{18,... | collective-permute-start | bytes 589832 | tf_op jit(solution)/shard_map/ppermute | solution.py:300
  74.5 2.0 %collective-permute-done.12.refs_1_ = bf16[384,256]{1,0:T(8,128)(2,1)S(1)} collective-permute-done((bf16[384,256]{1,0:T(8,128)(2,1)S(1)}, bf16[384,256]{1,0:T(8,128)(2,1)S(1)}, u32[]{:S(2)}, u32[]{:S(2)}) %collective-permute-start.12) | collective-permute-done | bytes 196640 | tf_op jit(solution)/shard_map/ppermute | solution.py:300
  76.6 4.2 %collective-permute-done.13.refs_2_ = bf16[384,256]{1,0:T(8,128)(2,1)S(1)} collective-permute-done((bf16[384,256]{1,0:T(8,128)(2,1)S(1)}, bf16[384,256]{1,0:T(8,128)(2,1)S(1)}, u32[]{:S(2)}, u32[]{:S(2)}) %collective-permute-start.13) | collective-permute-done | bytes 196640 | tf_op jit(solution)/shard_map/ppermute | solution.py:300
  85.9 1.9 %collective-permute-start.24 = (bf16[256,256]{1,0:T(8,128)(2,1)S(1)}, bf16[256,256]{1,0:T(8,128)(2,1)S(1)}, u32[]{:S(2)}, u32[]{:S(2)}) collective-permute-start(bf16[256,256]{1,0:T(8,128)(2,1)S(1)} %get-tuple-element.103), channel_id=1, source_target_pairs={{0,8},{2,10},{4,12},{6,14},{8,0},{10,2},{12,4},{14,6},{16,24},{18,... | collective-permute-start | bytes 393224 | tf_op jit(solution)/shard_map/ppermute | solution.py:300
  90.6 2.3 %collective-permute-start.19 = (bf16[128,256]{1,0:T(8,128)(2,1)S(1)}, bf16[128,256]{1,0:T(8,128)(2,1)S(1)}, u32[]{:S(2)}, u32[]{:S(2)}) collective-permute-start(bf16[128,256]{1,0:T(8,128)(2,1)S(1)} %slice.51), channel_id=1, source_target_pairs={{0,16},{2,18},{4,20},{6,22},{8,24},{10,26},{12,28},{14,30},{16,0},... | collective-permute-start | bytes 196616 | tf_op jit(solution)/shard_map/ppermute | solution.py:399
  93.2 2.3 %collective-permute-start.26 = (bf16[256,256]{1,0:T(8,128)(2,1)S(1)}, bf16[256,256]{1,0:T(8,128)(2,1)S(1)}, u32[]{:S(2)}, u32[]{:S(2)}) collective-permute-start(bf16[256,256]{1,0:T(8,128)(2,1)S(1)} %get-tuple-element.105), channel_id=1, source_target_pairs={{0,10},{2,8},{4,14},{6,12},{8,2},{10,0},{12,6},{14,4},{16,26},{18,... | collective-permute-start | bytes 393224 | tf_op jit(solution)/shard_map/ppermute | solution.py:300
  97.0 3.1 %collective-permute-start.21 = (bf16[512,256]{1,0:T(8,128)(2,1)S(1)}, bf16[512,256]{1,0:T(8,128)(2,1)S(1)}, u32[]{:S(2)}, u32[]{:S(2)}) collective-permute-start(bf16[512,256]{1,0:T(8,128)(2,1)S(1)} %slice.55), channel_id=1, source_target_pairs={{0,16},{2,18},{4,20},{6,22},{8,24},{10,26},{12,28},{14,30},{16,0},... | collective-permute-start | bytes 786440 | tf_op jit(solution)/shard_map/ppermute | solution.py:400
  101.7 4.4 %collective-permute-start.31 = (bf16[64,512]{1,0:T(8,128)(2,1)S(1)}, bf16[64,512]{1,0:T(8,128)(2,1)S(1)}, u32[]{:S(2)}, u32[]{:S(2)}) collective-permute-start(bf16[64,512]{1,0:T(8,128)(2,1)S(1)} %get-tuple-element.116), channel_id=1, source_target_pairs={{2,0},{4,2},{6,4},{8,6},{10,8},{12,10},{14,12},{16,14},{18,16},{20... | collective-permute-start | bytes 196616 | tf_op jit(solution)/shard_map/ppermute | solution.py:382
  107.3 5.0 %collective-permute-done.21.far_v_ref = bf16[512,256]{1,0:T(8,128)(2,1)S(1)} collective-permute-done((bf16[512,256]{1,0:T(8,128)(2,1)S(1)}, bf16[512,256]{1,0:T(8,128)(2,1)S(1)}, u32[]{:S(2)}, u32[]{:S(2)}) %collective-permute-start.21) | collective-permute-done | bytes 262176 | tf_op jit(solution)/shard_map/ppermute | solution.py:400
  113.6 3.2 %collective-permute-start.35 = (bf16[256,256]{1,0:T(8,128)(2,1)S(1)}, bf16[256,256]{1,0:T(8,128)(2,1)S(1)}, u32[]{:S(2)}, u32[]{:S(2)}) collective-permute-start(bf16[256,256]{1,0:T(8,128)(2,1)S(1)} %constant_dynamic-update-slice_fusion.refs_0_), channel_id=1, source_target_pairs={{0,12},{2,14},{4,8},{6,10},{8,4},{10,6},{12,0},{14,2},{16,28},{18,... | collective-permute-start | bytes 393224 | tf_op jit(solution)/shard_map/ppermute | solution.py:300
  119.1 2.9 %collective-permute-done.35.refs_3_ = bf16[256,256]{1,0:T(8,128)(2,1)S(1)} collective-permute-done((bf16[256,256]{1,0:T(8,128)(2,1)S(1)}, bf16[256,256]{1,0:T(8,128)(2,1)S(1)}, u32[]{:S(2)}, u32[]{:S(2)}) %collective-permute-start.35) | collective-permute-done | bytes 131104 | tf_op jit(solution)/shard_map/ppermute | solution.py:300
  122.0 5.8 %collective-permute-done.34.refs_2_ = bf16[256,256]{1,0:T(8,128)(2,1)S(1)} collective-permute-done((bf16[256,256]{1,0:T(8,128)(2,1)S(1)}, bf16[256,256]{1,0:T(8,128)(2,1)S(1)}, u32[]{:S(2)}, u32[]{:S(2)}) %collective-permute-start.34) | collective-permute-done | bytes 131104 | tf_op jit(solution)/shard_map/ppermute | solution.py:300
  127.8 1.9 %finish.1 = (bf16[512,256]{1,0:T(8,128)(2,1)}, bf16[512,256]{1,0:T(8,128)(2,1)}, f32[256,512]{1,0:T(8,128)}) custom-call(s32[2]{0:T(128)S(1)} %copy-done.5, s32[1,256]{1,0:T(1,128)S(1)} %copy-done.6, f32[512,256]{1,0:T(8,128)S(1)} %get-tuple-element.109.own_k_ref, f32[512,256]{1,0:T(8,128)S(1)} %get-tuple-element.110.own_v_ref, ...), custom_call_target="tpu_custom_call" | custom-call | tf_op jit(solution)/shard_map/finish/pallas_call | solution.py:424
  (91 shorter events, 33.6 us)
Async XLA Ops:
  0.6 23.8 %collective-permute-start = (bf16[512,256]{1,0:T(8,128)(2,1)}, bf16[512,256]{1,0:T(8,128)(2,1)S(1)}, u32[]{:S(2)}, u32[]{:S(2)}) collective-permute-start(bf16[512,256]{1,0:T(8,128)(2,1)} %bitcast.26), channel_id=1, source_target_pairs={{0,16},{2,18},{4,20},{6,22},{8,24},{10,26},{12,28},{14,30},{16,0},... | collective-permute-start | bytes 786440 | tf_op jit(solution)/shard_map/ppermute | solution.py:309
  9.5 13.3 %all-to-all-start = ((bf16[8,32,640]{2,1,0:T(8,128)(2,1)}), bf16[8,32,640]{2,1,0:T(8,128)(2,1)S(1)}, u32[]{:S(2)}, u32[]{:S(2)}) async-start(bf16[8,32,640]{2,1,0:T(8,128)(2,1)} %bitcast.36), calls=%async_computation | async-start | bytes 655360 | tf_op jit(solution)/shard_map/all_to_all | solution.py:295
  13.5 16.5 %collective-permute-start.1 = (bf16[512,256]{1,0:T(8,128)(2,1)}, bf16[512,256]{1,0:T(8,128)(2,1)S(1)}, u32[]{:S(2)}, u32[]{:S(2)}) collective-permute-start(bf16[512,256]{1,0:T(8,128)(2,1)} %get-tuple-element.66), channel_id=1, source_target_pairs={{0,16},{2,18},{4,20},{6,22},{8,24},{10,26},{12,28},{14,30},{16,0},... | collective-permute-start | bytes 786440 | tf_op jit(solution)/shard_map/ppermute | solution.py:324
  13.8 18.0 %collective-permute-start.3 = (bf16[64,512]{1,0:T(8,128)(2,1)S(1)}, bf16[64,512]{1,0:T(8,128)(2,1)S(1)}, u32[]{:S(2)}, u32[]{:S(2)}) collective-permute-start(bf16[64,512]{1,0:T(8,128)(2,1)S(1)} %pad_maximum_fusion), channel_id=1, source_target_pairs={{0,2},{2,4},{4,6},{6,8},{8,10},{10,12},{12,14},{14,16},{16,18},{18... | collective-permute-start | bytes 196616 | tf_op jit(solution)/shard_map/ppermute | solution.py:329
  14.1 17.7 %collective-permute-start.4 = (bf16[64,512]{1,0:T(8,128)(2,1)S(1)}, bf16[64,512]{1,0:T(8,128)(2,1)S(1)}, u32[]{:S(2)}, u32[]{:S(2)}) collective-permute-start(bf16[64,512]{1,0:T(8,128)(2,1)S(1)} %pad_maximum_fusion.1), channel_id=1, source_target_pairs={{2,0},{4,2},{6,4},{8,6},{10,8},{12,10},{14,12},{16,14},{18,16},{20... | collective-permute-start | bytes 196616 | tf_op jit(solution)/shard_map/ppermute | solution.py:330
  31.9 11.0 %collective-permute-start.5 = (bf16[288,512]{1,0:T(8,128)(2,1)S(1)}, bf16[288,512]{1,0:T(8,128)(2,1)S(1)}, u32[]{:S(2)}, u32[]{:S(2)}) collective-permute-start(bf16[288,512]{1,0:T(8,128)(2,1)S(1)} %get-tuple-element.79), channel_id=1, source_target_pairs={{0,12},{2,14},{4,8},{6,10},{8,4},{10,6},{12,0},{14,2},{16,28},{18,... | collective-permute-start | bytes 884744 | tf_op jit(solution)/shard_map/ppermute | solution.py:300
  32.2 14.9 %collective-permute-start.6 = (bf16[288,512]{1,0:T(8,128)(2,1)S(1)}, bf16[288,512]{1,0:T(8,128)(2,1)S(1)}, u32[]{:S(2)}, u32[]{:S(2)}) collective-permute-start(bf16[288,512]{1,0:T(8,128)(2,1)S(1)} %get-tuple-element.80), channel_id=1, source_target_pairs={{0,4},{2,6},{4,0},{6,2},{8,12},{10,14},{12,8},{14,10},{16,20},{18,... | collective-permute-start | bytes 884744 | tf_op jit(solution)/shard_map/ppermute | solution.py:300
  33.7 15.6 %collective-permute-start.7 = (bf16[288,512]{1,0:T(8,128)(2,1)S(1)}, bf16[288,512]{1,0:T(8,128)(2,1)S(1)}, u32[]{:S(2)}, u32[]{:S(2)}) collective-permute-start(bf16[288,512]{1,0:T(8,128)(2,1)S(1)} %get-tuple-element.81), channel_id=1, source_target_pairs={{0,8},{2,10},{4,12},{6,14},{8,0},{10,2},{12,4},{14,6},{16,24},{18,... | collective-permute-start | bytes 884744 | tf_op jit(solution)/shard_map/ppermute | solution.py:300
  35.4 19.9 %collective-permute-start.8 = (bf16[288,512]{1,0:T(8,128)(2,1)S(1)}, bf16[288,512]{1,0:T(8,128)(2,1)S(1)}, u32[]{:S(2)}, u32[]{:S(2)}) collective-permute-start(bf16[288,512]{1,0:T(8,128)(2,1)S(1)} %get-tuple-element.82), channel_id=1, source_target_pairs={{0,6},{2,4},{4,2},{6,0},{8,14},{10,12},{12,10},{14,8},{16,22},{18,... | collective-permute-start | bytes 884744 | tf_op jit(solution)/shard_map/ppermute | solution.py:300
  35.4 19.9 %collective-permute-start.9 = (bf16[288,512]{1,0:T(8,128)(2,1)S(1)}, bf16[288,512]{1,0:T(8,128)(2,1)S(1)}, u32[]{:S(2)}, u32[]{:S(2)}) collective-permute-start(bf16[288,512]{1,0:T(8,128)(2,1)S(1)} %get-tuple-element.83), channel_id=1, source_target_pairs={{0,10},{2,8},{4,14},{6,12},{8,2},{10,0},{12,6},{14,4},{16,26},{18,... | collective-permute-start | bytes 884744 | tf_op jit(solution)/shard_map/ppermute | solution.py:300
  42.8 12.5 %collective-permute-start.10 = (bf16[288,512]{1,0:T(8,128)(2,1)S(1)}, bf16[288,512]{1,0:T(8,128)(2,1)S(1)}, u32[]{:S(2)}, u32[]{:S(2)}) collective-permute-start(bf16[288,512]{1,0:T(8,128)(2,1)S(1)} %get-tuple-element.84), channel_id=1, source_target_pairs={{0,2},{2,0},{4,6},{6,4},{8,10},{10,8},{12,14},{14,12},{16,18},{18,... | collective-permute-start | bytes 884744 | tf_op jit(solution)/shard_map/ppermute | solution.py:300
  47.1 11.2 %collective-permute-start.11 = (bf16[288,512]{1,0:T(8,128)(2,1)S(1)}, bf16[288,512]{1,0:T(8,128)(2,1)S(1)}, u32[]{:S(2)}, u32[]{:S(2)}) collective-permute-start(bf16[288,512]{1,0:T(8,128)(2,1)S(1)} %get-tuple-element.85), channel_id=1, source_target_pairs={{0,14},{2,12},{4,10},{6,8},{8,6},{10,4},{12,2},{14,0},{16,30},{18,... | collective-permute-start | bytes 884744 | tf_op jit(solution)/shard_map/ppermute | solution.py:300
  70.8 11.7 %collective-permute-start.14 = (bf16[384,256]{1,0:T(8,128)(2,1)S(1)}, bf16[384,256]{1,0:T(8,128)(2,1)S(1)}, u32[]{:S(2)}, u32[]{:S(2)}) collective-permute-start(bf16[384,256]{1,0:T(8,128)(2,1)S(1)} %get-tuple-element.92), channel_id=1, source_target_pairs={{0,8},{2,10},{4,12},{6,14},{8,0},{10,2},{12,4},{14,6},{16,24},{18,... | collective-permute-start | bytes 589832 | tf_op jit(solution)/shard_map/ppermute | solution.py:300
  71.3 13.5 %collective-permute-start.15 = (bf16[384,256]{1,0:T(8,128)(2,1)S(1)}, bf16[384,256]{1,0:T(8,128)(2,1)S(1)}, u32[]{:S(2)}, u32[]{:S(2)}) collective-permute-start(bf16[384,256]{1,0:T(8,128)(2,1)S(1)} %get-tuple-element.93), channel_id=1, source_target_pairs={{0,6},{2,4},{4,2},{6,0},{8,14},{10,12},{12,10},{14,8},{16,22},{18,... | collective-permute-start | bytes 589832 | tf_op jit(solution)/shard_map/ppermute | solution.py:300
  73.1 12.8 %collective-permute-start.16 = (bf16[384,256]{1,0:T(8,128)(2,1)S(1)}, bf16[384,256]{1,0:T(8,128)(2,1)S(1)}, u32[]{:S(2)}, u32[]{:S(2)}) collective-permute-start(bf16[384,256]{1,0:T(8,128)(2,1)S(1)} %get-tuple-element.94), channel_id=1, source_target_pairs={{0,10},{2,8},{4,14},{6,12},{8,2},{10,0},{12,6},{14,4},{16,26},{18,... | collective-permute-start | bytes 589832 | tf_op jit(solution)/shard_map/ppermute | solution.py:300
  76.6 11.3 %collective-permute-start.17 = (bf16[384,256]{1,0:T(8,128)(2,1)S(1)}, bf16[384,256]{1,0:T(8,128)(2,1)S(1)}, u32[]{:S(2)}, u32[]{:S(2)}) collective-permute-start(bf16[384,256]{1,0:T(8,128)(2,1)S(1)} %get-tuple-element.95), channel_id=1, source_target_pairs={{0,2},{2,0},{4,6},{6,4},{8,10},{10,8},{12,14},{14,12},{16,18},{18,... | collective-permute-start | bytes 589832 | tf_op jit(solution)/shard_map/ppermute | solution.py:300
  82.5 10.7 %collective-permute-start.22 = (bf16[256,256]{1,0:T(8,128)(2,1)S(1)}, bf16[256,256]{1,0:T(8,128)(2,1)S(1)}, u32[]{:S(2)}, u32[]{:S(2)}) collective-permute-start(bf16[256,256]{1,0:T(8,128)(2,1)S(1)} %get-tuple-element.101), channel_id=1, source_target_pairs={{0,12},{2,14},{4,8},{6,10},{8,4},{10,6},{12,0},{14,2},{16,28},{18,... | collective-permute-start | bytes 393224 | tf_op jit(solution)/shard_map/ppermute | solution.py:300
  84.9 10.6 %collective-permute-start.23 = (bf16[256,256]{1,0:T(8,128)(2,1)S(1)}, bf16[256,256]{1,0:T(8,128)(2,1)S(1)}, u32[]{:S(2)}, u32[]{:S(2)}) collective-permute-start(bf16[256,256]{1,0:T(8,128)(2,1)S(1)} %get-tuple-element.102), channel_id=1, source_target_pairs={{0,4},{2,6},{4,0},{6,2},{8,12},{10,14},{12,8},{14,10},{16,20},{18,... | collective-permute-start | bytes 393224 | tf_op jit(solution)/shard_map/ppermute | solution.py:300
  97.0 15.3 %collective-permute-start.21 = (bf16[512,256]{1,0:T(8,128)(2,1)S(1)}, bf16[512,256]{1,0:T(8,128)(2,1)S(1)}, u32[]{:S(2)}, u32[]{:S(2)}) collective-permute-start(bf16[512,256]{1,0:T(8,128)(2,1)S(1)} %slice.55), channel_id=1, source_target_pairs={{0,16},{2,18},{4,20},{6,22},{8,24},{10,26},{12,28},{14,30},{16,0},... | collective-permute-start | bytes 786440 | tf_op jit(solution)/shard_map/ppermute | solution.py:400
  101.7 15.1 %collective-permute-start.30 = (bf16[64,512]{1,0:T(8,128)(2,1)S(1)}, bf16[64,512]{1,0:T(8,128)(2,1)S(1)}, u32[]{:S(2)}, u32[]{:S(2)}) collective-permute-start(bf16[64,512]{1,0:T(8,128)(2,1)S(1)} %get-tuple-element.115), channel_id=1, source_target_pairs={{0,2},{2,4},{4,6},{6,8},{8,10},{10,12},{12,14},{14,16},{16,18},{18... | collective-permute-start | bytes 196616 | tf_op jit(solution)/shard_map/ppermute | solution.py:383
  101.7 17.4 %collective-permute-start.31 = (bf16[64,512]{1,0:T(8,128)(2,1)S(1)}, bf16[64,512]{1,0:T(8,128)(2,1)S(1)}, u32[]{:S(2)}, u32[]{:S(2)}) collective-permute-start(bf16[64,512]{1,0:T(8,128)(2,1)S(1)} %get-tuple-element.116), channel_id=1, source_target_pairs={{2,0},{4,2},{6,4},{8,6},{10,8},{12,10},{14,12},{16,14},{18,16},{20... | collective-permute-start | bytes 196616 | tf_op jit(solution)/shard_map/ppermute | solution.py:382
  112.3 15.5 %collective-permute-start.29 = (bf16[512,256]{1,0:T(8,128)(2,1)S(1)}, bf16[512,256]{1,0:T(8,128)(2,1)S(1)}, u32[]{:S(2)}, u32[]{:S(2)}) collective-permute-start(bf16[512,256]{1,0:T(8,128)(2,1)S(1)} %get-tuple-element.113), channel_id=1, source_target_pairs={{0,16},{2,18},{4,20},{6,22},{8,24},{10,26},{12,28},{14,30},{16,0},... | collective-permute-start | bytes 786440 | tf_op jit(solution)/shard_map/ppermute | solution.py:413
  116.8 11.0 %collective-permute-start.34 = (bf16[256,256]{1,0:T(8,128)(2,1)S(1)}, bf16[256,256]{1,0:T(8,128)(2,1)S(1)}, u32[]{:S(2)}, u32[]{:S(2)}) collective-permute-start(bf16[256,256]{1,0:T(8,128)(2,1)S(1)} %constant_dynamic-update-slice_fusion.refs_0_), channel_id=1, source_target_pairs={{0,8},{2,10},{4,12},{6,14},{8,0},{10,2},{12,4},{14,6},{16,24},{18,... | collective-permute-start | bytes 393224 | tf_op jit(solution)/shard_map/ppermute | solution.py:300
  116.8 11.0 %collective-permute-start.33 = (bf16[256,256]{1,0:T(8,128)(2,1)S(1)}, bf16[256,256]{1,0:T(8,128)(2,1)S(1)}, u32[]{:S(2)}, u32[]{:S(2)}) collective-permute-start(bf16[256,256]{1,0:T(8,128)(2,1)S(1)} %constant_dynamic-update-slice_fusion.refs_0_), channel_id=1, source_target_pairs={{0,4},{2,6},{4,0},{6,2},{8,12},{10,14},{12,8},{14,10},{16,20},{18,... | collective-permute-start | bytes 393224 | tf_op jit(solution)/shard_map/ppermute | solution.py:300
  (22 other events, 220.0 us)

commit v9 on v8

--- a/solution.py
+++ b/solution.py
@@ -164,7 +164,7 @@
         kc_ref[:win] = pad_ref[pl.ds(base, win), :width]
         vc_ref[:win] = pad_ref[pl.ds(base, win), width:]
         for j in range(RAND):
-            slot = pl.ds(pl.multiple_of(place_ref[i * RAND + j], BLK), BLK)
+            slot = pl.ds(pl.multiple_of(place_ref[i * RAND + j], 16), BLK)
             kc_ref[win + j * BLK : win + (j + 1) * BLK] = arr_ref[slot, :width]
             vc_ref[win + j * BLK : win + (j + 1) * BLK] = arr_ref[slot, width:]
         q_by_head = by_head(q_ref[pl.ds(base, BLK), :])
@@ -411,7 +411,9 @@
     own_k, give_k = fold("fold_keys", dk_back, inner_k, 0)
     give_k, far_v = lax.optimization_barrier((give_k, far_v))
     far_k = lax.ppermute(give_k, "ctx", mirror)
-    share, own_k = lax.optimization_barrier((share, own_k))
+    share, own_k, from_high, from_low = lax.optimization_barrier(
+        (share, own_k, from_high, from_low)
+    )
     if direct:
         pair = jnp.concatenate([share, flip(share, 1)], axis=0)
         totals = [pair] + [flip(pair, mask) for mask in (2, 4, 6)]

time: 130 us -> 130 us (level)
  waiting for transfers between devices: 55 us -> 56.4 us
  starting transfers between devices: 53.2 us -> 51.9 us
    ppermute x1, starting transfers between devices: 4.44 us -> 1.44 us  [shards(): from_high = lax.ppermute(edge_low, 'ctx', backward)]
    ppermute x1, starting transfers between devices: 0.07 us -> 2.52 us  [shards(): far_k = lax.ppermute(give_k, 'ctx', mirror)]
where the time goes in v9:
time: 130 us
  waiting for transfers between devices  56.4 us (43%)
  starting transfers between devices  51.9 us (40%)
  Pallas kernels  16.5 us (13%)
  local copies, waits for them, and re-layouts  2.1 us (2%)
  matrix products  1.42 us (1%)
    ppermute x25, waiting for transfers between devices, flip(): return lax.ppermute(x, 'ctx', [(i, i ^ mask) for i in range(span)])  39.8 us
    ppermute x25, starting transfers between devices, flip(): return lax.ppermute(x, 'ctx', [(i, i ^ mask) for i in range(span)])  26.6 us
    pallas_call x1, Pallas kernels, shards(): pl.pallas_call(functools.partial(attend_kernel, half, capacity, direct),...  8.65 us
    ppermute x1, waiting for transfers between devices, shards(): mirror_v = lax.ppermute(v_after, 'ctx', mirror)  5.59 us
    ppermute x1, waiting for transfers between devices, shards(): far_v = lax.ppermute(give_v[:tokens], 'ctx', mirror)  5.56 us
    all_to_all x1, waiting for transfers between devices, swap(): lax.all_to_all(x, 'ctx', split_axis=0, concat_axis=0, axis_index_groups=h...  4.4 us
    ppermute x1, starting transfers between devices, shards(): high = lax.ppermute(key_value_edges[1], 'ctx', backward)  4.27 us
    ppermute x1, starting transfers between devices, shards(): mirror_k = lax.ppermute(k, 'ctx', mirror)  4.1 us
  transfers between devices with their start and end apart: 37, of which 16 were waited for; matrix products, arithmetic and copies ran while one was open for 2% of the time, Pallas kernels for 5%

profile of v9, /device:TPU:0, one launch (start us, length us, event | category | flops | bytes accessed | tf_op | source)
XLA Modules:
  0.0 129.8 jit_solution(4429029644012651239)
XLA Ops:
  0.6 4.1 %collective-permute-start = (bf16[512,256]{1,0:T(8,128)(2,1)}, bf16[512,256]{1,0:T(8,128)(2,1)S(1)}, u32[]{:S(2)}, u32[]{:S(2)}) collective-permute-start(bf16[512,256]{1,0:T(8,128)(2,1)} %bitcast.26), channel_id=1, source_target_pairs={{0,16},{2,18},{4,20},{6,22},{8,24},{10,26},{12,28},{14,30},{16,0},... | collective-permute-start | bytes 786440 | tf_op jit(solution)/shard_map/ppermute | solution.py:309
  6.7 2.8 %ask.1 = (bf16[256,640]{1,0:T(8,128)(2,1)}, s32[48]{0:T(128)}, bf16[512,256]{1,0:T(8,128)(2,1)}) custom-call(s32[2]{0:T(128)} %pad_add_fusion.here_ref, s32[24]{0:T(128)} %reshape.19.want_ref, s32[1,256]{1,0:T(1,128)} %pos_ref.3, bf16[512,256]{1,0:T(8,128)(2,1)} %bitcast.27, bf16[512,256]{1,0:T(8,128)(2,1)} %bitcast.30), custom_call_target="tpu_custom_call" | custom-call | tf_op jit(solution)/shard_map/ask/pallas_call | solution.py:310
  9.5 3.9 %all-to-all-start = ((bf16[8,32,640]{2,1,0:T(8,128)(2,1)}), bf16[8,32,640]{2,1,0:T(8,128)(2,1)S(1)}, u32[]{:S(2)}, u32[]{:S(2)}) async-start(bf16[8,32,640]{2,1,0:T(8,128)(2,1)} %bitcast.36), calls=%async_computation | async-start | bytes 655360 | tf_op jit(solution)/shard_map/all_to_all | solution.py:295
  14.1 4.3 %collective-permute-start.4 = (bf16[64,512]{1,0:T(8,128)(2,1)S(1)}, bf16[64,512]{1,0:T(8,128)(2,1)S(1)}, u32[]{:S(2)}, u32[]{:S(2)}) collective-permute-start(bf16[64,512]{1,0:T(8,128)(2,1)S(1)} %pad_maximum_fusion.1), channel_id=1, source_target_pairs={{2,0},{4,2},{6,4},{8,6},{10,8},{12,10},{14,12},{16,14},{18,16},{20... | collective-permute-start | bytes 196616 | tf_op jit(solution)/shard_map/ppermute | solution.py:330
  18.4 4.4 %all-to-all-done = bf16[8,32,640]{2,1,0:T(8,128)(2,1)S(1)} async-done(((bf16[8,32,640]{2,1,0:T(8,128)(2,1)}), bf16[8,32,640]{2,1,0:T(8,128)(2,1)S(1)}, u32[]{:S(2)}, u32[]{:S(2)}) %all-to-all-start) | async-done | bytes 327712 | tf_op jit(solution)/shard_map/all_to_all | solution.py:295
  24.4 5.6 %collective-permute-done.1.mv_ref = bf16[512,256]{1,0:T(8,128)(2,1)S(1)} collective-permute-done((bf16[512,256]{1,0:T(8,128)(2,1)}, bf16[512,256]{1,0:T(8,128)(2,1)S(1)}, u32[]{:S(2)}, u32[]{:S(2)}) %collective-permute-start.1) | collective-permute-done | bytes 262176 | tf_op jit(solution)/shard_map/ppermute | solution.py:324
  36.8 6.0 %collective-permute-done.5.refs_1_ = bf16[288,512]{1,0:T(8,128)(2,1)S(1)} collective-permute-done((bf16[288,512]{1,0:T(8,128)(2,1)S(1)}, bf16[288,512]{1,0:T(8,128)(2,1)S(1)}, u32[]{:S(2)}, u32[]{:S(2)}) %collective-permute-start.5) | collective-permute-done | bytes 294944 | tf_op jit(solution)/shard_map/ppermute | solution.py:300
  42.8 4.3 %collective-permute-done.6.refs_2_ = bf16[288,512]{1,0:T(8,128)(2,1)S(1)} collective-permute-done((bf16[288,512]{1,0:T(8,128)(2,1)S(1)}, bf16[288,512]{1,0:T(8,128)(2,1)S(1)}, u32[]{:S(2)}, u32[]{:S(2)}) %collective-permute-start.6) | collective-permute-done | bytes 294944 | tf_op jit(solution)/shard_map/ppermute | solution.py:300
  49.3 6.0 %collective-permute-done.8.refs_4_ = bf16[288,512]{1,0:T(8,128)(2,1)S(1)} collective-permute-done((bf16[288,512]{1,0:T(8,128)(2,1)S(1)}, bf16[288,512]{1,0:T(8,128)(2,1)S(1)}, u32[]{:S(2)}, u32[]{:S(2)}) %collective-permute-start.8) | collective-permute-done | bytes 294944 | tf_op jit(solution)/shard_map/ppermute | solution.py:300
  55.3 3.1 %collective-permute-done.11.refs_7_ = bf16[288,512]{1,0:T(8,128)(2,1)S(1)} collective-permute-done((bf16[288,512]{1,0:T(8,128)(2,1)S(1)}, bf16[288,512]{1,0:T(8,128)(2,1)S(1)}, u32[]{:S(2)}, u32[]{:S(2)}) %collective-permute-start.11) | collective-permute-done | bytes 294944 | tf_op jit(solution)/shard_map/ppermute | solution.py:300
  59.0 8.6 %attend.1 = (bf16[256,256]{1,0:T(8,128)(2,1)S(1)}, bf16[256,256]{1,0:T(8,128)(2,1)S(1)}, bf16[256,256]{1,0:T(8,128)(2,1)S(1)}, bf16[256,256]{1,0:T(8,128)(2,1)S(...) custom-call(s32[48]{0:T(128)S(1)} %copy-done.7, ...), custom_call_target="tpu_custom_call" | custom-call | tf_op jit(solution)/shard_map/attend/pallas_call | solution.py:354
  67.6 3.1 %collective-permute-start.12 = (bf16[384,256]{1,0:T(8,128)(2,1)S(1)}, bf16[384,256]{1,0:T(8,128)(2,1)S(1)}, u32[]{:S(2)}, u32[]{:S(2)}) collective-permute-start(bf16[384,256]{1,0:T(8,128)(2,1)S(1)} %get-tuple-element.92), channel_id=1, source_target_pairs={{0,12},{2,14},{4,8},{6,10},{8,4},{10,6},{12,0},{14,2},{16,28},{18,... | collective-permute-start | bytes 589832 | tf_op jit(solution)/shard_map/ppermute | solution.py:300
  74.5 2.0 %collective-permute-done.12.refs_1_ = bf16[384,256]{1,0:T(8,128)(2,1)S(1)} collective-permute-done((bf16[384,256]{1,0:T(8,128)(2,1)S(1)}, bf16[384,256]{1,0:T(8,128)(2,1)S(1)}, u32[]{:S(2)}, u32[]{:S(2)}) %collective-permute-start.12) | collective-permute-done | bytes 196640 | tf_op jit(solution)/shard_map/ppermute | solution.py:300
  76.6 4.2 %collective-permute-done.13.refs_2_ = bf16[384,256]{1,0:T(8,128)(2,1)S(1)} collective-permute-done((bf16[384,256]{1,0:T(8,128)(2,1)S(1)}, bf16[384,256]{1,0:T(8,128)(2,1)S(1)}, u32[]{:S(2)}, u32[]{:S(2)}) %collective-permute-start.13) | collective-permute-done | bytes 196640 | tf_op jit(solution)/shard_map/ppermute | solution.py:300
  90.6 2.3 %collective-permute-start.19 = (bf16[128,256]{1,0:T(8,128)(2,1)S(1)}, bf16[128,256]{1,0:T(8,128)(2,1)S(1)}, u32[]{:S(2)}, u32[]{:S(2)}) collective-permute-start(bf16[128,256]{1,0:T(8,128)(2,1)S(1)} %slice.51), channel_id=1, source_target_pairs={{0,16},{2,18},{4,20},{6,22},{8,24},{10,26},{12,28},{14,30},{16,0},... | collective-permute-start | bytes 196616 | tf_op jit(solution)/shard_map/ppermute | solution.py:399
  93.2 2.3 %collective-permute-start.26 = (bf16[256,256]{1,0:T(8,128)(2,1)S(1)}, bf16[256,256]{1,0:T(8,128)(2,1)S(1)}, u32[]{:S(2)}, u32[]{:S(2)}) collective-permute-start(bf16[256,256]{1,0:T(8,128)(2,1)S(1)} %get-tuple-element.107), channel_id=1, source_target_pairs={{0,10},{2,8},{4,14},{6,12},{8,2},{10,0},{12,6},{14,4},{16,26},{18,... | collective-permute-start | bytes 393224 | tf_op jit(solution)/shard_map/ppermute | solution.py:300
  97.0 3.1 %collective-permute-start.21 = (bf16[512,256]{1,0:T(8,128)(2,1)S(1)}, bf16[512,256]{1,0:T(8,128)(2,1)S(1)}, u32[]{:S(2)}, u32[]{:S(2)}) collective-permute-start(bf16[512,256]{1,0:T(8,128)(2,1)S(1)} %slice.55), channel_id=1, source_target_pairs={{0,16},{2,18},{4,20},{6,22},{8,24},{10,26},{12,28},{14,30},{16,0},... | collective-permute-start | bytes 786440 | tf_op jit(solution)/shard_map/ppermute | solution.py:400
  103.2 2.4 %collective-permute-done.28.refs_7_ = bf16[256,256]{1,0:T(8,128)(2,1)S(1)} collective-permute-done((bf16[256,256]{1,0:T(8,128)(2,1)S(1)}, bf16[256,256]{1,0:T(8,128)(2,1)S(1)}, u32[]{:S(2)}, u32[]{:S(2)}) %collective-permute-start.28) | collective-permute-done | bytes 131104 | tf_op jit(solution)/shard_map/ppermute | solution.py:300
  106.8 5.6 %collective-permute-done.21.far_v_ref = bf16[512,256]{1,0:T(8,128)(2,1)S(1)} collective-permute-done((bf16[512,256]{1,0:T(8,128)(2,1)S(1)}, bf16[512,256]{1,0:T(8,128)(2,1)S(1)}, u32[]{:S(2)}, u32[]{:S(2)}) %collective-permute-start.21) | collective-permute-done | bytes 262176 | tf_op jit(solution)/shard_map/ppermute | solution.py:400
  112.4 2.5 %collective-permute-start.31 = (bf16[512,256]{1,0:T(8,128)(2,1)S(1)}, bf16[512,256]{1,0:T(8,128)(2,1)S(1)}, u32[]{:S(2)}, u32[]{:S(2)}) collective-permute-start(bf16[512,256]{1,0:T(8,128)(2,1)S(1)} %get-tuple-element.117), channel_id=1, source_target_pairs={{0,16},{2,18},{4,20},{6,22},{8,24},{10,26},{12,28},{14,30},{16,0},... | collective-permute-start | bytes 786440 | tf_op jit(solution)/shard_map/ppermute | solution.py:413
  115.0 1.9 %collective-permute-start.35 = (bf16[256,256]{1,0:T(8,128)(2,1)S(1)}, bf16[256,256]{1,0:T(8,128)(2,1)S(1)}, u32[]{:S(2)}, u32[]{:S(2)}) collective-permute-start(bf16[256,256]{1,0:T(8,128)(2,1)S(1)} %constant_dynamic-update-slice_fusion.refs_0_), channel_id=1, source_target_pairs={{0,12},{2,14},{4,8},{6,10},{8,4},{10,6},{12,0},{14,2},{16,28},{18,... | collective-permute-start | bytes 393224 | tf_op jit(solution)/shard_map/ppermute | solution.py:300
  119.6 4.8 %collective-permute-done.35.refs_3_ = bf16[256,256]{1,0:T(8,128)(2,1)S(1)} collective-permute-done((bf16[256,256]{1,0:T(8,128)(2,1)S(1)}, bf16[256,256]{1,0:T(8,128)(2,1)S(1)}, u32[]{:S(2)}, u32[]{:S(2)}) %collective-permute-start.35) | collective-permute-done | bytes 131104 | tf_op jit(solution)/shard_map/ppermute | solution.py:300
  124.4 3.5 %collective-permute-done.34.refs_2_ = bf16[256,256]{1,0:T(8,128)(2,1)S(1)} collective-permute-done((bf16[256,256]{1,0:T(8,128)(2,1)S(1)}, bf16[256,256]{1,0:T(8,128)(2,1)S(1)}, u32[]{:S(2)}, u32[]{:S(2)}) %collective-permute-start.34) | collective-permute-done | bytes 131104 | tf_op jit(solution)/shard_map/ppermute | solution.py:300
  128.0 1.9 %finish.1 = (bf16[512,256]{1,0:T(8,128)(2,1)}, bf16[512,256]{1,0:T(8,128)(2,1)}, f32[256,512]{1,0:T(8,128)}) custom-call(s32[2]{0:T(128)S(1)} %copy-done.5, s32[1,256]{1,0:T(1,128)S(1)} %copy-done.6, f32[512,256]{1,0:T(8,128)S(1)} %get-tuple-element.113.own_k_ref, f32[512,256]{1,0:T(8,128)S(1)} %get-tuple-element.114.own_v_ref, ...), custom_call_target="tpu_custom_call" | custom-call | tf_op jit(solution)/shard_map/finish/pallas_call | solution.py:426
  (91 shorter events, 36.2 us)
Async XLA Ops:
  0.6 23.8 %collective-permute-start = (bf16[512,256]{1,0:T(8,128)(2,1)}, bf16[512,256]{1,0:T(8,128)(2,1)S(1)}, u32[]{:S(2)}, u32[]{:S(2)}) collective-permute-start(bf16[512,256]{1,0:T(8,128)(2,1)} %bitcast.26), channel_id=1, source_target_pairs={{0,16},{2,18},{4,20},{6,22},{8,24},{10,26},{12,28},{14,30},{16,0},... | collective-permute-start | bytes 786440 | tf_op jit(solution)/shard_map/ppermute | solution.py:309
  9.5 13.3 %all-to-all-start = ((bf16[8,32,640]{2,1,0:T(8,128)(2,1)}), bf16[8,32,640]{2,1,0:T(8,128)(2,1)S(1)}, u32[]{:S(2)}, u32[]{:S(2)}) async-start(bf16[8,32,640]{2,1,0:T(8,128)(2,1)} %bitcast.36), calls=%async_computation | async-start | bytes 655360 | tf_op jit(solution)/shard_map/all_to_all | solution.py:295
  13.5 16.5 %collective-permute-start.1 = (bf16[512,256]{1,0:T(8,128)(2,1)}, bf16[512,256]{1,0:T(8,128)(2,1)S(1)}, u32[]{:S(2)}, u32[]{:S(2)}) collective-permute-start(bf16[512,256]{1,0:T(8,128)(2,1)} %get-tuple-element.68), channel_id=1, source_target_pairs={{0,16},{2,18},{4,20},{6,22},{8,24},{10,26},{12,28},{14,30},{16,0},... | collective-permute-start | bytes 786440 | tf_op jit(solution)/shard_map/ppermute | solution.py:324
  13.8 18.0 %collective-permute-start.3 = (bf16[64,512]{1,0:T(8,128)(2,1)S(1)}, bf16[64,512]{1,0:T(8,128)(2,1)S(1)}, u32[]{:S(2)}, u32[]{:S(2)}) collective-permute-start(bf16[64,512]{1,0:T(8,128)(2,1)S(1)} %pad_maximum_fusion), channel_id=1, source_target_pairs={{0,2},{2,4},{4,6},{6,8},{8,10},{10,12},{12,14},{14,16},{16,18},{18... | collective-permute-start | bytes 196616 | tf_op jit(solution)/shard_map/ppermute | solution.py:329
  14.1 17.7 %collective-permute-start.4 = (bf16[64,512]{1,0:T(8,128)(2,1)S(1)}, bf16[64,512]{1,0:T(8,128)(2,1)S(1)}, u32[]{:S(2)}, u32[]{:S(2)}) collective-permute-start(bf16[64,512]{1,0:T(8,128)(2,1)S(1)} %pad_maximum_fusion.1), channel_id=1, source_target_pairs={{2,0},{4,2},{6,4},{8,6},{10,8},{12,10},{14,12},{16,14},{18,16},{20... | collective-permute-start | bytes 196616 | tf_op jit(solution)/shard_map/ppermute | solution.py:330
  31.9 11.0 %collective-permute-start.5 = (bf16[288,512]{1,0:T(8,128)(2,1)S(1)}, bf16[288,512]{1,0:T(8,128)(2,1)S(1)}, u32[]{:S(2)}, u32[]{:S(2)}) collective-permute-start(bf16[288,512]{1,0:T(8,128)(2,1)S(1)} %get-tuple-element.81), channel_id=1, source_target_pairs={{0,12},{2,14},{4,8},{6,10},{8,4},{10,6},{12,0},{14,2},{16,28},{18,... | collective-permute-start | bytes 884744 | tf_op jit(solution)/shard_map/ppermute | solution.py:300
  32.2 14.9 %collective-permute-start.6 = (bf16[288,512]{1,0:T(8,128)(2,1)S(1)}, bf16[288,512]{1,0:T(8,128)(2,1)S(1)}, u32[]{:S(2)}, u32[]{:S(2)}) collective-permute-start(bf16[288,512]{1,0:T(8,128)(2,1)S(1)} %get-tuple-element.82), channel_id=1, source_target_pairs={{0,4},{2,6},{4,0},{6,2},{8,12},{10,14},{12,8},{14,10},{16,20},{18,... | collective-permute-start | bytes 884744 | tf_op jit(solution)/shard_map/ppermute | solution.py:300
  33.7 15.6 %collective-permute-start.7 = (bf16[288,512]{1,0:T(8,128)(2,1)S(1)}, bf16[288,512]{1,0:T(8,128)(2,1)S(1)}, u32[]{:S(2)}, u32[]{:S(2)}) collective-permute-start(bf16[288,512]{1,0:T(8,128)(2,1)S(1)} %get-tuple-element.83), channel_id=1, source_target_pairs={{0,8},{2,10},{4,12},{6,14},{8,0},{10,2},{12,4},{14,6},{16,24},{18,... | collective-permute-start | bytes 884744 | tf_op jit(solution)/shard_map/ppermute | solution.py:300
  35.4 19.9 %collective-permute-start.8 = (bf16[288,512]{1,0:T(8,128)(2,1)S(1)}, bf16[288,512]{1,0:T(8,128)(2,1)S(1)}, u32[]{:S(2)}, u32[]{:S(2)}) collective-permute-start(bf16[288,512]{1,0:T(8,128)(2,1)S(1)} %get-tuple-element.84), channel_id=1, source_target_pairs={{0,6},{2,4},{4,2},{6,0},{8,14},{10,12},{12,10},{14,8},{16,22},{18,... | collective-permute-start | bytes 884744 | tf_op jit(solution)/shard_map/ppermute | solution.py:300
  35.4 19.9 %collective-permute-start.9 = (bf16[288,512]{1,0:T(8,128)(2,1)S(1)}, bf16[288,512]{1,0:T(8,128)(2,1)S(1)}, u32[]{:S(2)}, u32[]{:S(2)}) collective-permute-start(bf16[288,512]{1,0:T(8,128)(2,1)S(1)} %get-tuple-element.85), channel_id=1, source_target_pairs={{0,10},{2,8},{4,14},{6,12},{8,2},{10,0},{12,6},{14,4},{16,26},{18,... | collective-permute-start | bytes 884744 | tf_op jit(solution)/shard_map/ppermute | solution.py:300
  42.8 12.5 %collective-permute-start.10 = (bf16[288,512]{1,0:T(8,128)(2,1)S(1)}, bf16[288,512]{1,0:T(8,128)(2,1)S(1)}, u32[]{:S(2)}, u32[]{:S(2)}) collective-permute-start(bf16[288,512]{1,0:T(8,128)(2,1)S(1)} %get-tuple-element.86), channel_id=1, source_target_pairs={{0,2},{2,0},{4,6},{6,4},{8,10},{10,8},{12,14},{14,12},{16,18},{18,... | collective-permute-start | bytes 884744 | tf_op jit(solution)/shard_map/ppermute | solution.py:300
  47.1 11.2 %collective-permute-start.11 = (bf16[288,512]{1,0:T(8,128)(2,1)S(1)}, bf16[288,512]{1,0:T(8,128)(2,1)S(1)}, u32[]{:S(2)}, u32[]{:S(2)}) collective-permute-start(bf16[288,512]{1,0:T(8,128)(2,1)S(1)} %get-tuple-element.87), channel_id=1, source_target_pairs={{0,14},{2,12},{4,10},{6,8},{8,6},{10,4},{12,2},{14,0},{16,30},{18,... | collective-permute-start | bytes 884744 | tf_op jit(solution)/shard_map/ppermute | solution.py:300
  70.8 11.7 %collective-permute-start.14 = (bf16[384,256]{1,0:T(8,128)(2,1)S(1)}, bf16[384,256]{1,0:T(8,128)(2,1)S(1)}, u32[]{:S(2)}, u32[]{:S(2)}) collective-permute-start(bf16[384,256]{1,0:T(8,128)(2,1)S(1)} %get-tuple-element.94), channel_id=1, source_target_pairs={{0,8},{2,10},{4,12},{6,14},{8,0},{10,2},{12,4},{14,6},{16,24},{18,... | collective-permute-start | bytes 589832 | tf_op jit(solution)/shard_map/ppermute | solution.py:300
  71.3 13.5 %collective-permute-start.15 = (bf16[384,256]{1,0:T(8,128)(2,1)S(1)}, bf16[384,256]{1,0:T(8,128)(2,1)S(1)}, u32[]{:S(2)}, u32[]{:S(2)}) collective-permute-start(bf16[384,256]{1,0:T(8,128)(2,1)S(1)} %get-tuple-element.95), channel_id=1, source_target_pairs={{0,6},{2,4},{4,2},{6,0},{8,14},{10,12},{12,10},{14,8},{16,22},{18,... | collective-permute-start | bytes 589832 | tf_op jit(solution)/shard_map/ppermute | solution.py:300
  73.1 12.8 %collective-permute-start.16 = (bf16[384,256]{1,0:T(8,128)(2,1)S(1)}, bf16[384,256]{1,0:T(8,128)(2,1)S(1)}, u32[]{:S(2)}, u32[]{:S(2)}) collective-permute-start(bf16[384,256]{1,0:T(8,128)(2,1)S(1)} %get-tuple-element.96), channel_id=1, source_target_pairs={{0,10},{2,8},{4,14},{6,12},{8,2},{10,0},{12,6},{14,4},{16,26},{18,... | collective-permute-start | bytes 589832 | tf_op jit(solution)/shard_map/ppermute | solution.py:300
  76.6 11.3 %collective-permute-start.17 = (bf16[384,256]{1,0:T(8,128)(2,1)S(1)}, bf16[384,256]{1,0:T(8,128)(2,1)S(1)}, u32[]{:S(2)}, u32[]{:S(2)}) collective-permute-start(bf16[384,256]{1,0:T(8,128)(2,1)S(1)} %get-tuple-element.97), channel_id=1, source_target_pairs={{0,2},{2,0},{4,6},{6,4},{8,10},{10,8},{12,14},{14,12},{16,18},{18,... | collective-permute-start | bytes 589832 | tf_op jit(solution)/shard_map/ppermute | solution.py:300
  82.5 10.7 %collective-permute-start.22 = (bf16[256,256]{1,0:T(8,128)(2,1)S(1)}, bf16[256,256]{1,0:T(8,128)(2,1)S(1)}, u32[]{:S(2)}, u32[]{:S(2)}) collective-permute-start(bf16[256,256]{1,0:T(8,128)(2,1)S(1)} %get-tuple-element.103), channel_id=1, source_target_pairs={{0,12},{2,14},{4,8},{6,10},{8,4},{10,6},{12,0},{14,2},{16,28},{18,... | collective-permute-start | bytes 393224 | tf_op jit(solution)/shard_map/ppermute | solution.py:300
  84.9 10.7 %collective-permute-start.23 = (bf16[256,256]{1,0:T(8,128)(2,1)S(1)}, bf16[256,256]{1,0:T(8,128)(2,1)S(1)}, u32[]{:S(2)}, u32[]{:S(2)}) collective-permute-start(bf16[256,256]{1,0:T(8,128)(2,1)S(1)} %get-tuple-element.104), channel_id=1, source_target_pairs={{0,4},{2,6},{4,0},{6,2},{8,12},{10,14},{12,8},{14,10},{16,20},{18,... | collective-permute-start | bytes 393224 | tf_op jit(solution)/shard_map/ppermute | solution.py:300
  85.9 10.2 %collective-permute-start.24 = (bf16[256,256]{1,0:T(8,128)(2,1)S(1)}, bf16[256,256]{1,0:T(8,128)(2,1)S(1)}, u32[]{:S(2)}, u32[]{:S(2)}) collective-permute-start(bf16[256,256]{1,0:T(8,128)(2,1)S(1)} %get-tuple-element.105), channel_id=1, source_target_pairs={{0,8},{2,10},{4,12},{6,14},{8,0},{10,2},{12,4},{14,6},{16,24},{18,... | collective-permute-start | bytes 393224 | tf_op jit(solution)/shard_map/ppermute | solution.py:300
  97.0 15.3 %collective-permute-start.21 = (bf16[512,256]{1,0:T(8,128)(2,1)S(1)}, bf16[512,256]{1,0:T(8,128)(2,1)S(1)}, u32[]{:S(2)}, u32[]{:S(2)}) collective-permute-start(bf16[512,256]{1,0:T(8,128)(2,1)S(1)} %slice.55), channel_id=1, source_target_pairs={{0,16},{2,18},{4,20},{6,22},{8,24},{10,26},{12,28},{14,30},{16,0},... | collective-permute-start | bytes 786440 | tf_op jit(solution)/shard_map/ppermute | solution.py:400
  101.7 10.6 %collective-permute-start.29 = (bf16[64,512]{1,0:T(8,128)(2,1)S(1)}, bf16[64,512]{1,0:T(8,128)(2,1)S(1)}, u32[]{:S(2)}, u32[]{:S(2)}) collective-permute-start(bf16[64,512]{1,0:T(8,128)(2,1)S(1)} %get-tuple-element.111), channel_id=1, source_target_pairs={{2,0},{4,2},{6,4},{8,6},{10,8},{12,10},{14,12},{16,14},{18,16},{20... | collective-permute-start | bytes 196616 | tf_op jit(solution)/shard_map/ppermute | solution.py:382
  112.4 15.5 %collective-permute-start.31 = (bf16[512,256]{1,0:T(8,128)(2,1)S(1)}, bf16[512,256]{1,0:T(8,128)(2,1)S(1)}, u32[]{:S(2)}, u32[]{:S(2)}) collective-permute-start(bf16[512,256]{1,0:T(8,128)(2,1)S(1)} %get-tuple-element.117), channel_id=1, source_target_pairs={{0,16},{2,18},{4,20},{6,22},{8,24},{10,26},{12,28},{14,30},{16,0},... | collective-permute-start | bytes 786440 | tf_op jit(solution)/shard_map/ppermute | solution.py:413
  116.9 11.1 %collective-permute-start.34 = (bf16[256,256]{1,0:T(8,128)(2,1)S(1)}, bf16[256,256]{1,0:T(8,128)(2,1)S(1)}, u32[]{:S(2)}, u32[]{:S(2)}) collective-permute-start(bf16[256,256]{1,0:T(8,128)(2,1)S(1)} %constant_dynamic-update-slice_fusion.refs_0_), channel_id=1, source_target_pairs={{0,8},{2,10},{4,12},{6,14},{8,0},{10,2},{12,4},{14,6},{16,24},{18,... | collective-permute-start | bytes 393224 | tf_op jit(solution)/shard_map/ppermute | solution.py:300
  116.9 11.1 %collective-permute-start.33 = (bf16[256,256]{1,0:T(8,128)(2,1)S(1)}, bf16[256,256]{1,0:T(8,128)(2,1)S(1)}, u32[]{:S(2)}, u32[]{:S(2)}) collective-permute-start(bf16[256,256]{1,0:T(8,128)(2,1)S(1)} %constant_dynamic-update-slice_fusion.refs_0_), channel_id=1, source_target_pairs={{0,4},{2,6},{4,0},{6,2},{8,12},{10,14},{12,8},{14,10},{16,20},{18,... | collective-permute-start | bytes 393224 | tf_op jit(solution)/shard_map/ppermute | solution.py:300
  (22 other events, 221.3 us)
